TPU v7x, 32 devices: a whole 2x2x4 slice. The times are simulated.
32 devices in a mesh: dp: 8 (over z, core), et: 4 (over y, x).
Axes of the slice: x: 2, y: 2, z: 4, core: 2. Of those that a mesh axis runs over, the one named last changes fastest.
Arguments:
- pre_gate: bfloat16 [2048, 5376], P('dp', 'et'), may hold values from -6 to 6
- pre_up: bfloat16 [2048, 5376], P('dp', 'et'), may hold values from -6 to 6
- down_weight: bfloat16 [5376, 6144], P('et'), may hold values from -0.078125 to 0.078125
- row_token: int32 [2048], P('dp'), may hold values from 0 to 384, as said below
- block_count: int32 [8], P('dp'), may hold values from 1 to 2, as said below
- router_logits: float32 [3072, 16], P('dp'), as said below
- tokens_in: bfloat16 [3072, 6144], P('dp', 'et'), may hold values from -6 to 6
- out_grad: bfloat16 [3072, 6144], P('dp', 'et'), may hold values from -12 to 12
Outputs:
- combined: bfloat16 [3072, 6144], P('dp', 'et')
- grad_gate: bfloat16 [2048, 5376], P('dp', 'et')
- grad_up: bfloat16 [2048, 5376], P('dp', 'et')
- router_grad: float32 [16, 6144], P(None, 'et')
Inputs may be any that keep to these rules, and one draw needn't show every extreme that they name: `row_token`: within the 256 slots of one index of dp, the first r slots hold distinct tokens below 384 and the other slots hold 384, with r between 64 and 256; r = 256 on at least one index of dp. `block_count`: the number of blocks of 128 slots that hold r's live slots, rounded up, on each index of dp. `router_logits`: finite router scores.
All inputs are finite; a program needn't handle non-finite values.
Results may differ from a plain program's by a relative error of at most 0.0051.
Values may be sent and summed in bfloat16 or wider, within the bound.
No kernel may reach another device: no remote copies, remote signals or barrier semaphores. Data moves between devices by JAX's collectives and lax.ppermute only.
A program may use at most 128 MiB of HBM per device.

v0:
```python
import jax
import jax.numpy as jnp
from jax import lax
from jax.sharding import PartitionSpec as P

BLOCK = 128


def body(pre_gate, pre_up, down_weight, row_token, block_count, router_logits, tokens_in, out_grad):
    slot_count = pre_gate.shape[0]
    tok_count = tokens_in.shape[0]
    slot_ids = jnp.arange(slot_count, dtype=jnp.int32)
    live_slot = (slot_ids // BLOCK < block_count[0]) & (row_token < tok_count)
    scatter_index = jnp.where(live_slot, row_token, tok_count)
    safe_index = jnp.minimum(scatter_index, tok_count - 1)
    router_probs = jax.nn.softmax(router_logits, axis=-1)
    first_prob = router_probs[:, 0]
    row_prob = jnp.where(live_slot, first_prob[safe_index], 0.0)
    gate_value = pre_gate.astype(jnp.float32)
    up_value = pre_up.astype(jnp.float32)
    sigmoid_gate = jax.nn.sigmoid(gate_value)
    hidden = jnp.where(live_slot[:, None], gate_value * sigmoid_gate * up_value, 0.0).astype(
        jnp.bfloat16
    )
    partial_out = jnp.dot(hidden, down_weight, preferred_element_type=jnp.float32)
    expert_out = lax.psum_scatter(partial_out, "et", scatter_dimension=1, tiled=True)
    combined = (
        jnp.zeros((tok_count, expert_out.shape[1]), jnp.float32)
        .at[scatter_index]
        .add(row_prob[:, None] * expert_out, mode="drop")
        .astype(jnp.bfloat16)
    )
    local_rows = jnp.where(live_slot[:, None], out_grad[safe_index], 0.0)
    dot_part = jnp.sum(local_rows.astype(jnp.float32) * expert_out, axis=1)
    weight_grad = lax.psum(dot_part, "et")
    gathered = lax.all_gather(out_grad, "et", axis=1, tiled=True)
    slot_rows = jnp.where(live_slot[:, None], gathered[safe_index], 0.0)
    raw_back = lax.dot_general(
        slot_rows, down_weight, (((1,), (1,)), ((), ())), preferred_element_type=jnp.float32
    )
    hidden_grad = row_prob[:, None] * raw_back
    grad_up = (hidden_grad * gate_value * sigmoid_gate).astype(jnp.bfloat16)
    grad_gate = (
        hidden_grad * up_value * sigmoid_gate * (1.0 + gate_value * (1.0 - sigmoid_gate))
    ).astype(jnp.bfloat16)
    token_weight = (
        jnp.zeros((tok_count,), jnp.float32).at[scatter_index].add(weight_grad, mode="drop")
    )
    one_hot = (jnp.arange(router_probs.shape[1]) == 0).astype(jnp.float32)
    logit_grad = (
        first_prob[:, None] * (one_hot[None, :] - router_probs) * token_weight[:, None]
    ).astype(jnp.bfloat16)
    router_part = jnp.dot(logit_grad.T, tokens_in, preferred_element_type=jnp.float32)
    all_tokens = tok_count * lax.axis_size("dp")
    router_grad = lax.psum(router_part, "dp") * all_tokens ** (-0.5)
    return (combined, grad_gate, grad_up, router_grad)


def solution(mesh):
    in_specs = (
        P("dp", "et"),
        P("dp", "et"),
        P("et", None),
        P("dp"),
        P("dp"),
        P("dp", None),
        P("dp", "et"),
        P("dp", "et"),
    )
    out_specs = (P("dp", "et"), P("dp", "et"), P("dp", "et"), P(None, "et"))
    return jax.shard_map(body, mesh=mesh, in_specs=in_specs, out_specs=out_specs, check_vma=False)
```

profile of v0, /device:TPU:0, one launch (start us, length us, event | category | flops | bytes accessed | tf_op | source)
XLA Modules:
  0.0 216.8 jit_solution(5880184278702968662)
XLA Ops:
  7.2 0.0 copy-start
  7.2 0.0 copy-start.2
  7.2 0.0 all-gather.2.cloned.1.call-start
  7.2 0.7 all-gather.2.cloned.1.call-update
  7.9 0.0 reduce-scatter.2.cloned.1.call-start
  8.6 0.7 compare_select_fusion
  9.3 0.0 copy-done.2
  9.3 13.3 %fusion.22 = f32[256,6144]{1,0:T(8,128)} fusion(bf16[1344,6144]{1,0:T(8,128)(2,1)} %param.10, bf16[256,1344]{0,1:T(8,128)(2,1)S(1)} %copy-done.2, bf16[256,1344]{0,1:T(8,128)(2,1)} %param.8, pred[256]{0:T(512)(128)(4,1)S(1)} %get-tuple-element.5), kind=kOutput, calls=%fused_computation.32 | convolution fusion | flops 4230955008 | bytes 24183040 | tf_op jit(solution)/shard_map/dot_general | solution.py:25
  22.7 0.0 copy-start.1
  22.7 0.0 reduce-scatter.2.cloned.1.call-update
  22.7 0.0 all-reduce.2.cloned.1.call-start
  22.8 1.2 copy-done.1
  23.9 1.3 gather_fusion.2
  25.2 0.0 copy-done.5
  25.3 1.9 gather_fusion
  27.3 0.0 copy-done.6
  27.3 42.4 %all-gather.2.cloned.1.call-done = bf16[384,6144]{1,0:T(8,128)(2,1)} async-done(((bf16[384,1536]{1,0:T(8,128)(2,1)}), bf16[384,6144]{1,0:T(8,128)(2,1)}) %all-gather.2.cloned.1.call-update) | async-done | bytes 4718608 | tf_op jit(solution)/shard_map/all_gather | solution.py:36
  69.7 10.4 %gather_fusion.1 = bf16[256,6144]{1,0:T(8,128)(2,1)} fusion(bf16[384,6144]{1,0:T(8,128)(2,1)} %all-gather.2.cloned.1.call-done, s32[1024]{0:T(1024)S(1)} %pad_clamp_fusion), kind=kCustom, calls=%fused_computation.1 | custom fusion | bytes 6292480 | tf_op jit(solution)/shard_map/gather | solution.py:37
  80.1 62.8 %reduce-scatter.2.cloned.1.call-done = f32[256,1536]{1,0:T(8,128)} async-done(((f32[256,6144]{1,0:T(8,128)}), f32[256,1536]{1,0:T(8,128)}) %reduce-scatter.2.cloned.1.call-update) | async-done | bytes 1572880 | tf_op jit(solution)/shard_map/reduce_scatter | solution.py:26
  142.9 1.8 multiply_reduce_fusion
  144.7 9.1 %psum.14 = f32[256]{0:T(256)S(1)} all-reduce(f32[256]{0:T(256)S(1)} %multiply_reduce_fusion), channel_id=1, replica_groups=mesh['dp'=8,'et'=4] {'et'}, use_global_device_ids=true, to_apply=%region_5.6 | all-reduce | flops 256 | bytes 2048 | tf_op jit(solution)/shard_map/psum | solution.py:35
  153.8 2.3 %scatter_custom_fusion.1 = f32[384]{0:T(512)S(1)} fusion(s32[256]{0:T(256)S(1)} %compare_select_fusion.1, f32[256]{0:T(256)S(1)} %psum.14, f32[]{:T(128)} %constant.12.clone.1), kind=kCustom, calls=%fused_computation.55 | custom fusion | flops 256 | bytes 1540 | tf_op jit(solution)/shard_map/scatter-add | solution.py:47
  156.1 0.0 copy-done
  156.1 1.0 fusion.29
  157.0 0.0 all-reduce.2.cloned.1.call-update
  157.1 0.0 copy-done.3
  157.1 0.0 copy-done.4
  157.1 13.0 %fusion.19 = (bf16[256,1344]{0,1:T(8,128)(2,1)}, bf16[256,1344]{0,1:T(8,128)(2,1)}) fusion(bf16[256,1344]{0,1:T(8,128)(2,1)S(1)} %copy-done.4, bf16[256,1344]{0,1:T(8,128)(2,1)S(1)} %copy-done.3, bf16[1344,6144]{1,0:T(8,128)(2,1)} %param.10, bf16[256,6144]{1,0:T(8,128)(2,1)} %gather_fusion.1, pred[256]{0:T(512)(128)(4,1)S(1)} %get-tuple-element.5, ...), kind=kOutput, calls=%fused_computation.29 | convolution fusion | flops 4234936320 | bytes 22414592 | tf_op jit(solution)/shard_map/dot_general | solution.py:38
  170.1 4.6 %scatter_custom_fusion = f32[384,1536]{1,0:T(8,128)S(1)} fusion(s32[256]{0:T(256)S(1)} %compare_select_fusion.1, f32[256,1536]{1,0:T(8,128)} %reduce-scatter.2.cloned.1.call-done, f32[]{:T(128)} %constant.12.clone.1, f32[256]{0:T(256)S(1)} %broadcast_select_fusion), kind=kCustom, calls=%fused_computation.17 | custom fusion | flops 786432 | bytes 3933188 | tf_op jit(solution)/shard_map/scatter-add | solution.py:30
  174.8 1.1 convert_element_type.38
  175.9 32.8 %all-reduce.2.cloned.1.call-done = f32[16,1536]{1,0:T(8,128)} async-done(((f32[16,1536]{1,0:T(8,128)}), f32[16,1536]{1,0:T(8,128)}) %all-reduce.2.cloned.1.call-update) | async-done | bytes 98320 | tf_op jit(solution)/shard_map/psum | solution.py:55
  208.7 1.5 broadcast_multiply_fusion
  (12 shorter events, 0.1 us)
Async XLA Ops:
  7.2 148.9 %copy-start = (bf16[384,1536]{1,0:T(8,128)(2,1)S(1)}, bf16[384,1536]{1,0:T(8,128)(2,1)}, u32[]{:S(2)}) copy-start(bf16[384,1536]{1,0:T(8,128)(2,1)} %param.14) | copy-start | bytes 3538948
  7.2 2.1 copy-start.2
  7.2 62.5 %all-gather.2.cloned.1.call-start = ((), (), s32[]{:S(2)}) async-start(), calls=%async_computation.2 | async-start | bytes 5898240 | tf_op jit(solution)/shard_map/all_gather | solution.py:36
  7.9 135.0 %reduce-scatter.2.cloned.1.call-start = ((), (), s32[]{:S(2)}) async-start(), calls=%async_computation.1 | async-start | bytes 7864320 | tf_op jit(solution)/shard_map/reduce_scatter | solution.py:26
  22.7 1.3 copy-start.1
  22.7 186.0 %all-reduce.2.cloned.1.call-start = ((), (), s32[]{:S(2)}) async-start(), calls=%async_computation.3 | async-start | bytes 196608 | tf_op jit(solution)/shard_map/psum | solution.py:55
  23.9 1.3 copy-start.5
  23.9 3.3 %copy-start.6 = (s32[256]{0:T(256)S(1)}, s32[256]{0:T(256)}, u32[]{:S(2)}) copy-start(s32[256]{0:T(256)} %param.11) | copy-start | bytes 3076
  80.1 77.0 %copy-start.3 = (bf16[256,1344]{0,1:T(8,128)(2,1)S(1)}, bf16[256,1344]{0,1:T(8,128)(2,1)}, u32[]{:S(2)}) copy-start(bf16[256,1344]{0,1:T(8,128)(2,1)} %param.9) | copy-start | bytes 2064388
  80.1 77.0 %copy-start.4 = (bf16[256,1344]{0,1:T(8,128)(2,1)S(1)}, bf16[256,1344]{0,1:T(8,128)(2,1)}, u32[]{:S(2)}) copy-start(bf16[256,1344]{0,1:T(8,128)(2,1)} %param.8) | copy-start | bytes 2064388
Sparse Core Ops, SparseCore 0:
  9.9 59.7 all-gather.1
  72.7 70.2 reduce-scatter.1
  157.2 51.4 all-reduce.1
where the time goes:
time: 217 us
  waiting for transfers between devices  139 us (64%)
  matrix products  27.3 us (13%)
  local copies, waits for them, and re-layouts  14.8 us (7%)
  between operations  14.5 us (7%)
  other arithmetic  12.2 us (6%)
  blocking collectives  9.1 us (4%)
    reduce_scatter x1, waiting for transfers between devices, body(): lax.psum_scatter(partial_out, 'et', scatter_dimension=1, tiled=True)  62.8 us
    all_gather x1, waiting for transfers between devices, body(): gathered = lax.all_gather(out_grad, 'et', axis=1, tiled=True)  42.4 us
    psum x1, waiting for transfers between devices, body(): router_grad = lax.psum(router_part, 'dp') * all_tokens ** (-0.5)  32.8 us
    dot_general x1, matrix products, body(): jnp.dot(hidden, down_weight, preferred_element_type=jnp.float32)  13.3 us
    dot_general x1, matrix products, body(): lax.dot_general(slot_rows, down_weight, (((1,), (1,)), ((), ())), preferr...  13 us
    gather x1, local copies, waits for them, and re-layouts, body(): slot_rows = jnp.where(live_slot[:, None], gathered[safe_index], 0.0)  10.4 us
    psum x1, blocking collectives, body(): weight_grad = lax.psum(dot_part, 'et')  9.1 us
    scatter-add x1, other arithmetic, body(): combined = jnp.zeros((tok_count, expert_out.shape[1]), jnp.float32).at[sc...  4.63 us
  transfers between devices with their start and end apart: 3, of which 3 were waited for; matrix products, arithmetic and copies ran while one was open for 21% of the time, Pallas kernels for 0%

commit v1 on v0

v1 whole, which is shorter than its diff:
```python
import functools

import jax
import jax.numpy as jnp
from jax import lax
from jax.experimental import pallas as pl
from jax.experimental.pallas import tpu as pltpu
from jax.sharding import PartitionSpec as P

BLOCK = 128
F32 = jnp.float32
BF16 = jnp.bfloat16


def params(mib=24):
    return pltpu.CompilerParams(vmem_limit_bytes=mib * 1024 * 1024)


def cost(flops, size, trans=0):
    return pl.CostEstimate(flops=flops, bytes_accessed=size, transcendentals=trans)


def row_step(rows, most=336):
    best = 16
    for step in range(16, most + 1, 16):
        if rows % step == 0:
            best = step
    return best


def live_lanes(row_ref, count_ref, tok_count):
    rows = row_ref[...]
    slots = lax.broadcasted_iota(jnp.int32, rows.shape, 1)
    return (slots // BLOCK < count_ref[0]) & (rows < tok_count)


def token_of_slot(row_ref, count_ref, tok_count):
    live = live_lanes(row_ref, count_ref, tok_count)
    rows = jnp.where(live, row_ref[...], tok_count)
    tokens = lax.broadcasted_iota(jnp.int32, (tok_count, rows.shape[1]), 0)
    return tokens == rows


def softmax_rows(logits):
    top = jnp.max(logits, axis=0, keepdims=True)
    raised = jnp.exp(logits - top)
    return raised / jnp.sum(raised, axis=0, keepdims=True)


def thirds(value):
    high = value.astype(BF16)
    rest = value - high.astype(F32)
    mid = rest.astype(BF16)
    return high, mid, (rest - mid.astype(F32)).astype(BF16)


def picked(row, mask, dims):
    total = None
    for term in thirds(row):
        part = lax.dot_general(
            jnp.broadcast_to(term, (16, row.shape[1])), mask, (dims, ((), ())), preferred_element_type=F32
        )
        total = part if total is None else total + part
    return total[0:1, :]


def gather_kernel(tok_count, row_ref, grad_ref, *refs):
    n = len(refs) // 2
    outs, made, sem = refs[:n], refs[n:-1], refs[-1]
    rows = row_ref[...]
    column = jnp.broadcast_to(rows, (8, rows.shape[1])).T[:, 0:1]
    tokens = lax.broadcasted_iota(jnp.int32, (rows.shape[1], tok_count), 1)
    mask = (tokens == column).astype(F32).astype(BF16)
    puts = []
    for at, (stage, out) in enumerate(zip(made, outs)):
        width = out.shape[1]
        stage[...] = jnp.dot(
            mask, grad_ref[:, at * width : (at + 1) * width], preferred_element_type=F32
        ).astype(BF16)
        puts.append(pltpu.make_async_copy(stage, out, sem.at[at]))
        puts[-1].start()
    for put in puts:
        put.wait()


def depth_parts(hid):
    half = -(-hid // 512) * 256
    return [(0, half), (half, hid)] if half < hid else [(0, hid)]


def tile_of(ref, rows, me_ref, key, cuts, width):
    flip, cut = key
    at = ((me_ref[0] ^ flip) * cuts + cut) * width
    return ref[rows, pl.ds(pl.multiple_of(at, 128), width)]


def first_forward_kernel(keys, cuts, me_ref, gate_ref, up_ref, weight_ref, *rest):
    n = len(keys)
    outs, kept_ref, hidden_ref, stages = rest[:n], rest[n], rest[n + 1], rest[n + 2 : 2 * n + 2]
    in_sem, out_sem = rest[2 * n + 2 :]
    width = outs[0].shape[1]
    parts = depth_parts(kept_ref.shape[0])

    def fetch(p):
        here = pl.ds(parts[p][0], parts[p][1] - parts[p][0])
        return pltpu.make_async_copy(weight_ref.at[here, :], kept_ref.at[here, :], in_sem.at[p])

    for p in range(len(parts)):
        fetch(p).start()
    gate = gate_ref[...].astype(F32)
    up = up_ref[...].astype(F32)
    hidden_ref[...] = (gate * jax.nn.sigmoid(gate) * up).astype(BF16).T
    puts = []
    for p, (start, stop) in enumerate(parts):
        fetch(p).wait()
        for k, (stage, out) in enumerate(zip(stages, outs)):
            part = jnp.dot(
                hidden_ref[:, start:stop],
                tile_of(kept_ref, pl.ds(start, stop - start), me_ref, keys[k], cuts, width),
                preferred_element_type=F32,
            )
            if p > 0:
                part = part + stage[...].astype(F32)
            stage[...] = part.astype(stage.dtype)
            if p == len(parts) - 1:
                puts.append(pltpu.make_async_copy(stage, out, out_sem.at[k]))
                puts[-1].start()
    for put in puts:
        put.wait()


def next_forward_kernel(keys, cuts, me_ref, row_ref, count_ref, logit_ref, hidden_ref, kept_ref, *refs):
    outs, (prob_ref, pick_ref, weight_ref) = refs[:-3], refs[-3:]
    tok_count = logit_ref.shape[1]
    mask = token_of_slot(row_ref, count_ref, tok_count)
    pick = mask.astype(F32).astype(BF16)
    prob = picked(softmax_rows(logit_ref[...])[0:1, :], pick, ((1,), (0,)))
    prob_ref[...] = prob
    pick_ref[...] = pick
    weight_ref[...] = jnp.sum(jnp.where(mask, prob, 0.0), axis=1, keepdims=True)
    for key, out in zip(keys, outs):
        tile = tile_of(kept_ref, slice(None), me_ref, key, cuts, out.shape[1])
        out[...] = jnp.dot(hidden_ref[...], tile, preferred_element_type=F32).astype(out.dtype)


def times_rows(keys, cuts, me_ref, kept_ref, here, pieces):
    total = None
    for key, piece in zip(keys, pieces):
        part = lax.dot_general(
            tile_of(kept_ref, here, me_ref, key, cuts, piece.shape[1]),
            piece[...],
            (((1,), (1,)), ((), ())),
            preferred_element_type=F32,
        )
        total = part if total is None else total + part
    return total


def dot_kernel(n_pairs, has_dot, *refs):
    total = None
    for k in range(n_pairs):
        product = refs[k][...].astype(F32) * refs[n_pairs + k][...].astype(F32)
        total = product if total is None else total + product
    column = jnp.sum(total, axis=1, keepdims=True)
    row = jnp.broadcast_to(column, (column.shape[0], 128)).T[0:1, :]
    refs[-1][...] = row + refs[-2][...] if has_dot else row


def back_kernel(keys, cuts, has_acc, me_ref, *refs):
    n = len(keys)
    pieces, kept_ref, out_ref = refs[:n], refs[n], refs[-1]
    rows = out_ref.shape[0]
    step = row_step(rows)
    for j in range(rows // step):
        here = pl.ds(j * step, step)
        part = times_rows(keys, cuts, me_ref, kept_ref, here, pieces)
        out_ref[here, :] = part + refs[-2][here, :] if has_acc else part


def final_back_kernel(keys, cuts, me_ref, prob_ref, gate_ref, up_ref, *refs):
    n = len(keys)
    pieces, kept_ref, acc_ref = refs[:n], refs[n], refs[n + 1]
    dgate_ref, dup_ref, dgate, dup, sem = refs[n + 2 :]
    rows = acc_ref.shape[0]
    step = row_step(rows)
    prob = prob_ref[...]
    puts = []
    for j in range(rows // step):
        here = pl.ds(j * step, step)
        raw = acc_ref[here, :] + times_rows(keys, cuts, me_ref, kept_ref, here, pieces)
        gate = gate_ref[here, :].astype(F32)
        up = up_ref[here, :].astype(F32)
        sig = jax.nn.sigmoid(gate)
        act = gate * sig
        scaled = prob * raw
        dup[here, :] = (scaled * act).astype(BF16)
        dgate[here, :] = (scaled * up * sig * (1.0 + gate * (1.0 - sig))).astype(BF16)
        for side, (made, out) in enumerate(((dgate, dgate_ref), (dup, dup_ref))):
            puts.append(pltpu.make_async_copy(made.at[here, :], out.at[here, :], sem.at[side, j]))
            puts[-1].start()
    for put in puts:
        put.wait()


def router_kernel(scale, pick_ref, logit_ref, tokens_ref, *refs):
    dots, out_ref = refs[:-1], refs[-1]
    weight = dots[0][...]
    for other in dots[1:]:
        weight = weight + other[...]
    spread = picked(weight, pick_ref[...], ((1,), (1,)))
    probs = softmax_rows(logit_ref[...])
    expert = lax.broadcasted_iota(jnp.int32, probs.shape, 0)
    hot = jnp.where(expert == 0, 1.0, 0.0)
    logit_grad = (probs[0:1, :] * (hot - probs) * spread).astype(BF16)
    out_ref[...] = jnp.dot(logit_grad, tokens_ref[...], preferred_element_type=F32) * scale


def place_kernel(pick_ref, *refs):
    parts, placed_ref = refs[:-1], refs[-1]
    pick = pick_ref[...]
    value = parts[0][...].astype(F32)
    for part in parts[1:]:
        value = value + part[...].astype(F32)
    high = value.astype(BF16)
    low = (value - high.astype(F32)).astype(BF16)
    placed_ref[...] = jnp.dot(pick, high, preferred_element_type=F32) + jnp.dot(
        pick, low, preferred_element_type=F32
    )


def combine_kernel(cut, n_sums, placed_ref, pick_ref, weight_ref, last_ref, *refs):
    sums, (made, sem) = refs[:n_sums], refs[-2:]
    out_ref = refs[-4] if n_sums else refs[-3]
    rows, width = made.shape
    step = row_step(rows, 128)
    puts = []
    for j in range(rows // step):
        here = pl.ds(j * step, step)
        last = jnp.dot(pick_ref[here, :], last_ref[...], preferred_element_type=F32)
        made[here, :] = (weight_ref[here, :] * (placed_ref[here, :] + last)).astype(BF16)
        puts.append(
            pltpu.make_async_copy(made.at[here, :], out_ref.at[here, pl.ds(cut * width, width)], sem.at[j])
        )
        puts[-1].start()
    if n_sums:
        refs[-3][...] = sums[0][...].astype(F32) + sums[1][...].astype(F32)
    for put in puts:
        put.wait()


def smem():
    return pl.BlockSpec(memory_space=pltpu.SMEM)


def vmem():
    return pl.BlockSpec(memory_space=pltpu.VMEM)


def body(pre_gate, pre_up, down_weight, row_token, block_count, router_logits, tokens_in, out_grad):
    n_et, n_dp = lax.axis_size("et"), lax.axis_size("dp")
    slots, hid = pre_gate.shape
    tok_count, feat = tokens_in.shape
    experts = router_logits.shape[1]
    square = n_et == 4 and feat % 256 == 0
    cuts = 2 if square else 1
    width = feat // cuts
    me = lax.axis_index("et")

    def swap(value, flip, axis="et", size=n_et):
        return lax.ppermute(value, axis, [(i, i ^ flip) for i in range(size)])

    rows = row_token.reshape(1, slots)
    gate_t, up_t, logits_t = pre_gate.T, pre_up.T, router_logits.T

    own = pl.pallas_call(
        functools.partial(gather_kernel, tok_count),
        out_shape=[jax.ShapeDtypeStruct((slots, width), BF16)] * cuts,
        in_specs=[vmem(), vmem()],
        out_specs=[pl.BlockSpec(memory_space=pl.ANY)] * cuts,
        scratch_shapes=[pltpu.VMEM((slots, width), BF16)] * cuts + [pltpu.SemaphoreType.DMA((cuts,))],
        compiler_params=params(60),
        cost_estimate=cost(1, 1),
        name="gather_rows",
    )(rows, out_grad)

    spot, *own = lax.optimization_barrier((me.reshape(1), *own))

    def results(plan):
        kinds = [
            F32 if flip == 0 or (square and (flip, cut) in ((2, 0), (1, 1))) else BF16 for flip, cut in plan
        ]
        return kinds, [jax.ShapeDtypeStruct((slots, width), kind) for kind in kinds]

    if square:
        plans = [[(0, 0), (0, 1), (1, 0), (2, 1)], [(3, 0), (3, 1), (1, 1), (2, 0)]]
    else:
        plans = [[(0, 0)], [(flip, 0) for flip in range(1, n_et)]]
    part = {}
    kinds, shapes = results(plans[0])
    *outs, kept, hidden = pl.pallas_call(
        functools.partial(first_forward_kernel, plans[0], cuts),
        out_shape=shapes
        + [jax.ShapeDtypeStruct(down_weight.shape, BF16), jax.ShapeDtypeStruct((slots, hid), BF16)],
        in_specs=[smem(), vmem(), vmem(), pl.BlockSpec(memory_space=pl.ANY)],
        out_specs=[pl.BlockSpec(memory_space=pl.ANY)] * len(kinds) + [vmem()] * 2,
        scratch_shapes=[pltpu.VMEM((slots, width), kind) for kind in kinds]
        + [pltpu.SemaphoreType.DMA((2,)), pltpu.SemaphoreType.DMA((len(kinds),))],
        compiler_params=params(28),
        cost_estimate=cost(1, 1),
        name="forward_0",
    )(spot, gate_t, up_t, down_weight)
    part.update(zip(plans[0], outs))
    block_count, hidden = lax.optimization_barrier((block_count, hidden))

    if square:
        x0, x1, y1, y0 = swap(own[0], 1), swap(own[1], 1), swap(own[1], 2), swap(own[0], 2)
        x0, y1, hidden = lax.optimization_barrier((x0, y1, hidden))
        far = {(3, 0): swap(x0, 2), (3, 1): swap(y1, 1)}
        near = [{(0, 0): own[0], (0, 1): own[1], (1, 0): x0, (2, 1): y1}, {(1, 1): x1, (2, 0): y0}]
    else:
        far = {(flip, 0): swap(own[0], flip) for flip in range(1, n_et)}
        near = [{(0, 0): own[0]}]
    kinds, shapes = results(plans[1])
    *outs, prob, pick, weight = pl.pallas_call(
        functools.partial(next_forward_kernel, plans[1], cuts),
        out_shape=shapes
        + [
            jax.ShapeDtypeStruct((1, slots), F32),
            jax.ShapeDtypeStruct((tok_count, slots), BF16),
            jax.ShapeDtypeStruct((tok_count, 1), F32),
        ],
        in_specs=[smem(), vmem(), smem()] + [vmem()] * 3,
        out_specs=[vmem()] * (len(kinds) + 3),
        compiler_params=params(),
        cost_estimate=cost(1, 1),
        name="forward_1",
    )(spot, rows, block_count, logits_t, hidden, kept)
    part.update(zip(plans[1], outs))

    acc = None
    for at, pieces in enumerate(near):
        before = [] if acc is None else [acc]
        acc = pl.pallas_call(
            functools.partial(back_kernel, [*pieces], cuts, bool(before)),
            out_shape=jax.ShapeDtypeStruct((hid, slots), F32),
            in_specs=[smem()] + [vmem()] * (len(pieces) + 1 + len(before)),
            out_specs=vmem(),
            compiler_params=params(),
            cost_estimate=cost(1, 1),
            name="back_near_%d" % at,
        )(spot, *pieces.values(), kept, *before)
        if square and at == 0:
            part[3, 0], part[3, 1], acc = lax.optimization_barrier((part[3, 0], part[3, 1], acc))

    dot = None
    for pieces in [*near, far]:
        before = [] if dot is None else [dot]
        if before:
            *values, acc = lax.optimization_barrier((*pieces.values(), acc))
            pieces = dict(zip(pieces, values))
        dot = pl.pallas_call(
            functools.partial(dot_kernel, len(pieces), bool(before)),
            out_shape=jax.ShapeDtypeStruct((1, slots), F32),
            in_specs=[vmem()] * (2 * len(pieces) + len(before)),
            out_specs=vmem(),
            compiler_params=params(),
            cost_estimate=cost(1, 1),
            name="dot_part",
        )(*pieces.values(), *[part[key] for key in pieces], *before)
    dots = [dot] + [swap(dot, flip) for flip in range(1, n_et)]

    step = row_step(hid)
    dgate, dup = pl.pallas_call(
        functools.partial(final_back_kernel, [*far], cuts),
        out_shape=[
            jax.ShapeDtypeStruct((hid, slots), BF16),
            jax.ShapeDtypeStruct((hid, slots), BF16),
        ],
        in_specs=[smem()] + [vmem()] * (len(far) + 5),
        out_specs=[pl.BlockSpec(memory_space=pl.ANY)] * 2,
        scratch_shapes=[
            pltpu.VMEM((hid, slots), BF16),
            pltpu.VMEM((hid, slots), BF16),
            pltpu.SemaphoreType.DMA((2, hid // step)),
        ],
        compiler_params=params(),
        cost_estimate=cost(1, 1),
        name="back_far",
    )(spot, prob, gate_t, up_t, *far.values(), kept, acc)

    if square:
        via_x, via_y = swap(part[3, 0], 1), swap(part[3, 1], 2)
        out_x, out_y, dgate = lax.optimization_barrier((part[1, 0], part[2, 1], dgate))
        *dots, via_x, via_y, dgate = lax.optimization_barrier((*dots, via_x, via_y, dgate))
        direct_x, direct_y = swap(out_x, 1), swap(out_y, 2)
        sum_y = (part[2, 0] + via_x.astype(F32)).astype(BF16)
        sum_x = (part[1, 1] + via_y.astype(F32)).astype(BF16)
        groups = [[part[0, 0], direct_x, swap(sum_y, 2)], [part[0, 1], direct_y, swap(sum_x, 1)]]
    else:
        groups = [[part[0, 0]] + [swap(part[flip, 0], flip) for flip in range(1, n_et)]]

    scale = (tok_count * n_dp) ** -0.5
    router = pl.pallas_call(
        functools.partial(router_kernel, scale),
        out_shape=jax.ShapeDtypeStruct((experts, feat), F32),
        in_specs=[vmem()] * (3 + len(dots)),
        out_specs=vmem(),
        compiler_params=params(),
        cost_estimate=cost(1, 1),
        name="router_part",
    )(pick, logits_t, tokens_in, *dots)
    halves = [router, jnp.zeros_like(router)]
    flip = 1
    while flip < n_dp:
        sent = router if flip == 1 else (halves[0].astype(F32) + halves[1].astype(F32)).astype(BF16)
        if square and flip == 4:
            sent, direct_x, direct_y = lax.optimization_barrier((sent, direct_x, direct_y))
            groups[0][1], groups[1][1] = direct_x, direct_y
        halves = [sent, swap(sent, flip, "dp", n_dp)]
        flip *= 2

    combined = None
    for cut in reversed(range(cuts)):
        *parts, last = groups[cut]
        placed = pl.pallas_call(
            place_kernel,
            out_shape=jax.ShapeDtypeStruct((tok_count, width), F32),
            in_specs=[vmem()] * (1 + len(parts)),
            out_specs=vmem(),
            compiler_params=params(),
            cost_estimate=cost(1, 1),
            name="place_%d" % cut,
        )(pick, *parts)
        before = [] if combined is None else [combined]
        sums = halves if cut == 0 else []
        combined, *router = pl.pallas_call(
            functools.partial(combine_kernel, cut, len(sums)),
            out_shape=[jax.ShapeDtypeStruct((tok_count, feat), BF16)]
            + [jax.ShapeDtypeStruct((experts, feat), F32)] * (len(sums) // 2),
            in_specs=[vmem()] * (4 + len(sums)) + [pl.BlockSpec(memory_space=pl.ANY)] * len(before),
            out_specs=[pl.BlockSpec(memory_space=pl.ANY)] + [vmem()] * (len(sums) // 2),
            scratch_shapes=[
                pltpu.VMEM((tok_count, width), BF16),
                pltpu.SemaphoreType.DMA((tok_count // row_step(tok_count, 128),)),
            ],
            input_output_aliases={4 + len(sums): 0} if before else {},
            compiler_params=params(),
            cost_estimate=cost(1, 1),
            name="combine_%d" % cut,
        )(placed, pick, weight, last, *sums, *before)

    return combined, dgate.T, dup.T, router[0]


def solution(mesh):
    in_specs = (
        P("dp", "et"),
        P("dp", "et"),
        P("et", None),
        P("dp"),
        P("dp"),
        P("dp", None),
        P("dp", "et"),
        P("dp", "et"),
    )
    out_specs = (P("dp", "et"), P("dp", "et"), P("dp", "et"), P(None, "et"))
    return jax.shard_map(body, mesh=mesh, in_specs=in_specs, out_specs=out_specs, check_vma=False)
```

time: 217 us -> 63 us (0.29)
  waiting for transfers between devices: 139 us -> 11.2 us
  matrix products: 27.3 us -> 0 us
  Pallas kernels: 0 us -> 26.3 us
  starting transfers between devices: 0.12 us -> 21.2 us
  between operations: 14.5 us -> 1.63 us
  local copies, waits for them, and re-layouts: 14.8 us -> 2.22 us
  other arithmetic: 12.2 us -> 0.2 us
  blocking collectives: 9.1 us -> 0 us
    reduce_scatter x1 -> x0, waiting for transfers between devices: 62.8 us -> none  [body(): lax.psum_scatter(partial_out, 'et', scatter_dimension=1, tiled=True)]
    all_gather x1 -> x0, waiting for transfers between devices: 42.4 us -> none  [body(): gathered = lax.all_gather(out_grad, 'et', axis=1, tiled=True)]
    psum x1 -> x0, waiting for transfers between devices: 32.8 us -> none  [body(): router_grad = lax.psum(router_part, 'dp') * all_tokens ** (-0.5)]
    dot_general x3 -> x0, matrix products: 27.3 us -> none  [the longest x1 13.3 us: body(): jnp.dot(hidden, down_weight, preferred_element_type=jnp.float32)]
    pallas_call x0 -> x14, Pallas kernels: none -> 26.3 us  [the longest x1 8.82 us: body(): pl.pallas_call(functools.partial(first_forward_kernel, plans[0], cuts), o...]
    ppermute x0 -> x18, starting transfers between devices: none -> 21.2 us  [swap(): return lax.ppermute(value, axis, [(i, i ^ flip) for i in range(size)])]
    gather x3 -> x0, local copies, waits for them, and re-layouts: 13.6 us -> none  [the longest x1 10.4 us: body(): slot_rows = jnp.where(live_slot[:, None], gathered[safe_index], 0.0)]
    ppermute x0 -> x18, waiting for transfers between devices: none -> 11.2 us  [swap(): return lax.ppermute(value, axis, [(i, i ^ flip) for i in range(size)])]
  transfers between devices with their start and end apart: 3 -> 18, of which waited for: 3 -> 7; matrix products, arithmetic and copies ran while one was open for 21% -> 0% of each run, Pallas kernels for 0% -> 35%
where the time goes in v1:
time: 63 us; the launch traced here: 62.8 us
  Pallas kernels  26.3 us (42%)
  starting transfers between devices  21.2 us (34%)
  waiting for transfers between devices  11.2 us (18%)
  local copies, waits for them, and re-layouts  2.22 us (4%)
  between operations  1.63 us (3%)
    ppermute x18, starting transfers between devices, swap(): return lax.ppermute(value, axis, [(i, i ^ flip) for i in range(size)])  21.2 us
    ppermute x18, waiting for transfers between devices, swap(): return lax.ppermute(value, axis, [(i, i ^ flip) for i in range(size)])  11.2 us
    pallas_call x1, Pallas kernels, body(): pl.pallas_call(functools.partial(first_forward_kernel, plans[0], cuts), o...  8.82 us
    pallas_call x2, Pallas kernels, body(): pl.pallas_call(functools.partial(back_kernel, [*pieces], cuts, bool(befor...  3.65 us
    pallas_call x1, Pallas kernels, body(): pl.pallas_call(functools.partial(gather_kernel, tok_count), out_shape=[ja...  2.82 us
    pallas_call x1, Pallas kernels, body(): pl.pallas_call(functools.partial(next_forward_kernel, plans[1], cuts), ou...  2.82 us
    pallas_call x2, Pallas kernels, body(): pl.pallas_call(functools.partial(combine_kernel, cut, len(sums)), out_sha...  2.79 us
    pallas_call x1, Pallas kernels, body(): pl.pallas_call(functools.partial(final_back_kernel, [*far], cuts), out_sh...  2.68 us
  transfers between devices with their start and end apart: 18, of which 7 were waited for; matrix products, arithmetic and copies ran while one was open for 0% of the time, Pallas kernels for 35%

profile of v1, /device:TPU:0, one launch (start us, length us, event | category | flops | bytes accessed | tf_op | source)
XLA Modules:
  0.0 62.8 jit_solution(5980470499831908617)
XLA Ops:
  0.6 2.8 %gather_rows.1 = (bf16[256,768]{1,0:T(8,128)(2,1)}, bf16[256,768]{1,0:T(8,128)(2,1)}) custom-call(s32[1,256]{1,0:T(1,128)} %bitcast.13, bf16[384,1536]{1,0:T(8,128)(2,1)} %grad_ref.1), custom_call_target="tpu_custom_call" | custom-call | flops 1 | bytes 1 | tf_op jit(solution)/shard_map/gather_rows/pallas_call | solution.py:275
  3.5 3.0 %collective-permute-start = (bf16[256,768]{1,0:T(8,128)(2,1)}, bf16[256,768]{1,0:T(8,128)(2,1)S(1)}, u32[]{:S(2)}, u32[]{:S(2)}) collective-permute-start(bf16[256,768]{1,0:T(8,128)(2,1)} %get-tuple-element.58.refs_0_), channel_id=1, source_target_pairs={{0,1},{1,0},{2,3},{3,2},{4,5},{5,4},{6,7},{7,6},{8,9},{9,8},{10,11... | collective-permute-start | bytes 1179656 | tf_op jit(solution)/shard_map/ppermute | solution.py:270
  6.5 1.5 %collective-permute-start.1 = (bf16[256,768]{1,0:T(8,128)(2,1)}, bf16[256,768]{1,0:T(8,128)(2,1)S(1)}, u32[]{:S(2)}, u32[]{:S(2)}) collective-permute-start(bf16[256,768]{1,0:T(8,128)(2,1)} %get-tuple-element.59.refs_1_), channel_id=1, source_target_pairs={{0,2},{1,3},{2,0},{3,1},{4,6},{5,7},{6,4},{7,5},{8,10},{9,11},{10,... | collective-permute-start | bytes 1179656 | tf_op jit(solution)/shard_map/ppermute | solution.py:270
  8.0 0.5 collective-permute-start.5
  8.6 1.1 %copy-done = bf16[256,1344]{0,1:T(8,128)(2,1)S(1)} copy-done((bf16[256,1344]{0,1:T(8,128)(2,1)S(1)}, bf16[256,1344]{0,1:T(8,128)(2,1)}, u32[]{:S(2)}) %copy-start) | copy-done | bytes 688152
  9.7 1.1 %copy-done.1 = bf16[256,1344]{0,1:T(8,128)(2,1)S(1)} copy-done((bf16[256,1344]{0,1:T(8,128)(2,1)S(1)}, bf16[256,1344]{0,1:T(8,128)(2,1)}, u32[]{:S(2)}) %copy-start.1) | copy-done | bytes 688152
  10.8 8.8 %forward_0.1 = (f32[256,768]{1,0:T(8,128)S(1)}, f32[256,768]{1,0:T(8,128)S(1)}, bf16[256,768]{1,0:T(8,128)(2,1)S(1)}, bf16[256,768]{1,0:T(8,128)(2,1)S(1)}, bf16...) custom-call(s32[1]{0:T(128)} %bitcast.me_ref, bf16[1344,256]{1,0:T(8,128)(2,1)S(1)} %bitcast.7, ...), custom_call_target="tpu_custom_call" | custom-call | flops 1 | bytes 1 | tf_op jit(solution)/shard_map/forward_0/pallas_call | solution.py:300
  19.6 2.0 %collective-permute-start.2 = (bf16[256,768]{1,0:T(8,128)(2,1)S(1)}, bf16[256,768]{1,0:T(8,128)(2,1)S(1)}, u32[]{:S(2)}, u32[]{:S(2)}) collective-permute-start(bf16[256,768]{1,0:T(8,128)(2,1)S(1)} %collective-permute-done.refs_2_), channel_id=1, source_target_pairs={{0,2},{1,3},{2,0},{3,1},{4,6},{5,7},{6,4},{7,5},{8,10},{9,11},{10,... | collective-permute-start | bytes 1179656 | tf_op jit(solution)/shard_map/ppermute | solution.py:270
  21.7 1.5 %collective-permute-start.3 = (bf16[256,768]{1,0:T(8,128)(2,1)S(1)}, bf16[256,768]{1,0:T(8,128)(2,1)S(1)}, u32[]{:S(2)}, u32[]{:S(2)}) collective-permute-start(bf16[256,768]{1,0:T(8,128)(2,1)S(1)} %collective-permute-done.1.refs_3_), channel_id=1, source_target_pairs={{0,1},{1,0},{2,3},{3,2},{4,5},{5,4},{6,7},{7,6},{8,9},{9,8},{10,11... | collective-permute-start | bytes 1179656 | tf_op jit(solution)/shard_map/ppermute | solution.py:270
  23.8 2.3 %back_near_0.1.refs_3_ = f32[1344,256]{1,0:T(8,128)S(1)} custom-call(s32[1]{0:T(128)} %bitcast.me_ref, bf16[256,768]{1,0:T(8,128)(2,1)S(1)} %copy-done.2, bf16[256,768]{1,0:T(8,128)(2,1)S(1)} %copy-done.3, bf16[256,768]{1,0:T(8,128)(2,1)S(1)} %collective-permute-done.refs_2_, bf16[256,768]{1,0:T(8,128)(2,1)S(1)} %collective-permute-done.1.refs_3_, ...), custom_call_target="tpu_custom_call" | custom-call | flops 1 | bytes 1 | tf_op jit(solution)/shard_map/back_near_0/pallas_call | solution.py:343
  26.2 2.8 %forward_1.1 = (bf16[256,768]{1,0:T(8,128)(2,1)S(1)}, bf16[256,768]{1,0:T(8,128)(2,1)S(1)}, f32[256,768]{1,0:T(8,128)S(1)}, f32[256,768]{1,0:T(8,128)S(1)}, f32[...) custom-call(s32[1]{0:T(128)} %bitcast.me_ref, s32[1,256]{1,0:T(1,128)S(1)} %bitcast.14, ...), custom_call_target="tpu_custom_call" | custom-call | flops 1 | bytes 1 | tf_op jit(solution)/shard_map/forward_1/pallas_call | solution.py:324
  29.0 0.6 collective-permute-start.9
  30.2 1.3 %back_near_1.1.refs_3_ = f32[1344,256]{1,0:T(8,128)S(1)} custom-call(s32[1]{0:T(128)} %bitcast.me_ref, bf16[256,768]{1,0:T(8,128)(2,1)S(1)} %collective-permute-done.4.refs_0_, bf16[256,768]{1,0:T(8,128)(2,1)S(1)} %collective-permute-done.5.refs_1_, bf16[1344,6144]{1,0:T(8,128)(2,1)S(1)} %get-tuple-element.62.kept_ref.refs_4_.refs_2_, ...), custom_call_target="tpu_custom_call" | custom-call | flops 1 | bytes 1 | tf_op jit(solution)/shard_map/back_near_1/pallas_call | solution.py:343
  31.8 3.8 %collective-permute-done.2.refs_0_ = bf16[256,768]{1,0:T(8,128)(2,1)S(1)} collective-permute-done((bf16[256,768]{1,0:T(8,128)(2,1)S(1)}, bf16[256,768]{1,0:T(8,128)(2,1)S(1)}, u32[]{:S(2)}, u32[]{:S(2)}) %collective-permute-start.2) | collective-permute-done | bytes 393248 | tf_op jit(solution)/shard_map/ppermute | solution.py:270
  35.9 1.5 %collective-permute-start.8 = (f32[1,256]{1,0:T(1,128)S(1)}, f32[1,256]{1,0:T(1,128)S(1)}, u32[]{:S(2)}, u32[]{:S(2)}) collective-permute-start(f32[1,256]{1,0:T(1,128)S(1)} %dot_part.5.refs_0_), channel_id=1, source_target_pairs={{0,3},{1,2},{2,1},{3,0},{4,7},{5,6},{6,5},{7,4},{8,11},{9,10},{10,... | collective-permute-start | bytes 3080 | tf_op jit(solution)/shard_map/ppermute | solution.py:270
  37.5 1.9 %collective-permute-start.6 = (f32[1,256]{1,0:T(1,128)S(1)}, f32[1,256]{1,0:T(1,128)S(1)}, u32[]{:S(2)}, u32[]{:S(2)}) collective-permute-start(f32[1,256]{1,0:T(1,128)S(1)} %dot_part.5.refs_0_), channel_id=1, source_target_pairs={{0,1},{1,0},{2,3},{3,2},{4,5},{5,4},{6,7},{7,6},{8,9},{9,8},{10,11... | collective-permute-start | bytes 3080 | tf_op jit(solution)/shard_map/ppermute | solution.py:270
  39.4 2.7 %back_far.1 = (bf16[1344,256]{1,0:T(8,128)(2,1)}, bf16[1344,256]{1,0:T(8,128)(2,1)}) custom-call(s32[1]{0:T(128)} %bitcast.me_ref, f32[1,256]{1,0:T(1,128)S(1)} %get-tuple-element.82.prob_ref, bf16[1344,256]{1,0:T(8,128)(2,1)S(1)} %bitcast.8, bf16[1344,256]{1,0:T(8,128)(2,1)S(1)} %bitcast.10, bf16[256,768]{1,0:T(8,128)(2,1)S(1)} %collective-permute-done.2.refs_0_, ...), custom_call_target="tpu_custom_call" | custom-call | flops 1 | bytes 1 | tf_op jit(solution)/shard_map/back_far/pallas_call | solution.py:373
  42.1 0.7 %collective-permute-start.13 = (bf16[256,768]{1,0:T(8,128)(2,1)S(1)}, bf16[256,768]{1,0:T(8,128)(2,1)S(1)}, u32[]{:S(2)}, u32[]{:S(2)}) collective-permute-start(bf16[256,768]{1,0:T(8,128)(2,1)S(1)} %get-tuple-element.90.refs_6_), channel_id=1, source_target_pairs={{0,1},{1,0},{2,3},{3,2},{4,5},{5,4},{6,7},{7,6},{8,9},{9,8},{10,11... | collective-permute-start | bytes 1179656 | tf_op jit(solution)/shard_map/ppermute | solution.py:270
  42.8 1.5 %collective-permute-start.14 = (bf16[256,768]{1,0:T(8,128)(2,1)S(1)}, bf16[256,768]{1,0:T(8,128)(2,1)S(1)}, u32[]{:S(2)}, u32[]{:S(2)}) collective-permute-start(bf16[256,768]{1,0:T(8,128)(2,1)S(1)} %get-tuple-element.91.refs_7_), channel_id=1, source_target_pairs={{0,2},{1,3},{2,0},{3,1},{4,6},{5,7},{6,4},{7,5},{8,10},{9,11},{10,... | collective-permute-start | bytes 1179656 | tf_op jit(solution)/shard_map/ppermute | solution.py:270
  44.4 0.6 router_part.1
  45.1 1.2 %collective-permute-done.11 = f32[16,1536]{1,0:T(8,128)S(1)} collective-permute-done((f32[16,1536]{1,0:T(8,128)S(1)}, f32[16,1536]{1,0:T(8,128)S(1)}, u32[]{:S(2)}, u32[]{:S(2)}) %collective-permute-start.11) | collective-permute-done | bytes 98336 | tf_op jit(solution)/shard_map/ppermute | solution.py:270
  46.3 1.6 %collective-permute-start.12 = (bf16[16,1536]{1,0:T(8,128)(2,1)S(1)}, bf16[16,1536]{1,0:T(8,128)(2,1)S(1)}, u32[]{:S(2)}, u32[]{:S(2)}) collective-permute-start(bf16[16,1536]{1,0:T(8,128)(2,1)S(1)} %add_convert_fusion.3), channel_id=1, source_target_pairs={{0,8},{4,12},{8,0},{12,4},{16,24},{20,28},{24,16},{28,20},{1,9},{5... | collective-permute-start | bytes 147464 | tf_op jit(solution)/shard_map/ppermute | solution.py:270
  48.0 0.6 collective-permute-start.15
  48.6 1.4 %collective-permute-start.17 = (bf16[256,768]{1,0:T(8,128)(2,1)S(1)}, bf16[256,768]{1,0:T(8,128)(2,1)S(1)}, u32[]{:S(2)}, u32[]{:S(2)}) collective-permute-start(bf16[256,768]{1,0:T(8,128)(2,1)S(1)} %add_convert_fusion), channel_id=1, source_target_pairs={{0,1},{1,0},{2,3},{3,2},{4,5},{5,4},{6,7},{7,6},{8,9},{9,8},{10,11... | collective-permute-start | bytes 1179656 | tf_op jit(solution)/shard_map/ppermute | solution.py:270
  50.5 0.9 %collective-permute-done.13.refs_1_ = bf16[256,768]{1,0:T(8,128)(2,1)S(1)} collective-permute-done((bf16[256,768]{1,0:T(8,128)(2,1)S(1)}, bf16[256,768]{1,0:T(8,128)(2,1)S(1)}, u32[]{:S(2)}, u32[]{:S(2)}) %collective-permute-start.13) | collective-permute-done | bytes 393248 | tf_op jit(solution)/shard_map/ppermute | solution.py:270
  51.4 3.0 %collective-permute-done.14.refs_1_ = bf16[256,768]{1,0:T(8,128)(2,1)S(1)} collective-permute-done((bf16[256,768]{1,0:T(8,128)(2,1)S(1)}, bf16[256,768]{1,0:T(8,128)(2,1)S(1)}, u32[]{:S(2)}, u32[]{:S(2)}) %collective-permute-start.14) | collective-permute-done | bytes 393248 | tf_op jit(solution)/shard_map/ppermute | solution.py:270
  54.4 2.6 %collective-permute-start.16 = (bf16[16,1536]{1,0:T(8,128)(2,1)S(1)}, bf16[16,1536]{1,0:T(8,128)(2,1)S(1)}, u32[]{:S(2)}, u32[]{:S(2)}) collective-permute-start(bf16[16,1536]{1,0:T(8,128)(2,1)S(1)} %add_convert_fusion.2.refs_0_), channel_id=1, source_target_pairs={{0,16},{4,20},{8,24},{12,28},{16,0},{20,4},{24,8},{28,12},{1,17},{... | collective-permute-start | bytes 147464 | tf_op jit(solution)/shard_map/ppermute | solution.py:270
  57.0 0.5 place_0.1.placed_ref
  57.5 0.5 place_1.1.placed_ref
  58.1 1.5 %collective-permute-done.17.last_ref = bf16[256,768]{1,0:T(8,128)(2,1)S(1)} collective-permute-done((bf16[256,768]{1,0:T(8,128)(2,1)S(1)}, bf16[256,768]{1,0:T(8,128)(2,1)S(1)}, u32[]{:S(2)}, u32[]{:S(2)}) %collective-permute-start.17) | collective-permute-done | bytes 393248 | tf_op jit(solution)/shard_map/ppermute | solution.py:270
  59.5 1.1 %combine_1.1.refs_2_ = bf16[384,1536]{1,0:T(8,128)(2,1)} custom-call(f32[384,768]{1,0:T(8,128)S(1)} %place_1.1.placed_ref, bf16[384,256]{1,0:T(8,128)(2,1)S(1)} %get-tuple-element.63.pick_ref, f32[384,1]{1,0:T(8,128)S(1)} %get-tuple-element.93.weight_ref, bf16[256,768]{1,0:T(8,128)(2,1)S(1)} %collective-permute-done.17.last_ref), custom_call_target="tpu_custom_call" | custom-call | flops 1 | bytes 1 | tf_op jit(solution)/shard_map/combine_1/pallas_call | solution.py:436
  60.9 1.7 %combine_0.1 = (bf16[384,1536]{1,0:T(8,128)(2,1)}, f32[16,1536]{1,0:T(8,128)}) custom-call(f32[384,768]{1,0:T(8,128)S(1)} %place_0.1.placed_ref, bf16[384,256]{1,0:T(8,128)(2,1)S(1)} %get-tuple-element.63.pick_ref, f32[384,1]{1,0:T(8,128)S(1)} %get-tuple-element.93.weight_ref, ...), custom_call_target="tpu_custom_call", output_to_operand_aliasing={{0}: (6, {})} | custom-call | flops 1 | bytes 1 | tf_op jit(solution)/shard_map/combine_0/pallas_call | solution.py:436
  (36 shorter events, 2.4 us)
Async XLA Ops:
  3.5 16.1 %collective-permute-start = (bf16[256,768]{1,0:T(8,128)(2,1)}, bf16[256,768]{1,0:T(8,128)(2,1)S(1)}, u32[]{:S(2)}, u32[]{:S(2)}) collective-permute-start(bf16[256,768]{1,0:T(8,128)(2,1)} %get-tuple-element.58.refs_0_), channel_id=1, source_target_pairs={{0,1},{1,0},{2,3},{3,2},{4,5},{5,4},{6,7},{7,6},{8,9},{9,8},{10,11... | collective-permute-start | bytes 1179656 | tf_op jit(solution)/shard_map/ppermute | solution.py:270
  6.5 13.1 %collective-permute-start.1 = (bf16[256,768]{1,0:T(8,128)(2,1)}, bf16[256,768]{1,0:T(8,128)(2,1)S(1)}, u32[]{:S(2)}, u32[]{:S(2)}) collective-permute-start(bf16[256,768]{1,0:T(8,128)(2,1)} %get-tuple-element.59.refs_1_), channel_id=1, source_target_pairs={{0,2},{1,3},{2,0},{3,1},{4,6},{5,7},{6,4},{7,5},{8,10},{9,11},{10,... | collective-permute-start | bytes 1179656 | tf_op jit(solution)/shard_map/ppermute | solution.py:270
  8.0 21.6 %collective-permute-start.5 = (bf16[256,768]{1,0:T(8,128)(2,1)}, bf16[256,768]{1,0:T(8,128)(2,1)S(1)}, u32[]{:S(2)}, u32[]{:S(2)}) collective-permute-start(bf16[256,768]{1,0:T(8,128)(2,1)} %get-tuple-element.58.refs_0_), channel_id=1, source_target_pairs={{0,2},{1,3},{2,0},{3,1},{4,6},{5,7},{6,4},{7,5},{8,10},{9,11},{10,... | collective-permute-start | bytes 1179656 | tf_op jit(solution)/shard_map/ppermute | solution.py:270
  8.5 21.7 %collective-permute-start.4 = (bf16[256,768]{1,0:T(8,128)(2,1)}, bf16[256,768]{1,0:T(8,128)(2,1)S(1)}, u32[]{:S(2)}, u32[]{:S(2)}) collective-permute-start(bf16[256,768]{1,0:T(8,128)(2,1)} %get-tuple-element.59.refs_1_), channel_id=1, source_target_pairs={{0,1},{1,0},{2,3},{3,2},{4,5},{5,4},{6,7},{7,6},{8,9},{9,8},{10,11... | collective-permute-start | bytes 1179656 | tf_op jit(solution)/shard_map/ppermute | solution.py:270
  8.6 1.1 %copy-start = (bf16[256,1344]{0,1:T(8,128)(2,1)S(1)}, bf16[256,1344]{0,1:T(8,128)(2,1)}, u32[]{:S(2)}) copy-start(bf16[256,1344]{0,1:T(8,128)(2,1)} %param.8) | copy-start | bytes 2064388
  9.7 1.1 %copy-start.1 = (bf16[256,1344]{0,1:T(8,128)(2,1)S(1)}, bf16[256,1344]{0,1:T(8,128)(2,1)}, u32[]{:S(2)}) copy-start(bf16[256,1344]{0,1:T(8,128)(2,1)} %param.9) | copy-start | bytes 2064388
  10.8 13.0 %copy-start.2 = (bf16[256,768]{1,0:T(8,128)(2,1)S(1)}, bf16[256,768]{1,0:T(8,128)(2,1)}, u32[]{:S(2)}) copy-start(bf16[256,768]{1,0:T(8,128)(2,1)} %get-tuple-element.58.refs_0_) | copy-start | bytes 1179652
  10.8 13.0 %copy-start.3 = (bf16[256,768]{1,0:T(8,128)(2,1)S(1)}, bf16[256,768]{1,0:T(8,128)(2,1)}, u32[]{:S(2)}) copy-start(bf16[256,768]{1,0:T(8,128)(2,1)} %get-tuple-element.59.refs_1_) | copy-start | bytes 1179652
  19.6 15.9 %collective-permute-start.2 = (bf16[256,768]{1,0:T(8,128)(2,1)S(1)}, bf16[256,768]{1,0:T(8,128)(2,1)S(1)}, u32[]{:S(2)}, u32[]{:S(2)}) collective-permute-start(bf16[256,768]{1,0:T(8,128)(2,1)S(1)} %collective-permute-done.refs_2_), channel_id=1, source_target_pairs={{0,2},{1,3},{2,0},{3,1},{4,6},{5,7},{6,4},{7,5},{8,10},{9,11},{10,... | collective-permute-start | bytes 1179656 | tf_op jit(solution)/shard_map/ppermute | solution.py:270
  21.7 13.9 %collective-permute-start.3 = (bf16[256,768]{1,0:T(8,128)(2,1)S(1)}, bf16[256,768]{1,0:T(8,128)(2,1)S(1)}, u32[]{:S(2)}, u32[]{:S(2)}) collective-permute-start(bf16[256,768]{1,0:T(8,128)(2,1)S(1)} %collective-permute-done.1.refs_3_), channel_id=1, source_target_pairs={{0,1},{1,0},{2,3},{3,2},{4,5},{5,4},{6,7},{7,6},{8,9},{9,8},{10,11... | collective-permute-start | bytes 1179656 | tf_op jit(solution)/shard_map/ppermute | solution.py:270
  23.8 2.4 %copy-start.5 = (f32[384,16]{0,1:T(8,128)S(1)}, f32[384,16]{0,1:T(8,128)}, u32[]{:S(2)}) copy-start(f32[384,16]{0,1:T(8,128)} %param.13) | copy-start | bytes 73732
  23.8 2.4 %copy-start.6 = (s32[256]{0:T(256)S(1)}, s32[256]{0:T(256)}, u32[]{:S(2)}) copy-start(s32[256]{0:T(256)} %param.11) | copy-start | bytes 3076
  29.0 13.1 %collective-permute-start.9 = (bf16[256,768]{1,0:T(8,128)(2,1)S(1)}, bf16[256,768]{1,0:T(8,128)(2,1)S(1)}, u32[]{:S(2)}, u32[]{:S(2)}) collective-permute-start(bf16[256,768]{1,0:T(8,128)(2,1)S(1)} %get-tuple-element.73.refs_2_), channel_id=1, source_target_pairs={{0,1},{1,0},{2,3},{3,2},{4,5},{5,4},{6,7},{7,6},{8,9},{9,8},{10,11... | collective-permute-start | bytes 1179656 | tf_op jit(solution)/shard_map/ppermute | solution.py:270
  29.6 13.2 %collective-permute-start.10 = (bf16[256,768]{1,0:T(8,128)(2,1)S(1)}, bf16[256,768]{1,0:T(8,128)(2,1)S(1)}, u32[]{:S(2)}, u32[]{:S(2)}) collective-permute-start(bf16[256,768]{1,0:T(8,128)(2,1)S(1)} %get-tuple-element.74.refs_3_), channel_id=1, source_target_pairs={{0,2},{1,3},{2,0},{3,1},{4,6},{5,7},{6,4},{7,5},{8,10},{9,11},{10,... | collective-permute-start | bytes 1179656 | tf_op jit(solution)/shard_map/ppermute | solution.py:270
  35.9 8.5 %collective-permute-start.8 = (f32[1,256]{1,0:T(1,128)S(1)}, f32[1,256]{1,0:T(1,128)S(1)}, u32[]{:S(2)}, u32[]{:S(2)}) collective-permute-start(f32[1,256]{1,0:T(1,128)S(1)} %dot_part.5.refs_0_), channel_id=1, source_target_pairs={{0,3},{1,2},{2,1},{3,0},{4,7},{5,6},{6,5},{7,4},{8,11},{9,10},{10,... | collective-permute-start | bytes 3080 | tf_op jit(solution)/shard_map/ppermute | solution.py:270
  37.4 6.9 %collective-permute-start.7 = (f32[1,256]{1,0:T(1,128)S(1)}, f32[1,256]{1,0:T(1,128)S(1)}, u32[]{:S(2)}, u32[]{:S(2)}) collective-permute-start(f32[1,256]{1,0:T(1,128)S(1)} %dot_part.5.refs_0_), channel_id=1, source_target_pairs={{0,2},{1,3},{2,0},{3,1},{4,6},{5,7},{6,4},{7,5},{8,10},{9,11},{10,... | collective-permute-start | bytes 3080 | tf_op jit(solution)/shard_map/ppermute | solution.py:270
  37.5 6.8 %collective-permute-start.6 = (f32[1,256]{1,0:T(1,128)S(1)}, f32[1,256]{1,0:T(1,128)S(1)}, u32[]{:S(2)}, u32[]{:S(2)}) collective-permute-start(f32[1,256]{1,0:T(1,128)S(1)} %dot_part.5.refs_0_), channel_id=1, source_target_pairs={{0,1},{1,0},{2,3},{3,2},{4,5},{5,4},{6,7},{7,6},{8,9},{9,8},{10,11... | collective-permute-start | bytes 3080 | tf_op jit(solution)/shard_map/ppermute | solution.py:270
  39.4 5.0 %copy-start.4 = (bf16[384,1536]{1,0:T(8,128)(2,1)S(1)}, bf16[384,1536]{1,0:T(8,128)(2,1)}, u32[]{:S(2)}) copy-start(bf16[384,1536]{1,0:T(8,128)(2,1)} %tokens_ref.1) | copy-start | bytes 3538948
  42.1 9.2 %collective-permute-start.13 = (bf16[256,768]{1,0:T(8,128)(2,1)S(1)}, bf16[256,768]{1,0:T(8,128)(2,1)S(1)}, u32[]{:S(2)}, u32[]{:S(2)}) collective-permute-start(bf16[256,768]{1,0:T(8,128)(2,1)S(1)} %get-tuple-element.90.refs_6_), channel_id=1, source_target_pairs={{0,1},{1,0},{2,3},{3,2},{4,5},{5,4},{6,7},{7,6},{8,9},{9,8},{10,11... | collective-permute-start | bytes 1179656 | tf_op jit(solution)/shard_map/ppermute | solution.py:270
  42.8 11.5 %collective-permute-start.14 = (bf16[256,768]{1,0:T(8,128)(2,1)S(1)}, bf16[256,768]{1,0:T(8,128)(2,1)S(1)}, u32[]{:S(2)}, u32[]{:S(2)}) collective-permute-start(bf16[256,768]{1,0:T(8,128)(2,1)S(1)} %get-tuple-element.91.refs_7_), channel_id=1, source_target_pairs={{0,2},{1,3},{2,0},{3,1},{4,6},{5,7},{6,4},{7,5},{8,10},{9,11},{10,... | collective-permute-start | bytes 1179656 | tf_op jit(solution)/shard_map/ppermute | solution.py:270
  45.0 1.3 %collective-permute-start.11 = (f32[16,1536]{1,0:T(8,128)S(1)}, f32[16,1536]{1,0:T(8,128)S(1)}, u32[]{:S(2)}, u32[]{:S(2)}) collective-permute-start(f32[16,1536]{1,0:T(8,128)S(1)} %router_part.1), channel_id=1, source_target_pairs={{0,4},{4,0},{8,12},{12,8},{16,20},{20,16},{24,28},{28,24},{1,5},{5... | collective-permute-start | bytes 294920 | tf_op jit(solution)/shard_map/ppermute | solution.py:270
  46.3 4.2 %collective-permute-start.12 = (bf16[16,1536]{1,0:T(8,128)(2,1)S(1)}, bf16[16,1536]{1,0:T(8,128)(2,1)S(1)}, u32[]{:S(2)}, u32[]{:S(2)}) collective-permute-start(bf16[16,1536]{1,0:T(8,128)(2,1)S(1)} %add_convert_fusion.3), channel_id=1, source_target_pairs={{0,8},{4,12},{8,0},{12,4},{16,24},{20,28},{24,16},{28,20},{1,9},{5... | collective-permute-start | bytes 147464 | tf_op jit(solution)/shard_map/ppermute | solution.py:270
  48.0 12.9 %collective-permute-start.15 = (bf16[256,768]{1,0:T(8,128)(2,1)S(1)}, bf16[256,768]{1,0:T(8,128)(2,1)S(1)}, u32[]{:S(2)}, u32[]{:S(2)}) collective-permute-start(bf16[256,768]{1,0:T(8,128)(2,1)S(1)} %add_convert_fusion.1), channel_id=1, source_target_pairs={{0,2},{1,3},{2,0},{3,1},{4,6},{5,7},{6,4},{7,5},{8,10},{9,11},{10,... | collective-permute-start | bytes 1179656 | tf_op jit(solution)/shard_map/ppermute | solution.py:270
  48.6 10.9 %collective-permute-start.17 = (bf16[256,768]{1,0:T(8,128)(2,1)S(1)}, bf16[256,768]{1,0:T(8,128)(2,1)S(1)}, u32[]{:S(2)}, u32[]{:S(2)}) collective-permute-start(bf16[256,768]{1,0:T(8,128)(2,1)S(1)} %add_convert_fusion), channel_id=1, source_target_pairs={{0,1},{1,0},{2,3},{3,2},{4,5},{5,4},{6,7},{7,6},{8,9},{9,8},{10,11... | collective-permute-start | bytes 1179656 | tf_op jit(solution)/shard_map/ppermute | solution.py:270
  54.4 6.6 %collective-permute-start.16 = (bf16[16,1536]{1,0:T(8,128)(2,1)S(1)}, bf16[16,1536]{1,0:T(8,128)(2,1)S(1)}, u32[]{:S(2)}, u32[]{:S(2)}) collective-permute-start(bf16[16,1536]{1,0:T(8,128)(2,1)S(1)} %add_convert_fusion.2.refs_0_), channel_id=1, source_target_pairs={{0,16},{4,20},{8,24},{12,28},{16,0},{20,4},{24,8},{28,12},{1,17},{... | collective-permute-start | bytes 147464 | tf_op jit(solution)/shard_map/ppermute | solution.py:270

commit v2 on v1

--- a/solution.py
+++ b/solution.py
@@ -64,19 +64,28 @@
     return total[0:1, :]
 
 
-def gather_kernel(tok_count, row_ref, grad_ref, *refs):
-    n = len(refs) // 2
-    outs, made, sem = refs[:n], refs[n:-1], refs[-1]
+def gather_kernel(tok_count, row_hbm, grad_hbm, *refs):
+    n = (len(refs) - 3) // 2
+    outs, made, (row_ref, grad_ref, sem) = refs[:n], refs[n : 2 * n], refs[2 * n :]
+    width = outs[0].shape[1]
+    spans = [pl.ds(at * width, width) for at in range(n)]
+    fetches = [
+        pltpu.make_async_copy(grad_hbm.at[:, span], grad_ref.at[:, span], sem.at[n + at])
+        for at, span in enumerate(spans)
+    ]
+    fetch_rows = pltpu.make_async_copy(row_hbm, row_ref, sem.at[2 * n])
+    fetch_rows.start()
+    for fetch in fetches:
+        fetch.start()
+    fetch_rows.wait()
     rows = row_ref[...]
     column = jnp.broadcast_to(rows, (8, rows.shape[1])).T[:, 0:1]
     tokens = lax.broadcasted_iota(jnp.int32, (rows.shape[1], tok_count), 1)
     mask = (tokens == column).astype(F32).astype(BF16)
     puts = []
     for at, (stage, out) in enumerate(zip(made, outs)):
-        width = out.shape[1]
-        stage[...] = jnp.dot(
-            mask, grad_ref[:, at * width : (at + 1) * width], preferred_element_type=F32
-        ).astype(BF16)
+        fetches[at].wait()
+        stage[...] = jnp.dot(mask, grad_ref[:, spans[at]], preferred_element_type=F32).astype(BF16)
         puts.append(pltpu.make_async_copy(stage, out, sem.at[at]))
         puts[-1].start()
     for put in puts:
@@ -228,9 +237,16 @@
     )
 
 
-def combine_kernel(cut, n_sums, placed_ref, pick_ref, weight_ref, last_ref, *refs):
-    sums, (made, sem) = refs[:n_sums], refs[-2:]
-    out_ref = refs[-4] if n_sums else refs[-3]
+def combine_kernel(cut, has_router, placed_ref, pick_ref, weight_ref, last_ref, *refs):
+    if has_router:
+        *terms, out_ref, router_ref, made, sem, one, two, total, router_sem = refs[:2] + refs[-8:]
+        fetches = [
+            pltpu.make_async_copy(term, held, router_sem.at[at]) for at, (term, held) in enumerate(zip(terms, (one, two)))
+        ]
+        for fetch in fetches:
+            fetch.start()
+    else:
+        out_ref, made, sem = refs[-3:]
     rows, width = made.shape
     step = row_step(rows, 128)
     puts = []
@@ -242,8 +258,12 @@
             pltpu.make_async_copy(made.at[here, :], out_ref.at[here, pl.ds(cut * width, width)], sem.at[j])
         )
         puts[-1].start()
-    if n_sums:
-        refs[-3][...] = sums[0][...].astype(F32) + sums[1][...].astype(F32)
+    if has_router:
+        for fetch in fetches:
+            fetch.wait()
+        total[...] = one[...].astype(F32) + two[...].astype(F32)
+        puts.append(pltpu.make_async_copy(total, router_ref, router_sem.at[2]))
+        puts[-1].start()
     for put in puts:
         put.wait()
 
@@ -275,10 +295,15 @@
     own = pl.pallas_call(
         functools.partial(gather_kernel, tok_count),
         out_shape=[jax.ShapeDtypeStruct((slots, width), BF16)] * cuts,
-        in_specs=[vmem(), vmem()],
+        in_specs=[pl.BlockSpec(memory_space=pl.ANY)] * 2,
         out_specs=[pl.BlockSpec(memory_space=pl.ANY)] * cuts,
-        scratch_shapes=[pltpu.VMEM((slots, width), BF16)] * cuts + [pltpu.SemaphoreType.DMA((cuts,))],
-        compiler_params=params(60),
+        scratch_shapes=[pltpu.VMEM((slots, width), BF16)] * cuts
+        + [
+            pltpu.VMEM((1, slots), jnp.int32),
+            pltpu.VMEM((tok_count, feat), BF16),
+            pltpu.SemaphoreType.DMA((2 * cuts + 1,)),
+        ],
+        compiler_params=params(61),
         cost_estimate=cost(1, 1),
         name="gather_rows",
     )(rows, out_grad)
@@ -414,8 +439,8 @@
     while flip < n_dp:
         sent = router if flip == 1 else (halves[0].astype(F32) + halves[1].astype(F32)).astype(BF16)
         if square and flip == 4:
-            sent, direct_x, direct_y = lax.optimization_barrier((sent, direct_x, direct_y))
-            groups[0][1], groups[1][1] = direct_x, direct_y
+            sent, direct_x = lax.optimization_barrier((sent, direct_x))
+            groups[0][1] = direct_x
         halves = [sent, swap(sent, flip, "dp", n_dp)]
         flip *= 2
 
@@ -432,24 +457,27 @@
             name="place_%d" % cut,
         )(pick, *parts)
         before = [] if combined is None else [combined]
-        sums = halves if cut == 0 else []
-        combined, *router = pl.pallas_call(
-            functools.partial(combine_kernel, cut, len(sums)),
+        sums = halves if cut == cuts - 1 else []
+        combined, *total = pl.pallas_call(
+            functools.partial(combine_kernel, cut, bool(sums)),
             out_shape=[jax.ShapeDtypeStruct((tok_count, feat), BF16)]
             + [jax.ShapeDtypeStruct((experts, feat), F32)] * (len(sums) // 2),
-            in_specs=[vmem()] * (4 + len(sums)) + [pl.BlockSpec(memory_space=pl.ANY)] * len(before),
-            out_specs=[pl.BlockSpec(memory_space=pl.ANY)] + [vmem()] * (len(sums) // 2),
+            in_specs=[vmem()] * 4 + [pl.BlockSpec(memory_space=pl.ANY)] * len([*sums, *before]),
+            out_specs=[pl.BlockSpec(memory_space=pl.ANY)] * (1 + len(sums) // 2),
             scratch_shapes=[
                 pltpu.VMEM((tok_count, width), BF16),
                 pltpu.SemaphoreType.DMA((tok_count // row_step(tok_count, 128),)),
-            ],
+            ]
+            + [pltpu.VMEM((experts, feat), term.dtype) for term in sums]
+            + [pltpu.VMEM((experts, feat), F32), pltpu.SemaphoreType.DMA((3,))] * (len(sums) // 2),
             input_output_aliases={4 + len(sums): 0} if before else {},
             compiler_params=params(),
             cost_estimate=cost(1, 1),
             name="combine_%d" % cut,
         )(placed, pick, weight, last, *sums, *before)
-
-    return combined, dgate.T, dup.T, router[0]
+        router = total[0] if total else router
+
+    return combined, dgate.T, dup.T, router
 
 
 def solution(mesh):

time: 63 us -> 62.3 us (0.989)
  transfers between devices with their start and end apart: 18 -> 18, of which waited for: 7 -> 6; matrix products, arithmetic and copies ran while one was open for 0% -> 0% of each run, Pallas kernels for 35% -> 35%
where the time goes in v2:
time: 62.3 us; the launch traced here: 62.1 us
  Pallas kernels  25.8 us (41%)
  starting transfers between devices  21.6 us (35%)
  waiting for transfers between devices  10.7 us (17%)
  local copies, waits for them, and re-layouts  2.22 us (4%)
  between operations  1.64 us (3%)
    ppermute x18, starting transfers between devices, swap(): return lax.ppermute(value, axis, [(i, i ^ flip) for i in range(size)])  21.6 us
    ppermute x18, waiting for transfers between devices, swap(): return lax.ppermute(value, axis, [(i, i ^ flip) for i in range(size)])  10.7 us
    pallas_call x1, Pallas kernels, body(): pl.pallas_call(functools.partial(first_forward_kernel, plans[0], cuts), o...  8.82 us
    pallas_call x2, Pallas kernels, body(): pl.pallas_call(functools.partial(back_kernel, [*pieces], cuts, bool(befor...  3.65 us
    pallas_call x1, Pallas kernels, body(): pl.pallas_call(functools.partial(next_forward_kernel, plans[1], cuts), ou...  2.82 us
    pallas_call x1, Pallas kernels, body(): pl.pallas_call(functools.partial(gather_kernel, tok_count), out_shape=[ja...  2.75 us
    pallas_call x1, Pallas kernels, body(): pl.pallas_call(functools.partial(final_back_kernel, [*far], cuts), out_sh...  2.69 us
    pallas_call x2, Pallas kernels, body(): pl.pallas_call(functools.partial(combine_kernel, cut, bool(sums)), out_sh...  2.31 us
  transfers between devices with their start and end apart: 18, of which 6 were waited for; matrix products, arithmetic and copies ran while one was open for 0% of the time, Pallas kernels for 35%

profile of v2, /device:TPU:0, one launch (start us, length us, event | category | flops | bytes accessed | tf_op | source)
XLA Modules:
  0.0 62.1 jit_solution(2980873763460364984)
XLA Ops:
  0.6 2.7 %gather_rows.1 = (bf16[256,768]{1,0:T(8,128)(2,1)}, bf16[256,768]{1,0:T(8,128)(2,1)}) custom-call(s32[1,256]{1,0:T(1,128)} %bitcast.13, bf16[384,1536]{1,0:T(8,128)(2,1)} %grad_hbm.1), custom_call_target="tpu_custom_call" | custom-call | flops 1 | bytes 1 | tf_op jit(solution)/shard_map/gather_rows/pallas_call | solution.py:295
  3.4 3.0 %collective-permute-start = (bf16[256,768]{1,0:T(8,128)(2,1)}, bf16[256,768]{1,0:T(8,128)(2,1)S(1)}, u32[]{:S(2)}, u32[]{:S(2)}) collective-permute-start(bf16[256,768]{1,0:T(8,128)(2,1)} %get-tuple-element.57.refs_0_), channel_id=1, source_target_pairs={{0,1},{1,0},{2,3},{3,2},{4,5},{5,4},{6,7},{7,6},{8,9},{9,8},{10,11... | collective-permute-start | bytes 1179656 | tf_op jit(solution)/shard_map/ppermute | solution.py:290
  6.4 1.5 %collective-permute-start.1 = (bf16[256,768]{1,0:T(8,128)(2,1)}, bf16[256,768]{1,0:T(8,128)(2,1)S(1)}, u32[]{:S(2)}, u32[]{:S(2)}) collective-permute-start(bf16[256,768]{1,0:T(8,128)(2,1)} %get-tuple-element.58.refs_1_), channel_id=1, source_target_pairs={{0,2},{1,3},{2,0},{3,1},{4,6},{5,7},{6,4},{7,5},{8,10},{9,11},{10,... | collective-permute-start | bytes 1179656 | tf_op jit(solution)/shard_map/ppermute | solution.py:290
  7.9 0.5 collective-permute-start.5
  8.5 1.1 %copy-done = bf16[256,1344]{0,1:T(8,128)(2,1)S(1)} copy-done((bf16[256,1344]{0,1:T(8,128)(2,1)S(1)}, bf16[256,1344]{0,1:T(8,128)(2,1)}, u32[]{:S(2)}) %copy-start) | copy-done | bytes 688152
  9.6 1.1 %copy-done.1 = bf16[256,1344]{0,1:T(8,128)(2,1)S(1)} copy-done((bf16[256,1344]{0,1:T(8,128)(2,1)S(1)}, bf16[256,1344]{0,1:T(8,128)(2,1)}, u32[]{:S(2)}) %copy-start.1) | copy-done | bytes 688152
  10.7 8.8 %forward_0.1 = (f32[256,768]{1,0:T(8,128)S(1)}, f32[256,768]{1,0:T(8,128)S(1)}, bf16[256,768]{1,0:T(8,128)(2,1)S(1)}, bf16[256,768]{1,0:T(8,128)(2,1)S(1)}, bf16...) custom-call(s32[1]{0:T(128)} %bitcast.me_ref, bf16[1344,256]{1,0:T(8,128)(2,1)S(1)} %bitcast.7, ...), custom_call_target="tpu_custom_call" | custom-call | flops 1 | bytes 1 | tf_op jit(solution)/shard_map/forward_0/pallas_call | solution.py:325
  19.6 2.0 %collective-permute-start.2 = (bf16[256,768]{1,0:T(8,128)(2,1)S(1)}, bf16[256,768]{1,0:T(8,128)(2,1)S(1)}, u32[]{:S(2)}, u32[]{:S(2)}) collective-permute-start(bf16[256,768]{1,0:T(8,128)(2,1)S(1)} %collective-permute-done.refs_2_), channel_id=1, source_target_pairs={{0,2},{1,3},{2,0},{3,1},{4,6},{5,7},{6,4},{7,5},{8,10},{9,11},{10,... | collective-permute-start | bytes 1179656 | tf_op jit(solution)/shard_map/ppermute | solution.py:290
  21.6 1.5 %collective-permute-start.3 = (bf16[256,768]{1,0:T(8,128)(2,1)S(1)}, bf16[256,768]{1,0:T(8,128)(2,1)S(1)}, u32[]{:S(2)}, u32[]{:S(2)}) collective-permute-start(bf16[256,768]{1,0:T(8,128)(2,1)S(1)} %collective-permute-done.1.refs_3_), channel_id=1, source_target_pairs={{0,1},{1,0},{2,3},{3,2},{4,5},{5,4},{6,7},{7,6},{8,9},{9,8},{10,11... | collective-permute-start | bytes 1179656 | tf_op jit(solution)/shard_map/ppermute | solution.py:290
  23.8 2.3 %back_near_0.1.refs_3_ = f32[1344,256]{1,0:T(8,128)S(1)} custom-call(s32[1]{0:T(128)} %bitcast.me_ref, bf16[256,768]{1,0:T(8,128)(2,1)S(1)} %copy-done.2, bf16[256,768]{1,0:T(8,128)(2,1)S(1)} %copy-done.3, bf16[256,768]{1,0:T(8,128)(2,1)S(1)} %collective-permute-done.refs_2_, bf16[256,768]{1,0:T(8,128)(2,1)S(1)} %collective-permute-done.1.refs_3_, ...), custom_call_target="tpu_custom_call" | custom-call | flops 1 | bytes 1 | tf_op jit(solution)/shard_map/back_near_0/pallas_call | solution.py:368
  26.1 2.8 %forward_1.1 = (bf16[256,768]{1,0:T(8,128)(2,1)S(1)}, bf16[256,768]{1,0:T(8,128)(2,1)S(1)}, f32[256,768]{1,0:T(8,128)S(1)}, f32[256,768]{1,0:T(8,128)S(1)}, f32[...) custom-call(s32[1]{0:T(128)} %bitcast.me_ref, s32[1,256]{1,0:T(1,128)S(1)} %bitcast.14, ...), custom_call_target="tpu_custom_call" | custom-call | flops 1 | bytes 1 | tf_op jit(solution)/shard_map/forward_1/pallas_call | solution.py:349
  29.0 0.6 collective-permute-start.9
  30.1 1.3 %back_near_1.1.refs_3_ = f32[1344,256]{1,0:T(8,128)S(1)} custom-call(s32[1]{0:T(128)} %bitcast.me_ref, bf16[256,768]{1,0:T(8,128)(2,1)S(1)} %collective-permute-done.4.refs_0_, bf16[256,768]{1,0:T(8,128)(2,1)S(1)} %collective-permute-done.5.refs_1_, bf16[1344,6144]{1,0:T(8,128)(2,1)S(1)} %get-tuple-element.61.kept_ref.refs_4_.refs_2_, ...), custom_call_target="tpu_custom_call" | custom-call | flops 1 | bytes 1 | tf_op jit(solution)/shard_map/back_near_1/pallas_call | solution.py:368
  31.7 3.8 %collective-permute-done.2.refs_0_ = bf16[256,768]{1,0:T(8,128)(2,1)S(1)} collective-permute-done((bf16[256,768]{1,0:T(8,128)(2,1)S(1)}, bf16[256,768]{1,0:T(8,128)(2,1)S(1)}, u32[]{:S(2)}, u32[]{:S(2)}) %collective-permute-start.2) | collective-permute-done | bytes 393248 | tf_op jit(solution)/shard_map/ppermute | solution.py:290
  35.8 1.5 %collective-permute-start.8 = (f32[1,256]{1,0:T(1,128)S(1)}, f32[1,256]{1,0:T(1,128)S(1)}, u32[]{:S(2)}, u32[]{:S(2)}) collective-permute-start(f32[1,256]{1,0:T(1,128)S(1)} %dot_part.5.refs_0_), channel_id=1, source_target_pairs={{0,3},{1,2},{2,1},{3,0},{4,7},{5,6},{6,5},{7,4},{8,11},{9,10},{10,... | collective-permute-start | bytes 3080 | tf_op jit(solution)/shard_map/ppermute | solution.py:290
  37.5 1.9 %collective-permute-start.6 = (f32[1,256]{1,0:T(1,128)S(1)}, f32[1,256]{1,0:T(1,128)S(1)}, u32[]{:S(2)}, u32[]{:S(2)}) collective-permute-start(f32[1,256]{1,0:T(1,128)S(1)} %dot_part.5.refs_0_), channel_id=1, source_target_pairs={{0,1},{1,0},{2,3},{3,2},{4,5},{5,4},{6,7},{7,6},{8,9},{9,8},{10,11... | collective-permute-start | bytes 3080 | tf_op jit(solution)/shard_map/ppermute | solution.py:290
  39.4 2.7 %back_far.1 = (bf16[1344,256]{1,0:T(8,128)(2,1)}, bf16[1344,256]{1,0:T(8,128)(2,1)}) custom-call(s32[1]{0:T(128)} %bitcast.me_ref, f32[1,256]{1,0:T(1,128)S(1)} %get-tuple-element.81.prob_ref, bf16[1344,256]{1,0:T(8,128)(2,1)S(1)} %bitcast.8, bf16[1344,256]{1,0:T(8,128)(2,1)S(1)} %bitcast.10, bf16[256,768]{1,0:T(8,128)(2,1)S(1)} %collective-permute-done.2.refs_0_, ...), custom_call_target="tpu_custom_call" | custom-call | flops 1 | bytes 1 | tf_op jit(solution)/shard_map/back_far/pallas_call | solution.py:398
  42.1 0.7 %collective-permute-start.13 = (bf16[256,768]{1,0:T(8,128)(2,1)S(1)}, bf16[256,768]{1,0:T(8,128)(2,1)S(1)}, u32[]{:S(2)}, u32[]{:S(2)}) collective-permute-start(bf16[256,768]{1,0:T(8,128)(2,1)S(1)} %get-tuple-element.89.refs_6_), channel_id=1, source_target_pairs={{0,1},{1,0},{2,3},{3,2},{4,5},{5,4},{6,7},{7,6},{8,9},{9,8},{10,11... | collective-permute-start | bytes 1179656 | tf_op jit(solution)/shard_map/ppermute | solution.py:290
  42.8 1.5 %collective-permute-start.15 = (bf16[256,768]{1,0:T(8,128)(2,1)S(1)}, bf16[256,768]{1,0:T(8,128)(2,1)S(1)}, u32[]{:S(2)}, u32[]{:S(2)}) collective-permute-start(bf16[256,768]{1,0:T(8,128)(2,1)S(1)} %get-tuple-element.93.refs_7_), channel_id=1, source_target_pairs={{0,2},{1,3},{2,0},{3,1},{4,6},{5,7},{6,4},{7,5},{8,10},{9,11},{10,... | collective-permute-start | bytes 1179656 | tf_op jit(solution)/shard_map/ppermute | solution.py:290
  44.3 0.6 router_part.1
  45.0 1.2 %collective-permute-done.11 = f32[16,1536]{1,0:T(8,128)S(1)} collective-permute-done((f32[16,1536]{1,0:T(8,128)S(1)}, f32[16,1536]{1,0:T(8,128)S(1)}, u32[]{:S(2)}, u32[]{:S(2)}) %collective-permute-start.11) | collective-permute-done | bytes 98336 | tf_op jit(solution)/shard_map/ppermute | solution.py:290
  46.2 1.6 %collective-permute-start.12 = (bf16[16,1536]{1,0:T(8,128)(2,1)S(1)}, bf16[16,1536]{1,0:T(8,128)(2,1)S(1)}, u32[]{:S(2)}, u32[]{:S(2)}) collective-permute-start(bf16[16,1536]{1,0:T(8,128)(2,1)S(1)} %add_convert_fusion.3), channel_id=1, source_target_pairs={{0,8},{4,12},{8,0},{12,4},{16,24},{20,28},{24,16},{28,20},{1,9},{5... | collective-permute-start | bytes 147464 | tf_op jit(solution)/shard_map/ppermute | solution.py:290
  48.0 0.6 collective-permute-start.14
  48.5 1.4 %collective-permute-start.16 = (bf16[256,768]{1,0:T(8,128)(2,1)S(1)}, bf16[256,768]{1,0:T(8,128)(2,1)S(1)}, u32[]{:S(2)}, u32[]{:S(2)}) collective-permute-start(bf16[256,768]{1,0:T(8,128)(2,1)S(1)} %add_convert_fusion), channel_id=1, source_target_pairs={{0,1},{1,0},{2,3},{3,2},{4,5},{5,4},{6,7},{7,6},{8,9},{9,8},{10,11... | collective-permute-start | bytes 1179656 | tf_op jit(solution)/shard_map/ppermute | solution.py:290
  49.9 0.5 collective-permute-done.12
  50.4 0.9 %collective-permute-done.13.refs_1_ = bf16[256,768]{1,0:T(8,128)(2,1)S(1)} collective-permute-done((bf16[256,768]{1,0:T(8,128)(2,1)S(1)}, bf16[256,768]{1,0:T(8,128)(2,1)S(1)}, u32[]{:S(2)}, u32[]{:S(2)}) %collective-permute-start.13) | collective-permute-done | bytes 393248 | tf_op jit(solution)/shard_map/ppermute | solution.py:290
  51.3 2.9 %collective-permute-start.17 = (bf16[16,1536]{1,0:T(8,128)(2,1)S(1)}, bf16[16,1536]{1,0:T(8,128)(2,1)S(1)}, u32[]{:S(2)}, u32[]{:S(2)}) collective-permute-start(bf16[16,1536]{1,0:T(8,128)(2,1)S(1)} %add_convert_fusion.2.refs_0_), channel_id=1, source_target_pairs={{0,16},{4,20},{8,24},{12,28},{16,0},{20,4},{24,8},{28,12},{1,17},{... | collective-permute-start | bytes 147464 | tf_op jit(solution)/shard_map/ppermute | solution.py:290
  54.3 0.5 place_0.1.placed_ref
  54.8 0.5 place_1.1.placed_ref
  55.4 4.1 %collective-permute-done.16.last_ref = bf16[256,768]{1,0:T(8,128)(2,1)S(1)} collective-permute-done((bf16[256,768]{1,0:T(8,128)(2,1)S(1)}, bf16[256,768]{1,0:T(8,128)(2,1)S(1)}, u32[]{:S(2)}, u32[]{:S(2)}) %collective-permute-start.16) | collective-permute-done | bytes 393248 | tf_op jit(solution)/shard_map/ppermute | solution.py:290
  59.5 1.2 %combine_1.1 = (bf16[384,1536]{1,0:T(8,128)(2,1)}, f32[16,1536]{1,0:T(8,128)}) custom-call(f32[384,768]{1,0:T(8,128)S(1)} %place_1.1.placed_ref, bf16[384,256]{1,0:T(8,128)(2,1)S(1)} %get-tuple-element.62.pick_ref, f32[384,1]{1,0:T(8,128)S(1)} %get-tuple-element.91.weight_ref, bf16[256,768]{1,0:T(8,128)(2,1)S(1)} %collective-permute-done.16.last_ref, ...), custom_call_target="tpu_custom_call" | custom-call | flops 1 | bytes 1 | tf_op jit(solution)/shard_map/combine_1/pallas_call | solution.py:461
  60.9 1.1 %combine_0.1 = bf16[384,1536]{1,0:T(8,128)(2,1)} custom-call(f32[384,768]{1,0:T(8,128)S(1)} %place_0.1.placed_ref, bf16[384,256]{1,0:T(8,128)(2,1)S(1)} %get-tuple-element.62.pick_ref, f32[384,1]{1,0:T(8,128)S(1)} %get-tuple-element.91.weight_ref, bf16[256,768]{1,0:T(8,128)(2,1)S(1)} %collective-permute-done.14.last_ref, ...), custom_call_target="tpu_custom_call", output_to_operand_aliasing={{}: (4, {})} | custom-call | flops 1 | bytes 1 | tf_op jit(solution)/shard_map/combine_0/pallas_call | solution.py:461
  (36 shorter events, 1.7 us)
Async XLA Ops:
  3.4 16.1 %collective-permute-start = (bf16[256,768]{1,0:T(8,128)(2,1)}, bf16[256,768]{1,0:T(8,128)(2,1)S(1)}, u32[]{:S(2)}, u32[]{:S(2)}) collective-permute-start(bf16[256,768]{1,0:T(8,128)(2,1)} %get-tuple-element.57.refs_0_), channel_id=1, source_target_pairs={{0,1},{1,0},{2,3},{3,2},{4,5},{5,4},{6,7},{7,6},{8,9},{9,8},{10,11... | collective-permute-start | bytes 1179656 | tf_op jit(solution)/shard_map/ppermute | solution.py:290
  6.4 13.2 %collective-permute-start.1 = (bf16[256,768]{1,0:T(8,128)(2,1)}, bf16[256,768]{1,0:T(8,128)(2,1)S(1)}, u32[]{:S(2)}, u32[]{:S(2)}) collective-permute-start(bf16[256,768]{1,0:T(8,128)(2,1)} %get-tuple-element.58.refs_1_), channel_id=1, source_target_pairs={{0,2},{1,3},{2,0},{3,1},{4,6},{5,7},{6,4},{7,5},{8,10},{9,11},{10,... | collective-permute-start | bytes 1179656 | tf_op jit(solution)/shard_map/ppermute | solution.py:290
  7.9 21.6 %collective-permute-start.5 = (bf16[256,768]{1,0:T(8,128)(2,1)}, bf16[256,768]{1,0:T(8,128)(2,1)S(1)}, u32[]{:S(2)}, u32[]{:S(2)}) collective-permute-start(bf16[256,768]{1,0:T(8,128)(2,1)} %get-tuple-element.57.refs_0_), channel_id=1, source_target_pairs={{0,2},{1,3},{2,0},{3,1},{4,6},{5,7},{6,4},{7,5},{8,10},{9,11},{10,... | collective-permute-start | bytes 1179656 | tf_op jit(solution)/shard_map/ppermute | solution.py:290
  8.4 21.7 %collective-permute-start.4 = (bf16[256,768]{1,0:T(8,128)(2,1)}, bf16[256,768]{1,0:T(8,128)(2,1)S(1)}, u32[]{:S(2)}, u32[]{:S(2)}) collective-permute-start(bf16[256,768]{1,0:T(8,128)(2,1)} %get-tuple-element.58.refs_1_), channel_id=1, source_target_pairs={{0,1},{1,0},{2,3},{3,2},{4,5},{5,4},{6,7},{7,6},{8,9},{9,8},{10,11... | collective-permute-start | bytes 1179656 | tf_op jit(solution)/shard_map/ppermute | solution.py:290
  8.5 1.1 %copy-start = (bf16[256,1344]{0,1:T(8,128)(2,1)S(1)}, bf16[256,1344]{0,1:T(8,128)(2,1)}, u32[]{:S(2)}) copy-start(bf16[256,1344]{0,1:T(8,128)(2,1)} %param.8) | copy-start | bytes 2064388
  9.6 1.1 %copy-start.1 = (bf16[256,1344]{0,1:T(8,128)(2,1)S(1)}, bf16[256,1344]{0,1:T(8,128)(2,1)}, u32[]{:S(2)}) copy-start(bf16[256,1344]{0,1:T(8,128)(2,1)} %param.9) | copy-start | bytes 2064388
  10.7 13.0 %copy-start.2 = (bf16[256,768]{1,0:T(8,128)(2,1)S(1)}, bf16[256,768]{1,0:T(8,128)(2,1)}, u32[]{:S(2)}) copy-start(bf16[256,768]{1,0:T(8,128)(2,1)} %get-tuple-element.57.refs_0_) | copy-start | bytes 1179652
  10.7 13.0 %copy-start.3 = (bf16[256,768]{1,0:T(8,128)(2,1)S(1)}, bf16[256,768]{1,0:T(8,128)(2,1)}, u32[]{:S(2)}) copy-start(bf16[256,768]{1,0:T(8,128)(2,1)} %get-tuple-element.58.refs_1_) | copy-start | bytes 1179652
  19.6 15.9 %collective-permute-start.2 = (bf16[256,768]{1,0:T(8,128)(2,1)S(1)}, bf16[256,768]{1,0:T(8,128)(2,1)S(1)}, u32[]{:S(2)}, u32[]{:S(2)}) collective-permute-start(bf16[256,768]{1,0:T(8,128)(2,1)S(1)} %collective-permute-done.refs_2_), channel_id=1, source_target_pairs={{0,2},{1,3},{2,0},{3,1},{4,6},{5,7},{6,4},{7,5},{8,10},{9,11},{10,... | collective-permute-start | bytes 1179656 | tf_op jit(solution)/shard_map/ppermute | solution.py:290
  21.6 13.9 %collective-permute-start.3 = (bf16[256,768]{1,0:T(8,128)(2,1)S(1)}, bf16[256,768]{1,0:T(8,128)(2,1)S(1)}, u32[]{:S(2)}, u32[]{:S(2)}) collective-permute-start(bf16[256,768]{1,0:T(8,128)(2,1)S(1)} %collective-permute-done.1.refs_3_), channel_id=1, source_target_pairs={{0,1},{1,0},{2,3},{3,2},{4,5},{5,4},{6,7},{7,6},{8,9},{9,8},{10,11... | collective-permute-start | bytes 1179656 | tf_op jit(solution)/shard_map/ppermute | solution.py:290
  23.8 2.4 %copy-start.5 = (f32[384,16]{0,1:T(8,128)S(1)}, f32[384,16]{0,1:T(8,128)}, u32[]{:S(2)}) copy-start(f32[384,16]{0,1:T(8,128)} %param.13) | copy-start | bytes 73732
  23.8 2.4 %copy-start.6 = (s32[256]{0:T(256)S(1)}, s32[256]{0:T(256)}, u32[]{:S(2)}) copy-start(s32[256]{0:T(256)} %param.11) | copy-start | bytes 3076
  29.0 13.1 %collective-permute-start.9 = (bf16[256,768]{1,0:T(8,128)(2,1)S(1)}, bf16[256,768]{1,0:T(8,128)(2,1)S(1)}, u32[]{:S(2)}, u32[]{:S(2)}) collective-permute-start(bf16[256,768]{1,0:T(8,128)(2,1)S(1)} %get-tuple-element.72.refs_2_), channel_id=1, source_target_pairs={{0,1},{1,0},{2,3},{3,2},{4,5},{5,4},{6,7},{7,6},{8,9},{9,8},{10,11... | collective-permute-start | bytes 1179656 | tf_op jit(solution)/shard_map/ppermute | solution.py:290
  29.6 13.2 %collective-permute-start.10 = (bf16[256,768]{1,0:T(8,128)(2,1)S(1)}, bf16[256,768]{1,0:T(8,128)(2,1)S(1)}, u32[]{:S(2)}, u32[]{:S(2)}) collective-permute-start(bf16[256,768]{1,0:T(8,128)(2,1)S(1)} %get-tuple-element.73.refs_3_), channel_id=1, source_target_pairs={{0,2},{1,3},{2,0},{3,1},{4,6},{5,7},{6,4},{7,5},{8,10},{9,11},{10,... | collective-permute-start | bytes 1179656 | tf_op jit(solution)/shard_map/ppermute | solution.py:290
  35.8 8.5 %collective-permute-start.8 = (f32[1,256]{1,0:T(1,128)S(1)}, f32[1,256]{1,0:T(1,128)S(1)}, u32[]{:S(2)}, u32[]{:S(2)}) collective-permute-start(f32[1,256]{1,0:T(1,128)S(1)} %dot_part.5.refs_0_), channel_id=1, source_target_pairs={{0,3},{1,2},{2,1},{3,0},{4,7},{5,6},{6,5},{7,4},{8,11},{9,10},{10,... | collective-permute-start | bytes 3080 | tf_op jit(solution)/shard_map/ppermute | solution.py:290
  37.3 6.9 %collective-permute-start.7 = (f32[1,256]{1,0:T(1,128)S(1)}, f32[1,256]{1,0:T(1,128)S(1)}, u32[]{:S(2)}, u32[]{:S(2)}) collective-permute-start(f32[1,256]{1,0:T(1,128)S(1)} %dot_part.5.refs_0_), channel_id=1, source_target_pairs={{0,2},{1,3},{2,0},{3,1},{4,6},{5,7},{6,4},{7,5},{8,10},{9,11},{10,... | collective-permute-start | bytes 3080 | tf_op jit(solution)/shard_map/ppermute | solution.py:290
  37.5 6.8 %collective-permute-start.6 = (f32[1,256]{1,0:T(1,128)S(1)}, f32[1,256]{1,0:T(1,128)S(1)}, u32[]{:S(2)}, u32[]{:S(2)}) collective-permute-start(f32[1,256]{1,0:T(1,128)S(1)} %dot_part.5.refs_0_), channel_id=1, source_target_pairs={{0,1},{1,0},{2,3},{3,2},{4,5},{5,4},{6,7},{7,6},{8,9},{9,8},{10,11... | collective-permute-start | bytes 3080 | tf_op jit(solution)/shard_map/ppermute | solution.py:290
  39.3 5.0 %copy-start.4 = (bf16[384,1536]{1,0:T(8,128)(2,1)S(1)}, bf16[384,1536]{1,0:T(8,128)(2,1)}, u32[]{:S(2)}) copy-start(bf16[384,1536]{1,0:T(8,128)(2,1)} %tokens_ref.1) | copy-start | bytes 3538948
  42.1 9.3 %collective-permute-start.13 = (bf16[256,768]{1,0:T(8,128)(2,1)S(1)}, bf16[256,768]{1,0:T(8,128)(2,1)S(1)}, u32[]{:S(2)}, u32[]{:S(2)}) collective-permute-start(bf16[256,768]{1,0:T(8,128)(2,1)S(1)} %get-tuple-element.89.refs_6_), channel_id=1, source_target_pairs={{0,1},{1,0},{2,3},{3,2},{4,5},{5,4},{6,7},{7,6},{8,9},{9,8},{10,11... | collective-permute-start | bytes 1179656 | tf_op jit(solution)/shard_map/ppermute | solution.py:290
  42.8 12.0 %collective-permute-start.15 = (bf16[256,768]{1,0:T(8,128)(2,1)S(1)}, bf16[256,768]{1,0:T(8,128)(2,1)S(1)}, u32[]{:S(2)}, u32[]{:S(2)}) collective-permute-start(bf16[256,768]{1,0:T(8,128)(2,1)S(1)} %get-tuple-element.93.refs_7_), channel_id=1, source_target_pairs={{0,2},{1,3},{2,0},{3,1},{4,6},{5,7},{6,4},{7,5},{8,10},{9,11},{10,... | collective-permute-start | bytes 1179656 | tf_op jit(solution)/shard_map/ppermute | solution.py:290
  44.9 1.3 %collective-permute-start.11 = (f32[16,1536]{1,0:T(8,128)S(1)}, f32[16,1536]{1,0:T(8,128)S(1)}, u32[]{:S(2)}, u32[]{:S(2)}) collective-permute-start(f32[16,1536]{1,0:T(8,128)S(1)} %router_part.1), channel_id=1, source_target_pairs={{0,4},{4,0},{8,12},{12,8},{16,20},{20,16},{24,28},{28,24},{1,5},{5... | collective-permute-start | bytes 294920 | tf_op jit(solution)/shard_map/ppermute | solution.py:290
  46.2 4.2 %collective-permute-start.12 = (bf16[16,1536]{1,0:T(8,128)(2,1)S(1)}, bf16[16,1536]{1,0:T(8,128)(2,1)S(1)}, u32[]{:S(2)}, u32[]{:S(2)}) collective-permute-start(bf16[16,1536]{1,0:T(8,128)(2,1)S(1)} %add_convert_fusion.3), channel_id=1, source_target_pairs={{0,8},{4,12},{8,0},{12,4},{16,24},{20,28},{24,16},{28,20},{1,9},{5... | collective-permute-start | bytes 147464 | tf_op jit(solution)/shard_map/ppermute | solution.py:290
  48.0 12.9 %collective-permute-start.14 = (bf16[256,768]{1,0:T(8,128)(2,1)S(1)}, bf16[256,768]{1,0:T(8,128)(2,1)S(1)}, u32[]{:S(2)}, u32[]{:S(2)}) collective-permute-start(bf16[256,768]{1,0:T(8,128)(2,1)S(1)} %add_convert_fusion.1), channel_id=1, source_target_pairs={{0,2},{1,3},{2,0},{3,1},{4,6},{5,7},{6,4},{7,5},{8,10},{9,11},{10,... | collective-permute-start | bytes 1179656 | tf_op jit(solution)/shard_map/ppermute | solution.py:290
  48.5 11.0 %collective-permute-start.16 = (bf16[256,768]{1,0:T(8,128)(2,1)S(1)}, bf16[256,768]{1,0:T(8,128)(2,1)S(1)}, u32[]{:S(2)}, u32[]{:S(2)}) collective-permute-start(bf16[256,768]{1,0:T(8,128)(2,1)S(1)} %add_convert_fusion), channel_id=1, source_target_pairs={{0,1},{1,0},{2,3},{3,2},{4,5},{5,4},{6,7},{7,6},{8,9},{9,8},{10,11... | collective-permute-start | bytes 1179656 | tf_op jit(solution)/shard_map/ppermute | solution.py:290
  51.3 8.2 %collective-permute-start.17 = (bf16[16,1536]{1,0:T(8,128)(2,1)S(1)}, bf16[16,1536]{1,0:T(8,128)(2,1)S(1)}, u32[]{:S(2)}, u32[]{:S(2)}) collective-permute-start(bf16[16,1536]{1,0:T(8,128)(2,1)S(1)} %add_convert_fusion.2.refs_0_), channel_id=1, source_target_pairs={{0,16},{4,20},{8,24},{12,28},{16,0},{20,4},{24,8},{28,12},{1,17},{... | collective-permute-start | bytes 147464 | tf_op jit(solution)/shard_map/ppermute | solution.py:290

commit v3 on v2

--- a/solution.py
+++ b/solution.py
@@ -64,32 +64,19 @@
     return total[0:1, :]
 
 
-def gather_kernel(tok_count, row_hbm, grad_hbm, *refs):
-    n = (len(refs) - 3) // 2
-    outs, made, (row_ref, grad_ref, sem) = refs[:n], refs[n : 2 * n], refs[2 * n :]
-    width = outs[0].shape[1]
-    spans = [pl.ds(at * width, width) for at in range(n)]
-    fetches = [
-        pltpu.make_async_copy(grad_hbm.at[:, span], grad_ref.at[:, span], sem.at[n + at])
-        for at, span in enumerate(spans)
-    ]
-    fetch_rows = pltpu.make_async_copy(row_hbm, row_ref, sem.at[2 * n])
-    fetch_rows.start()
-    for fetch in fetches:
-        fetch.start()
-    fetch_rows.wait()
+def mask_kernel(row_ref, mask_ref):
     rows = row_ref[...]
     column = jnp.broadcast_to(rows, (8, rows.shape[1])).T[:, 0:1]
-    tokens = lax.broadcasted_iota(jnp.int32, (rows.shape[1], tok_count), 1)
-    mask = (tokens == column).astype(F32).astype(BF16)
-    puts = []
-    for at, (stage, out) in enumerate(zip(made, outs)):
-        fetches[at].wait()
-        stage[...] = jnp.dot(mask, grad_ref[:, spans[at]], preferred_element_type=F32).astype(BF16)
-        puts.append(pltpu.make_async_copy(stage, out, sem.at[at]))
-        puts[-1].start()
-    for put in puts:
-        put.wait()
+    tokens = lax.broadcasted_iota(jnp.int32, mask_ref.shape, 1)
+    mask_ref[...] = (tokens == column).astype(F32).astype(BF16)
+
+
+def gather_kernel(mask_ref, grad_ref, *outs):
+    for at, out in enumerate(outs):
+        width = out.shape[1]
+        out[...] = jnp.dot(
+            mask_ref[...], grad_ref[:, at * width : (at + 1) * width], preferred_element_type=F32
+        ).astype(BF16)
 
 
 def depth_parts(hid):
@@ -292,21 +279,24 @@
     rows = row_token.reshape(1, slots)
     gate_t, up_t, logits_t = pre_gate.T, pre_up.T, router_logits.T
 
+    places = pl.pallas_call(
+        mask_kernel,
+        out_shape=jax.ShapeDtypeStruct((slots, tok_count), BF16),
+        in_specs=[vmem()],
+        out_specs=vmem(),
+        compiler_params=params(),
+        cost_estimate=cost(10**10, 1),
+        name="token_mask",
+    )(rows)
     own = pl.pallas_call(
-        functools.partial(gather_kernel, tok_count),
+        gather_kernel,
         out_shape=[jax.ShapeDtypeStruct((slots, width), BF16)] * cuts,
-        in_specs=[pl.BlockSpec(memory_space=pl.ANY)] * 2,
-        out_specs=[pl.BlockSpec(memory_space=pl.ANY)] * cuts,
-        scratch_shapes=[pltpu.VMEM((slots, width), BF16)] * cuts
-        + [
-            pltpu.VMEM((1, slots), jnp.int32),
-            pltpu.VMEM((tok_count, feat), BF16),
-            pltpu.SemaphoreType.DMA((2 * cuts + 1,)),
-        ],
-        compiler_params=params(61),
+        in_specs=[vmem(), vmem()],
+        out_specs=[vmem()] * cuts,
+        compiler_params=params(),
         cost_estimate=cost(1, 1),
         name="gather_rows",
-    )(rows, out_grad)
+    )(places, out_grad)
 
     spot, *own = lax.optimization_barrier((me.reshape(1), *own))
 

time: 62.3 us -> 62 us (level)
  waiting for transfers between devices: 10.7 us -> 13.5 us
  Pallas kernels: 25.8 us -> 23.8 us
    ppermute x18, waiting for transfers between devices: 10.7 us -> 13.5 us  [swap(): return lax.ppermute(value, axis, [(i, i ^ flip) for i in range(size)])]
    pallas_call x1 -> x2, Pallas kernels: 2.75 us -> 0.81 us  [the longest x1 0.56 us: body(): pl.pallas_call(gather_kernel, out_shape=[jax.ShapeDtypeStruct((slots, wid...]
where the time goes in v3:
time: 62 us; the launch traced here: 61.8 us
  Pallas kernels  23.8 us (38%)
  starting transfers between devices  21 us (34%)
  waiting for transfers between devices  13.5 us (22%)
  local copies, waits for them, and re-layouts  1.71 us (3%)
  between operations  1.64 us (3%)
    ppermute x18, starting transfers between devices, swap(): return lax.ppermute(value, axis, [(i, i ^ flip) for i in range(size)])  21 us
    ppermute x18, waiting for transfers between devices, swap(): return lax.ppermute(value, axis, [(i, i ^ flip) for i in range(size)])  13.5 us
    pallas_call x1, Pallas kernels, body(): pl.pallas_call(functools.partial(first_forward_kernel, plans[0], cuts), o...  8.75 us
    pallas_call x2, Pallas kernels, body(): pl.pallas_call(functools.partial(back_kernel, [*pieces], cuts, bool(befor...  3.64 us
    pallas_call x1, Pallas kernels, body(): pl.pallas_call(functools.partial(next_forward_kernel, plans[1], cuts), ou...  2.82 us
    pallas_call x1, Pallas kernels, body(): pl.pallas_call(functools.partial(final_back_kernel, [*far], cuts), out_sh...  2.68 us
    pallas_call x2, Pallas kernels, body(): pl.pallas_call(functools.partial(combine_kernel, cut, bool(sums)), out_sh...  2.32 us
    unnamed x14, local copies, waits for them, and re-layouts  1.71 us
  transfers between devices with their start and end apart: 18, of which 6 were waited for; matrix products, arithmetic and copies ran while one was open for 0% of the time, Pallas kernels for 35%

profile of v3, /device:TPU:0, one launch (start us, length us, event | category | flops | bytes accessed | tf_op | source)
XLA Modules:
  0.0 61.8 jit_solution(9602409555185685291)
XLA Ops:
  0.6 0.7 %copy-done.5 = s32[256]{0:T(256)S(1)} copy-done((s32[256]{0:T(256)S(1)}, s32[256]{0:T(256)}, u32[]{:S(2)}) %copy-start.5) | copy-done | bytes 1048
  1.6 1.0 %copy-done.3 = bf16[384,1536]{1,0:T(8,128)(2,1)S(1)} copy-done((bf16[384,1536]{1,0:T(8,128)(2,1)S(1)}, bf16[384,1536]{1,0:T(8,128)(2,1)}, u32[]{:S(2)}) %copy-start.3) | copy-done | bytes 1179672
  2.6 0.6 gather_rows.1
  3.2 3.0 %collective-permute-start = (bf16[256,768]{1,0:T(8,128)(2,1)S(1)}, bf16[256,768]{1,0:T(8,128)(2,1)S(1)}, u32[]{:S(2)}, u32[]{:S(2)}) collective-permute-start(bf16[256,768]{1,0:T(8,128)(2,1)S(1)} %get-tuple-element.57.refs_0_), channel_id=1, source_target_pairs={{0,1},{1,0},{2,3},{3,2},{4,5},{5,4},{6,7},{7,6},{8,9},{9,8},{10,11... | collective-permute-start | bytes 1179656 | tf_op jit(solution)/shard_map/ppermute | solution.py:277
  6.2 1.5 %collective-permute-start.1 = (bf16[256,768]{1,0:T(8,128)(2,1)S(1)}, bf16[256,768]{1,0:T(8,128)(2,1)S(1)}, u32[]{:S(2)}, u32[]{:S(2)}) collective-permute-start(bf16[256,768]{1,0:T(8,128)(2,1)S(1)} %get-tuple-element.58.refs_1_), channel_id=1, source_target_pairs={{0,2},{1,3},{2,0},{3,1},{4,6},{5,7},{6,4},{7,5},{8,10},{9,11},{10,... | collective-permute-start | bytes 1179656 | tf_op jit(solution)/shard_map/ppermute | solution.py:277
  8.3 8.7 %forward_0.1 = (f32[256,768]{1,0:T(8,128)S(1)}, f32[256,768]{1,0:T(8,128)S(1)}, bf16[256,768]{1,0:T(8,128)(2,1)S(1)}, bf16[256,768]{1,0:T(8,128)(2,1)S(1)}, bf16...) custom-call(s32[1]{0:T(128)} %bitcast.me_ref, bf16[1344,256]{1,0:T(8,128)(2,1)S(1)} %bitcast.7, ...), custom_call_target="tpu_custom_call" | custom-call | flops 1 | bytes 1 | tf_op jit(solution)/shard_map/forward_0/pallas_call | solution.py:315
  17.0 1.2 %collective-permute-done.1.refs_3_ = bf16[256,768]{1,0:T(8,128)(2,1)S(1)} collective-permute-done((bf16[256,768]{1,0:T(8,128)(2,1)S(1)}, bf16[256,768]{1,0:T(8,128)(2,1)S(1)}, u32[]{:S(2)}, u32[]{:S(2)}) %collective-permute-start.1) | collective-permute-done | bytes 393248 | tf_op jit(solution)/shard_map/ppermute | solution.py:277
  18.2 1.5 %collective-permute-start.2 = (bf16[256,768]{1,0:T(8,128)(2,1)S(1)}, bf16[256,768]{1,0:T(8,128)(2,1)S(1)}, u32[]{:S(2)}, u32[]{:S(2)}) collective-permute-start(bf16[256,768]{1,0:T(8,128)(2,1)S(1)} %collective-permute-done.refs_2_), channel_id=1, source_target_pairs={{0,2},{1,3},{2,0},{3,1},{4,6},{5,7},{6,4},{7,5},{8,10},{9,11},{10,... | collective-permute-start | bytes 1179656 | tf_op jit(solution)/shard_map/ppermute | solution.py:277
  19.7 0.9 %collective-permute-start.3 = (bf16[256,768]{1,0:T(8,128)(2,1)S(1)}, bf16[256,768]{1,0:T(8,128)(2,1)S(1)}, u32[]{:S(2)}, u32[]{:S(2)}) collective-permute-start(bf16[256,768]{1,0:T(8,128)(2,1)S(1)} %collective-permute-done.1.refs_3_), channel_id=1, source_target_pairs={{0,1},{1,0},{2,3},{3,2},{4,5},{5,4},{6,7},{7,6},{8,9},{9,8},{10,11... | collective-permute-start | bytes 1179656 | tf_op jit(solution)/shard_map/ppermute | solution.py:277
  21.3 2.3 %back_near_0.1.refs_3_ = f32[1344,256]{1,0:T(8,128)S(1)} custom-call(s32[1]{0:T(128)} %bitcast.me_ref, bf16[256,768]{1,0:T(8,128)(2,1)S(1)} %get-tuple-element.57.refs_0_, bf16[256,768]{1,0:T(8,128)(2,1)S(1)} %get-tuple-element.58.refs_1_, bf16[256,768]{1,0:T(8,128)(2,1)S(1)} %collective-permute-done.refs_2_, ...), custom_call_target="tpu_custom_call" | custom-call | flops 1 | bytes 1 | tf_op jit(solution)/shard_map/back_near_0/pallas_call | solution.py:358
  23.6 2.8 %forward_1.1 = (bf16[256,768]{1,0:T(8,128)(2,1)S(1)}, bf16[256,768]{1,0:T(8,128)(2,1)S(1)}, f32[256,768]{1,0:T(8,128)S(1)}, f32[256,768]{1,0:T(8,128)S(1)}, f32[...) custom-call(s32[1]{0:T(128)} %bitcast.me_ref, s32[1,256]{1,0:T(1,128)S(1)} %bitcast.14, ...), custom_call_target="tpu_custom_call" | custom-call | flops 1 | bytes 1 | tf_op jit(solution)/shard_map/forward_1/pallas_call | solution.py:339
  26.4 1.2 %collective-permute-start.9 = (bf16[256,768]{1,0:T(8,128)(2,1)S(1)}, bf16[256,768]{1,0:T(8,128)(2,1)S(1)}, u32[]{:S(2)}, u32[]{:S(2)}) collective-permute-start(bf16[256,768]{1,0:T(8,128)(2,1)S(1)} %get-tuple-element.72.refs_2_), channel_id=1, source_target_pairs={{0,1},{1,0},{2,3},{3,2},{4,5},{5,4},{6,7},{7,6},{8,9},{9,8},{10,11... | collective-permute-start | bytes 1179656 | tf_op jit(solution)/shard_map/ppermute | solution.py:277
  27.7 0.5 collective-permute-start.10
  28.6 1.3 %back_near_1.1.refs_3_ = f32[1344,256]{1,0:T(8,128)S(1)} custom-call(s32[1]{0:T(128)} %bitcast.me_ref, bf16[256,768]{1,0:T(8,128)(2,1)S(1)} %collective-permute-done.4.refs_0_, bf16[256,768]{1,0:T(8,128)(2,1)S(1)} %collective-permute-done.5.refs_1_, bf16[1344,6144]{1,0:T(8,128)(2,1)S(1)} %get-tuple-element.61.kept_ref.refs_4_.refs_2_, ...), custom_call_target="tpu_custom_call" | custom-call | flops 1 | bytes 1 | tf_op jit(solution)/shard_map/back_near_1/pallas_call | solution.py:358
  30.3 4.8 %collective-permute-done.2.refs_0_ = bf16[256,768]{1,0:T(8,128)(2,1)S(1)} collective-permute-done((bf16[256,768]{1,0:T(8,128)(2,1)S(1)}, bf16[256,768]{1,0:T(8,128)(2,1)S(1)}, u32[]{:S(2)}, u32[]{:S(2)}) %collective-permute-start.2) | collective-permute-done | bytes 393248 | tf_op jit(solution)/shard_map/ppermute | solution.py:277
  35.4 1.5 %collective-permute-start.8 = (f32[1,256]{1,0:T(1,128)S(1)}, f32[1,256]{1,0:T(1,128)S(1)}, u32[]{:S(2)}, u32[]{:S(2)}) collective-permute-start(f32[1,256]{1,0:T(1,128)S(1)} %dot_part.5.refs_0_), channel_id=1, source_target_pairs={{0,3},{1,2},{2,1},{3,0},{4,7},{5,6},{6,5},{7,4},{8,11},{9,10},{10,... | collective-permute-start | bytes 3080 | tf_op jit(solution)/shard_map/ppermute | solution.py:277
  37.0 1.9 %collective-permute-start.6 = (f32[1,256]{1,0:T(1,128)S(1)}, f32[1,256]{1,0:T(1,128)S(1)}, u32[]{:S(2)}, u32[]{:S(2)}) collective-permute-start(f32[1,256]{1,0:T(1,128)S(1)} %dot_part.5.refs_0_), channel_id=1, source_target_pairs={{0,1},{1,0},{2,3},{3,2},{4,5},{5,4},{6,7},{7,6},{8,9},{9,8},{10,11... | collective-permute-start | bytes 3080 | tf_op jit(solution)/shard_map/ppermute | solution.py:277
  38.9 2.7 %back_far.1 = (bf16[1344,256]{1,0:T(8,128)(2,1)}, bf16[1344,256]{1,0:T(8,128)(2,1)}) custom-call(s32[1]{0:T(128)} %bitcast.me_ref, f32[1,256]{1,0:T(1,128)S(1)} %get-tuple-element.81.prob_ref, bf16[1344,256]{1,0:T(8,128)(2,1)S(1)} %bitcast.8, bf16[1344,256]{1,0:T(8,128)(2,1)S(1)} %bitcast.10, bf16[256,768]{1,0:T(8,128)(2,1)S(1)} %collective-permute-done.2.refs_0_, ...), custom_call_target="tpu_custom_call" | custom-call | flops 1 | bytes 1 | tf_op jit(solution)/shard_map/back_far/pallas_call | solution.py:388
  41.6 0.7 %collective-permute-start.13 = (bf16[256,768]{1,0:T(8,128)(2,1)S(1)}, bf16[256,768]{1,0:T(8,128)(2,1)S(1)}, u32[]{:S(2)}, u32[]{:S(2)}) collective-permute-start(bf16[256,768]{1,0:T(8,128)(2,1)S(1)} %get-tuple-element.89.refs_6_), channel_id=1, source_target_pairs={{0,1},{1,0},{2,3},{3,2},{4,5},{5,4},{6,7},{7,6},{8,9},{9,8},{10,11... | collective-permute-start | bytes 1179656 | tf_op jit(solution)/shard_map/ppermute | solution.py:277
  42.3 1.5 %collective-permute-start.15 = (bf16[256,768]{1,0:T(8,128)(2,1)S(1)}, bf16[256,768]{1,0:T(8,128)(2,1)S(1)}, u32[]{:S(2)}, u32[]{:S(2)}) collective-permute-start(bf16[256,768]{1,0:T(8,128)(2,1)S(1)} %get-tuple-element.93.refs_7_), channel_id=1, source_target_pairs={{0,2},{1,3},{2,0},{3,1},{4,6},{5,7},{6,4},{7,5},{8,10},{9,11},{10,... | collective-permute-start | bytes 1179656 | tf_op jit(solution)/shard_map/ppermute | solution.py:277
  43.9 0.6 router_part.1
  44.6 1.2 %collective-permute-done.11 = f32[16,1536]{1,0:T(8,128)S(1)} collective-permute-done((f32[16,1536]{1,0:T(8,128)S(1)}, f32[16,1536]{1,0:T(8,128)S(1)}, u32[]{:S(2)}, u32[]{:S(2)}) %collective-permute-start.11) | collective-permute-done | bytes 98336 | tf_op jit(solution)/shard_map/ppermute | solution.py:277
  45.8 1.6 %collective-permute-start.12 = (bf16[16,1536]{1,0:T(8,128)(2,1)S(1)}, bf16[16,1536]{1,0:T(8,128)(2,1)S(1)}, u32[]{:S(2)}, u32[]{:S(2)}) collective-permute-start(bf16[16,1536]{1,0:T(8,128)(2,1)S(1)} %add_convert_fusion.3), channel_id=1, source_target_pairs={{0,8},{4,12},{8,0},{12,4},{16,24},{20,28},{24,16},{28,20},{1,9},{5... | collective-permute-start | bytes 147464 | tf_op jit(solution)/shard_map/ppermute | solution.py:277
  47.5 0.6 collective-permute-start.14
  48.1 1.4 %collective-permute-start.16 = (bf16[256,768]{1,0:T(8,128)(2,1)S(1)}, bf16[256,768]{1,0:T(8,128)(2,1)S(1)}, u32[]{:S(2)}, u32[]{:S(2)}) collective-permute-start(bf16[256,768]{1,0:T(8,128)(2,1)S(1)} %add_convert_fusion), channel_id=1, source_target_pairs={{0,1},{1,0},{2,3},{3,2},{4,5},{5,4},{6,7},{7,6},{8,9},{9,8},{10,11... | collective-permute-start | bytes 1179656 | tf_op jit(solution)/shard_map/ppermute | solution.py:277
  50.0 1.4 %collective-permute-done.13.refs_1_ = bf16[256,768]{1,0:T(8,128)(2,1)S(1)} collective-permute-done((bf16[256,768]{1,0:T(8,128)(2,1)S(1)}, bf16[256,768]{1,0:T(8,128)(2,1)S(1)}, u32[]{:S(2)}, u32[]{:S(2)}) %collective-permute-start.13) | collective-permute-done | bytes 393248 | tf_op jit(solution)/shard_map/ppermute | solution.py:277
  51.4 2.5 %collective-permute-start.17 = (bf16[16,1536]{1,0:T(8,128)(2,1)S(1)}, bf16[16,1536]{1,0:T(8,128)(2,1)S(1)}, u32[]{:S(2)}, u32[]{:S(2)}) collective-permute-start(bf16[16,1536]{1,0:T(8,128)(2,1)S(1)} %add_convert_fusion.2.refs_0_), channel_id=1, source_target_pairs={{0,16},{4,20},{8,24},{12,28},{16,0},{20,4},{24,8},{28,12},{1,17},{... | collective-permute-start | bytes 147464 | tf_op jit(solution)/shard_map/ppermute | solution.py:277
  53.8 0.5 place_0.1.placed_ref
  54.4 0.5 place_1.1.placed_ref
  54.9 4.4 %collective-permute-done.16.last_ref = bf16[256,768]{1,0:T(8,128)(2,1)S(1)} collective-permute-done((bf16[256,768]{1,0:T(8,128)(2,1)S(1)}, bf16[256,768]{1,0:T(8,128)(2,1)S(1)}, u32[]{:S(2)}, u32[]{:S(2)}) %collective-permute-start.16) | collective-permute-done | bytes 393248 | tf_op jit(solution)/shard_map/ppermute | solution.py:277
  59.3 1.2 %combine_1.1 = (bf16[384,1536]{1,0:T(8,128)(2,1)}, f32[16,1536]{1,0:T(8,128)}) custom-call(f32[384,768]{1,0:T(8,128)S(1)} %place_1.1.placed_ref, bf16[384,256]{1,0:T(8,128)(2,1)S(1)} %get-tuple-element.62.pick_ref, f32[384,1]{1,0:T(8,128)S(1)} %get-tuple-element.91.weight_ref, bf16[256,768]{1,0:T(8,128)(2,1)S(1)} %collective-permute-done.16.last_ref, ...), custom_call_target="tpu_custom_call" | custom-call | flops 1 | bytes 1 | tf_op jit(solution)/shard_map/combine_1/pallas_call | solution.py:451
  60.6 1.1 %combine_0.1 = bf16[384,1536]{1,0:T(8,128)(2,1)} custom-call(f32[384,768]{1,0:T(8,128)S(1)} %place_0.1.placed_ref, bf16[384,256]{1,0:T(8,128)(2,1)S(1)} %get-tuple-element.62.pick_ref, f32[384,1]{1,0:T(8,128)S(1)} %get-tuple-element.91.weight_ref, bf16[256,768]{1,0:T(8,128)(2,1)S(1)} %collective-permute-done.14.last_ref, ...), custom_call_target="tpu_custom_call", output_to_operand_aliasing={{}: (4, {})} | custom-call | flops 1 | bytes 1 | tf_op jit(solution)/shard_map/combine_0/pallas_call | solution.py:451
  (37 shorter events, 2.8 us)
Async XLA Ops:
  0.6 0.7 %copy-start.5 = (s32[256]{0:T(256)S(1)}, s32[256]{0:T(256)}, u32[]{:S(2)}) copy-start(s32[256]{0:T(256)} %param.11) | copy-start | bytes 3076
  1.3 1.3 %copy-start.3 = (bf16[384,1536]{1,0:T(8,128)(2,1)S(1)}, bf16[384,1536]{1,0:T(8,128)(2,1)}, u32[]{:S(2)}) copy-start(bf16[384,1536]{1,0:T(8,128)(2,1)} %grad_ref.1) | copy-start | bytes 3538948
  2.6 5.7 %copy-start = (bf16[256,1344]{0,1:T(8,128)(2,1)S(1)}, bf16[256,1344]{0,1:T(8,128)(2,1)}, u32[]{:S(2)}) copy-start(bf16[256,1344]{0,1:T(8,128)(2,1)} %param.8) | copy-start | bytes 2064388
  2.6 5.7 %copy-start.1 = (bf16[256,1344]{0,1:T(8,128)(2,1)S(1)}, bf16[256,1344]{0,1:T(8,128)(2,1)}, u32[]{:S(2)}) copy-start(bf16[256,1344]{0,1:T(8,128)(2,1)} %param.9) | copy-start | bytes 2064388
  3.2 13.9 %collective-permute-start = (bf16[256,768]{1,0:T(8,128)(2,1)S(1)}, bf16[256,768]{1,0:T(8,128)(2,1)S(1)}, u32[]{:S(2)}, u32[]{:S(2)}) collective-permute-start(bf16[256,768]{1,0:T(8,128)(2,1)S(1)} %get-tuple-element.57.refs_0_), channel_id=1, source_target_pairs={{0,1},{1,0},{2,3},{3,2},{4,5},{5,4},{6,7},{7,6},{8,9},{9,8},{10,11... | collective-permute-start | bytes 1179656 | tf_op jit(solution)/shard_map/ppermute | solution.py:277
  6.2 12.0 %collective-permute-start.1 = (bf16[256,768]{1,0:T(8,128)(2,1)S(1)}, bf16[256,768]{1,0:T(8,128)(2,1)S(1)}, u32[]{:S(2)}, u32[]{:S(2)}) collective-permute-start(bf16[256,768]{1,0:T(8,128)(2,1)S(1)} %get-tuple-element.58.refs_1_), channel_id=1, source_target_pairs={{0,2},{1,3},{2,0},{3,1},{4,6},{5,7},{6,4},{7,5},{8,10},{9,11},{10,... | collective-permute-start | bytes 1179656 | tf_op jit(solution)/shard_map/ppermute | solution.py:277
  7.7 20.0 %collective-permute-start.5 = (bf16[256,768]{1,0:T(8,128)(2,1)S(1)}, bf16[256,768]{1,0:T(8,128)(2,1)S(1)}, u32[]{:S(2)}, u32[]{:S(2)}) collective-permute-start(bf16[256,768]{1,0:T(8,128)(2,1)S(1)} %get-tuple-element.57.refs_0_), channel_id=1, source_target_pairs={{0,2},{1,3},{2,0},{3,1},{4,6},{5,7},{6,4},{7,5},{8,10},{9,11},{10,... | collective-permute-start | bytes 1179656 | tf_op jit(solution)/shard_map/ppermute | solution.py:277
  8.2 20.5 %collective-permute-start.4 = (bf16[256,768]{1,0:T(8,128)(2,1)S(1)}, bf16[256,768]{1,0:T(8,128)(2,1)S(1)}, u32[]{:S(2)}, u32[]{:S(2)}) collective-permute-start(bf16[256,768]{1,0:T(8,128)(2,1)S(1)} %get-tuple-element.58.refs_1_), channel_id=1, source_target_pairs={{0,1},{1,0},{2,3},{3,2},{4,5},{5,4},{6,7},{7,6},{8,9},{9,8},{10,11... | collective-permute-start | bytes 1179656 | tf_op jit(solution)/shard_map/ppermute | solution.py:277
  18.2 16.9 %collective-permute-start.2 = (bf16[256,768]{1,0:T(8,128)(2,1)S(1)}, bf16[256,768]{1,0:T(8,128)(2,1)S(1)}, u32[]{:S(2)}, u32[]{:S(2)}) collective-permute-start(bf16[256,768]{1,0:T(8,128)(2,1)S(1)} %collective-permute-done.refs_2_), channel_id=1, source_target_pairs={{0,2},{1,3},{2,0},{3,1},{4,6},{5,7},{6,4},{7,5},{8,10},{9,11},{10,... | collective-permute-start | bytes 1179656 | tf_op jit(solution)/shard_map/ppermute | solution.py:277
  19.7 15.3 %collective-permute-start.3 = (bf16[256,768]{1,0:T(8,128)(2,1)S(1)}, bf16[256,768]{1,0:T(8,128)(2,1)S(1)}, u32[]{:S(2)}, u32[]{:S(2)}) collective-permute-start(bf16[256,768]{1,0:T(8,128)(2,1)S(1)} %collective-permute-done.1.refs_3_), channel_id=1, source_target_pairs={{0,1},{1,0},{2,3},{3,2},{4,5},{5,4},{6,7},{7,6},{8,9},{9,8},{10,11... | collective-permute-start | bytes 1179656 | tf_op jit(solution)/shard_map/ppermute | solution.py:277
  21.2 2.4 %copy-start.4 = (f32[384,16]{0,1:T(8,128)S(1)}, f32[384,16]{0,1:T(8,128)}, u32[]{:S(2)}) copy-start(f32[384,16]{0,1:T(8,128)} %param.13) | copy-start | bytes 73732
  21.2 2.4 %copy-start.6 = (s32[256]{0:T(256)S(1)}, s32[256]{0:T(256)}, u32[]{:S(2)}) copy-start(s32[256]{0:T(256)} %param.11) | copy-start | bytes 3076
  26.4 15.2 %collective-permute-start.9 = (bf16[256,768]{1,0:T(8,128)(2,1)S(1)}, bf16[256,768]{1,0:T(8,128)(2,1)S(1)}, u32[]{:S(2)}, u32[]{:S(2)}) collective-permute-start(bf16[256,768]{1,0:T(8,128)(2,1)S(1)} %get-tuple-element.72.refs_2_), channel_id=1, source_target_pairs={{0,1},{1,0},{2,3},{3,2},{4,5},{5,4},{6,7},{7,6},{8,9},{9,8},{10,11... | collective-permute-start | bytes 1179656 | tf_op jit(solution)/shard_map/ppermute | solution.py:277
  27.7 14.7 %collective-permute-start.10 = (bf16[256,768]{1,0:T(8,128)(2,1)S(1)}, bf16[256,768]{1,0:T(8,128)(2,1)S(1)}, u32[]{:S(2)}, u32[]{:S(2)}) collective-permute-start(bf16[256,768]{1,0:T(8,128)(2,1)S(1)} %get-tuple-element.73.refs_3_), channel_id=1, source_target_pairs={{0,2},{1,3},{2,0},{3,1},{4,6},{5,7},{6,4},{7,5},{8,10},{9,11},{10,... | collective-permute-start | bytes 1179656 | tf_op jit(solution)/shard_map/ppermute | solution.py:277
  35.4 8.5 %collective-permute-start.8 = (f32[1,256]{1,0:T(1,128)S(1)}, f32[1,256]{1,0:T(1,128)S(1)}, u32[]{:S(2)}, u32[]{:S(2)}) collective-permute-start(f32[1,256]{1,0:T(1,128)S(1)} %dot_part.5.refs_0_), channel_id=1, source_target_pairs={{0,3},{1,2},{2,1},{3,0},{4,7},{5,6},{6,5},{7,4},{8,11},{9,10},{10,... | collective-permute-start | bytes 3080 | tf_op jit(solution)/shard_map/ppermute | solution.py:277
  36.9 6.9 %collective-permute-start.7 = (f32[1,256]{1,0:T(1,128)S(1)}, f32[1,256]{1,0:T(1,128)S(1)}, u32[]{:S(2)}, u32[]{:S(2)}) collective-permute-start(f32[1,256]{1,0:T(1,128)S(1)} %dot_part.5.refs_0_), channel_id=1, source_target_pairs={{0,2},{1,3},{2,0},{3,1},{4,6},{5,7},{6,4},{7,5},{8,10},{9,11},{10,... | collective-permute-start | bytes 3080 | tf_op jit(solution)/shard_map/ppermute | solution.py:277
  37.0 6.8 %collective-permute-start.6 = (f32[1,256]{1,0:T(1,128)S(1)}, f32[1,256]{1,0:T(1,128)S(1)}, u32[]{:S(2)}, u32[]{:S(2)}) collective-permute-start(f32[1,256]{1,0:T(1,128)S(1)} %dot_part.5.refs_0_), channel_id=1, source_target_pairs={{0,1},{1,0},{2,3},{3,2},{4,5},{5,4},{6,7},{7,6},{8,9},{9,8},{10,11... | collective-permute-start | bytes 3080 | tf_op jit(solution)/shard_map/ppermute | solution.py:277
  38.9 5.0 %copy-start.2 = (bf16[384,1536]{1,0:T(8,128)(2,1)S(1)}, bf16[384,1536]{1,0:T(8,128)(2,1)}, u32[]{:S(2)}) copy-start(bf16[384,1536]{1,0:T(8,128)(2,1)} %tokens_ref.1) | copy-start | bytes 3538948
  41.6 9.8 %collective-permute-start.13 = (bf16[256,768]{1,0:T(8,128)(2,1)S(1)}, bf16[256,768]{1,0:T(8,128)(2,1)S(1)}, u32[]{:S(2)}, u32[]{:S(2)}) collective-permute-start(bf16[256,768]{1,0:T(8,128)(2,1)S(1)} %get-tuple-element.89.refs_6_), channel_id=1, source_target_pairs={{0,1},{1,0},{2,3},{3,2},{4,5},{5,4},{6,7},{7,6},{8,9},{9,8},{10,11... | collective-permute-start | bytes 1179656 | tf_op jit(solution)/shard_map/ppermute | solution.py:277
  42.3 12.1 %collective-permute-start.15 = (bf16[256,768]{1,0:T(8,128)(2,1)S(1)}, bf16[256,768]{1,0:T(8,128)(2,1)S(1)}, u32[]{:S(2)}, u32[]{:S(2)}) collective-permute-start(bf16[256,768]{1,0:T(8,128)(2,1)S(1)} %get-tuple-element.93.refs_7_), channel_id=1, source_target_pairs={{0,2},{1,3},{2,0},{3,1},{4,6},{5,7},{6,4},{7,5},{8,10},{9,11},{10,... | collective-permute-start | bytes 1179656 | tf_op jit(solution)/shard_map/ppermute | solution.py:277
  44.5 1.3 %collective-permute-start.11 = (f32[16,1536]{1,0:T(8,128)S(1)}, f32[16,1536]{1,0:T(8,128)S(1)}, u32[]{:S(2)}, u32[]{:S(2)}) collective-permute-start(f32[16,1536]{1,0:T(8,128)S(1)} %router_part.1), channel_id=1, source_target_pairs={{0,4},{4,0},{8,12},{12,8},{16,20},{20,16},{24,28},{28,24},{1,5},{5... | collective-permute-start | bytes 294920 | tf_op jit(solution)/shard_map/ppermute | solution.py:277
  45.8 4.2 %collective-permute-start.12 = (bf16[16,1536]{1,0:T(8,128)(2,1)S(1)}, bf16[16,1536]{1,0:T(8,128)(2,1)S(1)}, u32[]{:S(2)}, u32[]{:S(2)}) collective-permute-start(bf16[16,1536]{1,0:T(8,128)(2,1)S(1)} %add_convert_fusion.3), channel_id=1, source_target_pairs={{0,8},{4,12},{8,0},{12,4},{16,24},{20,28},{24,16},{28,20},{1,9},{5... | collective-permute-start | bytes 147464 | tf_op jit(solution)/shard_map/ppermute | solution.py:277
  47.5 13.0 %collective-permute-start.14 = (bf16[256,768]{1,0:T(8,128)(2,1)S(1)}, bf16[256,768]{1,0:T(8,128)(2,1)S(1)}, u32[]{:S(2)}, u32[]{:S(2)}) collective-permute-start(bf16[256,768]{1,0:T(8,128)(2,1)S(1)} %add_convert_fusion.1), channel_id=1, source_target_pairs={{0,2},{1,3},{2,0},{3,1},{4,6},{5,7},{6,4},{7,5},{8,10},{9,11},{10,... | collective-permute-start | bytes 1179656 | tf_op jit(solution)/shard_map/ppermute | solution.py:277
  48.1 11.2 %collective-permute-start.16 = (bf16[256,768]{1,0:T(8,128)(2,1)S(1)}, bf16[256,768]{1,0:T(8,128)(2,1)S(1)}, u32[]{:S(2)}, u32[]{:S(2)}) collective-permute-start(bf16[256,768]{1,0:T(8,128)(2,1)S(1)} %add_convert_fusion), channel_id=1, source_target_pairs={{0,1},{1,0},{2,3},{3,2},{4,5},{5,4},{6,7},{7,6},{8,9},{9,8},{10,11... | collective-permute-start | bytes 1179656 | tf_op jit(solution)/shard_map/ppermute | solution.py:277
  51.4 7.9 %collective-permute-start.17 = (bf16[16,1536]{1,0:T(8,128)(2,1)S(1)}, bf16[16,1536]{1,0:T(8,128)(2,1)S(1)}, u32[]{:S(2)}, u32[]{:S(2)}) collective-permute-start(bf16[16,1536]{1,0:T(8,128)(2,1)S(1)} %add_convert_fusion.2.refs_0_), channel_id=1, source_target_pairs={{0,16},{4,20},{8,24},{12,28},{16,0},{20,4},{24,8},{28,12},{1,17},{... | collective-permute-start | bytes 147464 | tf_op jit(solution)/shard_map/ppermute | solution.py:277

commit v4 on v3

--- a/solution.py
+++ b/solution.py
@@ -211,8 +211,12 @@
     out_ref[...] = jnp.dot(logit_grad, tokens_ref[...], preferred_element_type=F32) * scale
 
 
-def place_kernel(pick_ref, *refs):
-    parts, placed_ref = refs[:-1], refs[-1]
+def place_kernel(has_router, pick_ref, *refs):
+    if has_router:
+        *parts, one, two, placed_ref, router_ref = refs
+        router_ref[...] = one[...].astype(F32) + two[...].astype(F32)
+    else:
+        *parts, placed_ref = refs
     pick = pick_ref[...]
     value = parts[0][...].astype(F32)
     for part in parts[1:]:
@@ -224,32 +228,28 @@
     )
 
 
-def combine_kernel(cut, has_router, placed_ref, pick_ref, weight_ref, last_ref, *refs):
-    if has_router:
-        *terms, out_ref, router_ref, made, sem, one, two, total, router_sem = refs[:2] + refs[-8:]
-        fetches = [
-            pltpu.make_async_copy(term, held, router_sem.at[at]) for at, (term, held) in enumerate(zip(terms, (one, two)))
-        ]
-        for fetch in fetches:
-            fetch.start()
-    else:
-        out_ref, made, sem = refs[-3:]
+def add_last_kernel(placed_ref, pick_ref, weight_ref, last_ref, out_ref):
+    last = jnp.dot(pick_ref[...], last_ref[...], preferred_element_type=F32)
+    out_ref[...] = (weight_ref[...] * (placed_ref[...] + last)).astype(BF16)
+
+
+def combine_kernel(n_done, placed_ref, pick_ref, weight_ref, last_ref, *refs):
+    done, (out_ref, made, sem) = refs[:n_done], refs[n_done:]
     rows, width = made.shape
     step = row_step(rows, 128)
-    puts = []
+    puts = [
+        pltpu.make_async_copy(ref, out_ref.at[:, pl.ds((1 + at) * width, width)], sem.at[at])
+        for at, ref in enumerate(done)
+    ]
+    for put in puts:
+        put.start()
     for j in range(rows // step):
         here = pl.ds(j * step, step)
         last = jnp.dot(pick_ref[here, :], last_ref[...], preferred_element_type=F32)
         made[here, :] = (weight_ref[here, :] * (placed_ref[here, :] + last)).astype(BF16)
         puts.append(
-            pltpu.make_async_copy(made.at[here, :], out_ref.at[here, pl.ds(cut * width, width)], sem.at[j])
+            pltpu.make_async_copy(made.at[here, :], out_ref.at[here, pl.ds(0, width)], sem.at[n_done + j])
         )
-        puts[-1].start()
-    if has_router:
-        for fetch in fetches:
-            fetch.wait()
-        total[...] = one[...].astype(F32) + two[...].astype(F32)
-        puts.append(pltpu.make_async_copy(total, router_ref, router_sem.at[2]))
         puts[-1].start()
     for put in puts:
         put.wait()
@@ -434,38 +434,46 @@
         halves = [sent, swap(sent, flip, "dp", n_dp)]
         flip *= 2
 
-    combined = None
+    done = []
     for cut in reversed(range(cuts)):
         *parts, last = groups[cut]
-        placed = pl.pallas_call(
-            place_kernel,
-            out_shape=jax.ShapeDtypeStruct((tok_count, width), F32),
-            in_specs=[vmem()] * (1 + len(parts)),
-            out_specs=vmem(),
+        sums = halves if cut == cuts - 1 else []
+        placed, *total = pl.pallas_call(
+            functools.partial(place_kernel, bool(sums)),
+            out_shape=[jax.ShapeDtypeStruct((tok_count, width), F32)]
+            + [jax.ShapeDtypeStruct((experts, feat), F32)] * (len(sums) // 2),
+            in_specs=[vmem()] * (1 + len(parts) + len(sums)),
+            out_specs=[vmem()] * (1 + len(sums) // 2),
             compiler_params=params(),
             cost_estimate=cost(1, 1),
             name="place_%d" % cut,
-        )(pick, *parts)
-        before = [] if combined is None else [combined]
-        sums = halves if cut == cuts - 1 else []
-        combined, *total = pl.pallas_call(
-            functools.partial(combine_kernel, cut, bool(sums)),
-            out_shape=[jax.ShapeDtypeStruct((tok_count, feat), BF16)]
-            + [jax.ShapeDtypeStruct((experts, feat), F32)] * (len(sums) // 2),
-            in_specs=[vmem()] * 4 + [pl.BlockSpec(memory_space=pl.ANY)] * len([*sums, *before]),
-            out_specs=[pl.BlockSpec(memory_space=pl.ANY)] * (1 + len(sums) // 2),
-            scratch_shapes=[
-                pltpu.VMEM((tok_count, width), BF16),
-                pltpu.SemaphoreType.DMA((tok_count // row_step(tok_count, 128),)),
-            ]
-            + [pltpu.VMEM((experts, feat), term.dtype) for term in sums]
-            + [pltpu.VMEM((experts, feat), F32), pltpu.SemaphoreType.DMA((3,))] * (len(sums) // 2),
-            input_output_aliases={4 + len(sums): 0} if before else {},
-            compiler_params=params(),
-            cost_estimate=cost(1, 1),
-            name="combine_%d" % cut,
-        )(placed, pick, weight, last, *sums, *before)
+        )(pick, *parts, *sums)
         router = total[0] if total else router
+        if cut > 0:
+            done.append(
+                pl.pallas_call(
+                    add_last_kernel,
+                    out_shape=jax.ShapeDtypeStruct((tok_count, width), BF16),
+                    in_specs=[vmem()] * 4,
+                    out_specs=vmem(),
+                    compiler_params=params(),
+                    cost_estimate=cost(1, 1),
+                    name="combine_%d" % cut,
+                )(placed, pick, weight, last)
+            )
+    combined = pl.pallas_call(
+        functools.partial(combine_kernel, len(done)),
+        out_shape=jax.ShapeDtypeStruct((tok_count, feat), BF16),
+        in_specs=[vmem()] * (4 + len(done)),
+        out_specs=pl.BlockSpec(memory_space=pl.ANY),
+        scratch_shapes=[
+            pltpu.VMEM((tok_count, width), BF16),
+            pltpu.SemaphoreType.DMA((len(done) + tok_count // row_step(tok_count, 128),)),
+        ],
+        compiler_params=params(),
+        cost_estimate=cost(1, 1),
+        name="combine_0",
+    )(placed, pick, weight, last, *done)
 
     return combined, dgate.T, dup.T, router
 

time: 62 us -> 61.9 us (level)
  transfers between devices with their start and end apart: 18 -> 18, of which waited for: 6 -> 8; matrix products, arithmetic and copies ran while one was open for 0% -> 0% of each run, Pallas kernels for 35% -> 35%
where the time goes in v4:
time: 61.9 us; the launch traced here: 61.7 us
  Pallas kernels  23.4 us (38%)
  starting transfers between devices  21 us (34%)
  waiting for transfers between devices  13.7 us (22%)
  local copies, waits for them, and re-layouts  1.71 us (3%)
  between operations  1.63 us (3%)
    ppermute x18, starting transfers between devices, swap(): return lax.ppermute(value, axis, [(i, i ^ flip) for i in range(size)])  21 us
    ppermute x18, waiting for transfers between devices, swap(): return lax.ppermute(value, axis, [(i, i ^ flip) for i in range(size)])  13.7 us
    pallas_call x1, Pallas kernels, body(): pl.pallas_call(functools.partial(first_forward_kernel, plans[0], cuts), o...  8.75 us
    pallas_call x2, Pallas kernels, body(): pl.pallas_call(functools.partial(back_kernel, [*pieces], cuts, bool(befor...  3.64 us
    pallas_call x1, Pallas kernels, body(): pl.pallas_call(functools.partial(next_forward_kernel, plans[1], cuts), ou...  2.82 us
    pallas_call x1, Pallas kernels, body(): pl.pallas_call(functools.partial(final_back_kernel, [*far], cuts), out_sh...  2.67 us
    unnamed x14, local copies, waits for them, and re-layouts  1.71 us
    pallas_call x2, Pallas kernels, body(): pl.pallas_call(functools.partial(place_kernel, bool(sums)), out_shape=[ja...  1.66 us
  transfers between devices with their start and end apart: 18, of which 8 were waited for; matrix products, arithmetic and copies ran while one was open for 0% of the time, Pallas kernels for 35%

profile of v4, /device:TPU:0, one launch (start us, length us, event | category | flops | bytes accessed | tf_op | source)
XLA Modules:
  0.0 61.7 jit_solution(12541689352360924019)
XLA Ops:
  0.6 0.7 %copy-done.5 = s32[256]{0:T(256)S(1)} copy-done((s32[256]{0:T(256)S(1)}, s32[256]{0:T(256)}, u32[]{:S(2)}) %copy-start.5) | copy-done | bytes 1048
  1.6 1.0 %copy-done.3 = bf16[384,1536]{1,0:T(8,128)(2,1)S(1)} copy-done((bf16[384,1536]{1,0:T(8,128)(2,1)S(1)}, bf16[384,1536]{1,0:T(8,128)(2,1)}, u32[]{:S(2)}) %copy-start.3) | copy-done | bytes 1179672
  2.6 0.6 gather_rows.1
  3.2 3.0 %collective-permute-start = (bf16[256,768]{1,0:T(8,128)(2,1)S(1)}, bf16[256,768]{1,0:T(8,128)(2,1)S(1)}, u32[]{:S(2)}, u32[]{:S(2)}) collective-permute-start(bf16[256,768]{1,0:T(8,128)(2,1)S(1)} %get-tuple-element.57.refs_0_), channel_id=1, source_target_pairs={{0,1},{1,0},{2,3},{3,2},{4,5},{5,4},{6,7},{7,6},{8,9},{9,8},{10,11... | collective-permute-start | bytes 1179656 | tf_op jit(solution)/shard_map/ppermute | solution.py:277
  6.2 1.5 %collective-permute-start.1 = (bf16[256,768]{1,0:T(8,128)(2,1)S(1)}, bf16[256,768]{1,0:T(8,128)(2,1)S(1)}, u32[]{:S(2)}, u32[]{:S(2)}) collective-permute-start(bf16[256,768]{1,0:T(8,128)(2,1)S(1)} %get-tuple-element.58.refs_1_), channel_id=1, source_target_pairs={{0,2},{1,3},{2,0},{3,1},{4,6},{5,7},{6,4},{7,5},{8,10},{9,11},{10,... | collective-permute-start | bytes 1179656 | tf_op jit(solution)/shard_map/ppermute | solution.py:277
  8.3 8.7 %forward_0.1 = (f32[256,768]{1,0:T(8,128)S(1)}, f32[256,768]{1,0:T(8,128)S(1)}, bf16[256,768]{1,0:T(8,128)(2,1)S(1)}, bf16[256,768]{1,0:T(8,128)(2,1)S(1)}, bf16...) custom-call(s32[1]{0:T(128)} %bitcast.me_ref, bf16[1344,256]{1,0:T(8,128)(2,1)S(1)} %bitcast.7, ...), custom_call_target="tpu_custom_call" | custom-call | flops 1 | bytes 1 | tf_op jit(solution)/shard_map/forward_0/pallas_call | solution.py:315
  17.0 1.2 %collective-permute-done.1.refs_3_ = bf16[256,768]{1,0:T(8,128)(2,1)S(1)} collective-permute-done((bf16[256,768]{1,0:T(8,128)(2,1)S(1)}, bf16[256,768]{1,0:T(8,128)(2,1)S(1)}, u32[]{:S(2)}, u32[]{:S(2)}) %collective-permute-start.1) | collective-permute-done | bytes 393248 | tf_op jit(solution)/shard_map/ppermute | solution.py:277
  18.2 1.5 %collective-permute-start.2 = (bf16[256,768]{1,0:T(8,128)(2,1)S(1)}, bf16[256,768]{1,0:T(8,128)(2,1)S(1)}, u32[]{:S(2)}, u32[]{:S(2)}) collective-permute-start(bf16[256,768]{1,0:T(8,128)(2,1)S(1)} %collective-permute-done.refs_2_), channel_id=1, source_target_pairs={{0,2},{1,3},{2,0},{3,1},{4,6},{5,7},{6,4},{7,5},{8,10},{9,11},{10,... | collective-permute-start | bytes 1179656 | tf_op jit(solution)/shard_map/ppermute | solution.py:277
  19.7 0.9 %collective-permute-start.3 = (bf16[256,768]{1,0:T(8,128)(2,1)S(1)}, bf16[256,768]{1,0:T(8,128)(2,1)S(1)}, u32[]{:S(2)}, u32[]{:S(2)}) collective-permute-start(bf16[256,768]{1,0:T(8,128)(2,1)S(1)} %collective-permute-done.1.refs_3_), channel_id=1, source_target_pairs={{0,1},{1,0},{2,3},{3,2},{4,5},{5,4},{6,7},{7,6},{8,9},{9,8},{10,11... | collective-permute-start | bytes 1179656 | tf_op jit(solution)/shard_map/ppermute | solution.py:277
  21.3 2.3 %back_near_0.1.refs_3_ = f32[1344,256]{1,0:T(8,128)S(1)} custom-call(s32[1]{0:T(128)} %bitcast.me_ref, bf16[256,768]{1,0:T(8,128)(2,1)S(1)} %get-tuple-element.57.refs_0_, bf16[256,768]{1,0:T(8,128)(2,1)S(1)} %get-tuple-element.58.refs_1_, bf16[256,768]{1,0:T(8,128)(2,1)S(1)} %collective-permute-done.refs_2_, ...), custom_call_target="tpu_custom_call" | custom-call | flops 1 | bytes 1 | tf_op jit(solution)/shard_map/back_near_0/pallas_call | solution.py:358
  23.6 2.8 %forward_1.1 = (bf16[256,768]{1,0:T(8,128)(2,1)S(1)}, bf16[256,768]{1,0:T(8,128)(2,1)S(1)}, f32[256,768]{1,0:T(8,128)S(1)}, f32[256,768]{1,0:T(8,128)S(1)}, f32[...) custom-call(s32[1]{0:T(128)} %bitcast.me_ref, s32[1,256]{1,0:T(1,128)S(1)} %bitcast.14, ...), custom_call_target="tpu_custom_call" | custom-call | flops 1 | bytes 1 | tf_op jit(solution)/shard_map/forward_1/pallas_call | solution.py:339
  26.4 1.2 %collective-permute-start.9 = (bf16[256,768]{1,0:T(8,128)(2,1)S(1)}, bf16[256,768]{1,0:T(8,128)(2,1)S(1)}, u32[]{:S(2)}, u32[]{:S(2)}) collective-permute-start(bf16[256,768]{1,0:T(8,128)(2,1)S(1)} %get-tuple-element.72.refs_2_), channel_id=1, source_target_pairs={{0,1},{1,0},{2,3},{3,2},{4,5},{5,4},{6,7},{7,6},{8,9},{9,8},{10,11... | collective-permute-start | bytes 1179656 | tf_op jit(solution)/shard_map/ppermute | solution.py:277
  28.6 1.3 %back_near_1.1.refs_3_ = f32[1344,256]{1,0:T(8,128)S(1)} custom-call(s32[1]{0:T(128)} %bitcast.me_ref, bf16[256,768]{1,0:T(8,128)(2,1)S(1)} %collective-permute-done.4.refs_0_, bf16[256,768]{1,0:T(8,128)(2,1)S(1)} %collective-permute-done.5.refs_1_, bf16[1344,6144]{1,0:T(8,128)(2,1)S(1)} %get-tuple-element.61.kept_ref.refs_4_.refs_2_, ...), custom_call_target="tpu_custom_call" | custom-call | flops 1 | bytes 1 | tf_op jit(solution)/shard_map/back_near_1/pallas_call | solution.py:358
  30.2 4.8 %collective-permute-done.2.refs_0_ = bf16[256,768]{1,0:T(8,128)(2,1)S(1)} collective-permute-done((bf16[256,768]{1,0:T(8,128)(2,1)S(1)}, bf16[256,768]{1,0:T(8,128)(2,1)S(1)}, u32[]{:S(2)}, u32[]{:S(2)}) %collective-permute-start.2) | collective-permute-done | bytes 393248 | tf_op jit(solution)/shard_map/ppermute | solution.py:277
  35.4 1.5 %collective-permute-start.8 = (f32[1,256]{1,0:T(1,128)S(1)}, f32[1,256]{1,0:T(1,128)S(1)}, u32[]{:S(2)}, u32[]{:S(2)}) collective-permute-start(f32[1,256]{1,0:T(1,128)S(1)} %dot_part.5.refs_0_), channel_id=1, source_target_pairs={{0,3},{1,2},{2,1},{3,0},{4,7},{5,6},{6,5},{7,4},{8,11},{9,10},{10,... | collective-permute-start | bytes 3080 | tf_op jit(solution)/shard_map/ppermute | solution.py:277
  37.0 1.9 %collective-permute-start.6 = (f32[1,256]{1,0:T(1,128)S(1)}, f32[1,256]{1,0:T(1,128)S(1)}, u32[]{:S(2)}, u32[]{:S(2)}) collective-permute-start(f32[1,256]{1,0:T(1,128)S(1)} %dot_part.5.refs_0_), channel_id=1, source_target_pairs={{0,1},{1,0},{2,3},{3,2},{4,5},{5,4},{6,7},{7,6},{8,9},{9,8},{10,11... | collective-permute-start | bytes 3080 | tf_op jit(solution)/shard_map/ppermute | solution.py:277
  38.9 2.7 %back_far.1 = (bf16[1344,256]{1,0:T(8,128)(2,1)}, bf16[1344,256]{1,0:T(8,128)(2,1)}) custom-call(s32[1]{0:T(128)} %bitcast.me_ref, f32[1,256]{1,0:T(1,128)S(1)} %get-tuple-element.81.prob_ref, bf16[1344,256]{1,0:T(8,128)(2,1)S(1)} %bitcast.8, bf16[1344,256]{1,0:T(8,128)(2,1)S(1)} %bitcast.10, bf16[256,768]{1,0:T(8,128)(2,1)S(1)} %collective-permute-done.2.refs_0_, ...), custom_call_target="tpu_custom_call" | custom-call | flops 1 | bytes 1 | tf_op jit(solution)/shard_map/back_far/pallas_call | solution.py:388
  41.6 0.7 %collective-permute-start.13 = (bf16[256,768]{1,0:T(8,128)(2,1)S(1)}, bf16[256,768]{1,0:T(8,128)(2,1)S(1)}, u32[]{:S(2)}, u32[]{:S(2)}) collective-permute-start(bf16[256,768]{1,0:T(8,128)(2,1)S(1)} %get-tuple-element.89.refs_6_), channel_id=1, source_target_pairs={{0,1},{1,0},{2,3},{3,2},{4,5},{5,4},{6,7},{7,6},{8,9},{9,8},{10,11... | collective-permute-start | bytes 1179656 | tf_op jit(solution)/shard_map/ppermute | solution.py:277
  42.3 1.5 %collective-permute-start.15 = (bf16[256,768]{1,0:T(8,128)(2,1)S(1)}, bf16[256,768]{1,0:T(8,128)(2,1)S(1)}, u32[]{:S(2)}, u32[]{:S(2)}) collective-permute-start(bf16[256,768]{1,0:T(8,128)(2,1)S(1)} %get-tuple-element.93.refs_7_), channel_id=1, source_target_pairs={{0,2},{1,3},{2,0},{3,1},{4,6},{5,7},{6,4},{7,5},{8,10},{9,11},{10,... | collective-permute-start | bytes 1179656 | tf_op jit(solution)/shard_map/ppermute | solution.py:277
  43.9 0.6 router_part.1
  44.6 1.2 %collective-permute-done.11 = f32[16,1536]{1,0:T(8,128)S(1)} collective-permute-done((f32[16,1536]{1,0:T(8,128)S(1)}, f32[16,1536]{1,0:T(8,128)S(1)}, u32[]{:S(2)}, u32[]{:S(2)}) %collective-permute-start.11) | collective-permute-done | bytes 98336 | tf_op jit(solution)/shard_map/ppermute | solution.py:277
  45.8 1.6 %collective-permute-start.12 = (bf16[16,1536]{1,0:T(8,128)(2,1)S(1)}, bf16[16,1536]{1,0:T(8,128)(2,1)S(1)}, u32[]{:S(2)}, u32[]{:S(2)}) collective-permute-start(bf16[16,1536]{1,0:T(8,128)(2,1)S(1)} %add_convert_fusion.3), channel_id=1, source_target_pairs={{0,8},{4,12},{8,0},{12,4},{16,24},{20,28},{24,16},{28,20},{1,9},{5... | collective-permute-start | bytes 147464 | tf_op jit(solution)/shard_map/ppermute | solution.py:277
  47.5 0.6 collective-permute-start.14
  48.1 1.4 %collective-permute-start.17 = (bf16[256,768]{1,0:T(8,128)(2,1)S(1)}, bf16[256,768]{1,0:T(8,128)(2,1)S(1)}, u32[]{:S(2)}, u32[]{:S(2)}) collective-permute-start(bf16[256,768]{1,0:T(8,128)(2,1)S(1)} %add_convert_fusion), channel_id=1, source_target_pairs={{0,1},{1,0},{2,3},{3,2},{4,5},{5,4},{6,7},{7,6},{8,9},{9,8},{10,11... | collective-permute-start | bytes 1179656 | tf_op jit(solution)/shard_map/ppermute | solution.py:277
  50.0 1.4 %collective-permute-done.13.refs_1_ = bf16[256,768]{1,0:T(8,128)(2,1)S(1)} collective-permute-done((bf16[256,768]{1,0:T(8,128)(2,1)S(1)}, bf16[256,768]{1,0:T(8,128)(2,1)S(1)}, u32[]{:S(2)}, u32[]{:S(2)}) %collective-permute-start.13) | collective-permute-done | bytes 393248 | tf_op jit(solution)/shard_map/ppermute | solution.py:277
  51.4 2.5 %collective-permute-start.16 = (bf16[16,1536]{1,0:T(8,128)(2,1)S(1)}, bf16[16,1536]{1,0:T(8,128)(2,1)S(1)}, u32[]{:S(2)}, u32[]{:S(2)}) collective-permute-start(bf16[16,1536]{1,0:T(8,128)(2,1)S(1)} %add_convert_fusion.2.refs_2_), channel_id=1, source_target_pairs={{0,16},{4,20},{8,24},{12,28},{16,0},{20,4},{24,8},{28,12},{1,17},{... | collective-permute-start | bytes 147464 | tf_op jit(solution)/shard_map/ppermute | solution.py:277
  53.8 0.5 place_0.1.placed_ref
  54.4 2.0 %collective-permute-done.16.refs_3_ = bf16[16,1536]{1,0:T(8,128)(2,1)S(1)} collective-permute-done((bf16[16,1536]{1,0:T(8,128)(2,1)S(1)}, bf16[16,1536]{1,0:T(8,128)(2,1)S(1)}, u32[]{:S(2)}, u32[]{:S(2)}) %collective-permute-start.16) | collective-permute-done | bytes 49184 | tf_op jit(solution)/shard_map/ppermute | solution.py:277
  56.4 1.1 %place_1.1 = (f32[384,768]{1,0:T(8,128)S(1)}, f32[16,1536]{1,0:T(8,128)}) custom-call(bf16[384,256]{1,0:T(8,128)(2,1)S(1)} %get-tuple-element.62.pick_ref, f32[256,768]{1,0:T(8,128)S(1)} %get-tuple-element.78.refs_5_.refs_0_, bf16[256,768]{1,0:T(8,128)(2,1)S(1)} %collective-permute-done.15.refs_1_, bf16[16,1536]{1,0:T(8,128)(2,1)S(1)} %add_convert_fusion.2.refs_2_, ...), custom_call_target="tpu_custom_call" | custom-call | flops 1 | bytes 1 | tf_op jit(solution)/shard_map/place_1/pallas_call | solution.py:441
  57.5 1.8 %collective-permute-done.17.last_ref = bf16[256,768]{1,0:T(8,128)(2,1)S(1)} collective-permute-done((bf16[256,768]{1,0:T(8,128)(2,1)S(1)}, bf16[256,768]{1,0:T(8,128)(2,1)S(1)}, u32[]{:S(2)}, u32[]{:S(2)}) %collective-permute-start.17) | collective-permute-done | bytes 393248 | tf_op jit(solution)/shard_map/ppermute | solution.py:277
  59.6 0.8 %collective-permute-done.14.last_ref = bf16[256,768]{1,0:T(8,128)(2,1)S(1)} collective-permute-done((bf16[256,768]{1,0:T(8,128)(2,1)S(1)}, bf16[256,768]{1,0:T(8,128)(2,1)S(1)}, u32[]{:S(2)}, u32[]{:S(2)}) %collective-permute-start.14) | collective-permute-done | bytes 393248 | tf_op jit(solution)/shard_map/ppermute | solution.py:277
  60.4 1.1 %combine_0.1 = bf16[384,1536]{1,0:T(8,128)(2,1)} custom-call(f32[384,768]{1,0:T(8,128)S(1)} %place_0.1.placed_ref, bf16[384,256]{1,0:T(8,128)(2,1)S(1)} %get-tuple-element.62.pick_ref, f32[384,1]{1,0:T(8,128)S(1)} %get-tuple-element.91.weight_ref, bf16[256,768]{1,0:T(8,128)(2,1)S(1)} %collective-permute-done.14.last_ref, bf16[384,768]{1,0:T(8,128)(2,1)S(1)} %combine_1.1.refs_0_), custom_call_target="tpu_custom_call" | custom-call | flops 1 | bytes 1 | tf_op jit(solution)/shard_map/combine_0/pallas_call | solution.py:464
  (37 shorter events, 3.6 us)
Async XLA Ops:
  0.6 0.7 %copy-start.5 = (s32[256]{0:T(256)S(1)}, s32[256]{0:T(256)}, u32[]{:S(2)}) copy-start(s32[256]{0:T(256)} %param.11) | copy-start | bytes 3076
  1.3 1.3 %copy-start.3 = (bf16[384,1536]{1,0:T(8,128)(2,1)S(1)}, bf16[384,1536]{1,0:T(8,128)(2,1)}, u32[]{:S(2)}) copy-start(bf16[384,1536]{1,0:T(8,128)(2,1)} %grad_ref.1) | copy-start | bytes 3538948
  2.6 5.7 %copy-start = (bf16[256,1344]{0,1:T(8,128)(2,1)S(1)}, bf16[256,1344]{0,1:T(8,128)(2,1)}, u32[]{:S(2)}) copy-start(bf16[256,1344]{0,1:T(8,128)(2,1)} %param.8) | copy-start | bytes 2064388
  2.6 5.7 %copy-start.1 = (bf16[256,1344]{0,1:T(8,128)(2,1)S(1)}, bf16[256,1344]{0,1:T(8,128)(2,1)}, u32[]{:S(2)}) copy-start(bf16[256,1344]{0,1:T(8,128)(2,1)} %param.9) | copy-start | bytes 2064388
  3.2 13.9 %collective-permute-start = (bf16[256,768]{1,0:T(8,128)(2,1)S(1)}, bf16[256,768]{1,0:T(8,128)(2,1)S(1)}, u32[]{:S(2)}, u32[]{:S(2)}) collective-permute-start(bf16[256,768]{1,0:T(8,128)(2,1)S(1)} %get-tuple-element.57.refs_0_), channel_id=1, source_target_pairs={{0,1},{1,0},{2,3},{3,2},{4,5},{5,4},{6,7},{7,6},{8,9},{9,8},{10,11... | collective-permute-start | bytes 1179656 | tf_op jit(solution)/shard_map/ppermute | solution.py:277
  6.2 12.0 %collective-permute-start.1 = (bf16[256,768]{1,0:T(8,128)(2,1)S(1)}, bf16[256,768]{1,0:T(8,128)(2,1)S(1)}, u32[]{:S(2)}, u32[]{:S(2)}) collective-permute-start(bf16[256,768]{1,0:T(8,128)(2,1)S(1)} %get-tuple-element.58.refs_1_), channel_id=1, source_target_pairs={{0,2},{1,3},{2,0},{3,1},{4,6},{5,7},{6,4},{7,5},{8,10},{9,11},{10,... | collective-permute-start | bytes 1179656 | tf_op jit(solution)/shard_map/ppermute | solution.py:277
  7.7 20.0 %collective-permute-start.5 = (bf16[256,768]{1,0:T(8,128)(2,1)S(1)}, bf16[256,768]{1,0:T(8,128)(2,1)S(1)}, u32[]{:S(2)}, u32[]{:S(2)}) collective-permute-start(bf16[256,768]{1,0:T(8,128)(2,1)S(1)} %get-tuple-element.57.refs_0_), channel_id=1, source_target_pairs={{0,2},{1,3},{2,0},{3,1},{4,6},{5,7},{6,4},{7,5},{8,10},{9,11},{10,... | collective-permute-start | bytes 1179656 | tf_op jit(solution)/shard_map/ppermute | solution.py:277
  8.2 20.5 %collective-permute-start.4 = (bf16[256,768]{1,0:T(8,128)(2,1)S(1)}, bf16[256,768]{1,0:T(8,128)(2,1)S(1)}, u32[]{:S(2)}, u32[]{:S(2)}) collective-permute-start(bf16[256,768]{1,0:T(8,128)(2,1)S(1)} %get-tuple-element.58.refs_1_), channel_id=1, source_target_pairs={{0,1},{1,0},{2,3},{3,2},{4,5},{5,4},{6,7},{7,6},{8,9},{9,8},{10,11... | collective-permute-start | bytes 1179656 | tf_op jit(solution)/shard_map/ppermute | solution.py:277
  18.2 16.9 %collective-permute-start.2 = (bf16[256,768]{1,0:T(8,128)(2,1)S(1)}, bf16[256,768]{1,0:T(8,128)(2,1)S(1)}, u32[]{:S(2)}, u32[]{:S(2)}) collective-permute-start(bf16[256,768]{1,0:T(8,128)(2,1)S(1)} %collective-permute-done.refs_2_), channel_id=1, source_target_pairs={{0,2},{1,3},{2,0},{3,1},{4,6},{5,7},{6,4},{7,5},{8,10},{9,11},{10,... | collective-permute-start | bytes 1179656 | tf_op jit(solution)/shard_map/ppermute | solution.py:277
  19.7 15.3 %collective-permute-start.3 = (bf16[256,768]{1,0:T(8,128)(2,1)S(1)}, bf16[256,768]{1,0:T(8,128)(2,1)S(1)}, u32[]{:S(2)}, u32[]{:S(2)}) collective-permute-start(bf16[256,768]{1,0:T(8,128)(2,1)S(1)} %collective-permute-done.1.refs_3_), channel_id=1, source_target_pairs={{0,1},{1,0},{2,3},{3,2},{4,5},{5,4},{6,7},{7,6},{8,9},{9,8},{10,11... | collective-permute-start | bytes 1179656 | tf_op jit(solution)/shard_map/ppermute | solution.py:277
  21.2 2.4 %copy-start.4 = (f32[384,16]{0,1:T(8,128)S(1)}, f32[384,16]{0,1:T(8,128)}, u32[]{:S(2)}) copy-start(f32[384,16]{0,1:T(8,128)} %param.13) | copy-start | bytes 73732
  21.2 2.4 %copy-start.6 = (s32[256]{0:T(256)S(1)}, s32[256]{0:T(256)}, u32[]{:S(2)}) copy-start(s32[256]{0:T(256)} %param.11) | copy-start | bytes 3076
  26.4 15.2 %collective-permute-start.9 = (bf16[256,768]{1,0:T(8,128)(2,1)S(1)}, bf16[256,768]{1,0:T(8,128)(2,1)S(1)}, u32[]{:S(2)}, u32[]{:S(2)}) collective-permute-start(bf16[256,768]{1,0:T(8,128)(2,1)S(1)} %get-tuple-element.72.refs_2_), channel_id=1, source_target_pairs={{0,1},{1,0},{2,3},{3,2},{4,5},{5,4},{6,7},{7,6},{8,9},{9,8},{10,11... | collective-permute-start | bytes 1179656 | tf_op jit(solution)/shard_map/ppermute | solution.py:277
  27.7 14.7 %collective-permute-start.10 = (bf16[256,768]{1,0:T(8,128)(2,1)S(1)}, bf16[256,768]{1,0:T(8,128)(2,1)S(1)}, u32[]{:S(2)}, u32[]{:S(2)}) collective-permute-start(bf16[256,768]{1,0:T(8,128)(2,1)S(1)} %get-tuple-element.73.refs_3_), channel_id=1, source_target_pairs={{0,2},{1,3},{2,0},{3,1},{4,6},{5,7},{6,4},{7,5},{8,10},{9,11},{10,... | collective-permute-start | bytes 1179656 | tf_op jit(solution)/shard_map/ppermute | solution.py:277
  35.4 8.5 %collective-permute-start.8 = (f32[1,256]{1,0:T(1,128)S(1)}, f32[1,256]{1,0:T(1,128)S(1)}, u32[]{:S(2)}, u32[]{:S(2)}) collective-permute-start(f32[1,256]{1,0:T(1,128)S(1)} %dot_part.5.refs_0_), channel_id=1, source_target_pairs={{0,3},{1,2},{2,1},{3,0},{4,7},{5,6},{6,5},{7,4},{8,11},{9,10},{10,... | collective-permute-start | bytes 3080 | tf_op jit(solution)/shard_map/ppermute | solution.py:277
  36.9 6.9 %collective-permute-start.7 = (f32[1,256]{1,0:T(1,128)S(1)}, f32[1,256]{1,0:T(1,128)S(1)}, u32[]{:S(2)}, u32[]{:S(2)}) collective-permute-start(f32[1,256]{1,0:T(1,128)S(1)} %dot_part.5.refs_0_), channel_id=1, source_target_pairs={{0,2},{1,3},{2,0},{3,1},{4,6},{5,7},{6,4},{7,5},{8,10},{9,11},{10,... | collective-permute-start | bytes 3080 | tf_op jit(solution)/shard_map/ppermute | solution.py:277
  37.0 6.8 %collective-permute-start.6 = (f32[1,256]{1,0:T(1,128)S(1)}, f32[1,256]{1,0:T(1,128)S(1)}, u32[]{:S(2)}, u32[]{:S(2)}) collective-permute-start(f32[1,256]{1,0:T(1,128)S(1)} %dot_part.5.refs_0_), channel_id=1, source_target_pairs={{0,1},{1,0},{2,3},{3,2},{4,5},{5,4},{6,7},{7,6},{8,9},{9,8},{10,11... | collective-permute-start | bytes 3080 | tf_op jit(solution)/shard_map/ppermute | solution.py:277
  38.9 5.0 %copy-start.2 = (bf16[384,1536]{1,0:T(8,128)(2,1)S(1)}, bf16[384,1536]{1,0:T(8,128)(2,1)}, u32[]{:S(2)}) copy-start(bf16[384,1536]{1,0:T(8,128)(2,1)} %tokens_ref.1) | copy-start | bytes 3538948
  41.6 9.8 %collective-permute-start.13 = (bf16[256,768]{1,0:T(8,128)(2,1)S(1)}, bf16[256,768]{1,0:T(8,128)(2,1)S(1)}, u32[]{:S(2)}, u32[]{:S(2)}) collective-permute-start(bf16[256,768]{1,0:T(8,128)(2,1)S(1)} %get-tuple-element.89.refs_6_), channel_id=1, source_target_pairs={{0,1},{1,0},{2,3},{3,2},{4,5},{5,4},{6,7},{7,6},{8,9},{9,8},{10,11... | collective-permute-start | bytes 1179656 | tf_op jit(solution)/shard_map/ppermute | solution.py:277
  42.3 12.0 %collective-permute-start.15 = (bf16[256,768]{1,0:T(8,128)(2,1)S(1)}, bf16[256,768]{1,0:T(8,128)(2,1)S(1)}, u32[]{:S(2)}, u32[]{:S(2)}) collective-permute-start(bf16[256,768]{1,0:T(8,128)(2,1)S(1)} %get-tuple-element.93.refs_7_), channel_id=1, source_target_pairs={{0,2},{1,3},{2,0},{3,1},{4,6},{5,7},{6,4},{7,5},{8,10},{9,11},{10,... | collective-permute-start | bytes 1179656 | tf_op jit(solution)/shard_map/ppermute | solution.py:277
  44.5 1.3 %collective-permute-start.11 = (f32[16,1536]{1,0:T(8,128)S(1)}, f32[16,1536]{1,0:T(8,128)S(1)}, u32[]{:S(2)}, u32[]{:S(2)}) collective-permute-start(f32[16,1536]{1,0:T(8,128)S(1)} %router_part.1), channel_id=1, source_target_pairs={{0,4},{4,0},{8,12},{12,8},{16,20},{20,16},{24,28},{28,24},{1,5},{5... | collective-permute-start | bytes 294920 | tf_op jit(solution)/shard_map/ppermute | solution.py:277
  45.8 4.2 %collective-permute-start.12 = (bf16[16,1536]{1,0:T(8,128)(2,1)S(1)}, bf16[16,1536]{1,0:T(8,128)(2,1)S(1)}, u32[]{:S(2)}, u32[]{:S(2)}) collective-permute-start(bf16[16,1536]{1,0:T(8,128)(2,1)S(1)} %add_convert_fusion.3), channel_id=1, source_target_pairs={{0,8},{4,12},{8,0},{12,4},{16,24},{20,28},{24,16},{28,20},{1,9},{5... | collective-permute-start | bytes 147464 | tf_op jit(solution)/shard_map/ppermute | solution.py:277
  47.5 12.9 %collective-permute-start.14 = (bf16[256,768]{1,0:T(8,128)(2,1)S(1)}, bf16[256,768]{1,0:T(8,128)(2,1)S(1)}, u32[]{:S(2)}, u32[]{:S(2)}) collective-permute-start(bf16[256,768]{1,0:T(8,128)(2,1)S(1)} %add_convert_fusion.1), channel_id=1, source_target_pairs={{0,2},{1,3},{2,0},{3,1},{4,6},{5,7},{6,4},{7,5},{8,10},{9,11},{10,... | collective-permute-start | bytes 1179656 | tf_op jit(solution)/shard_map/ppermute | solution.py:277
  48.1 11.2 %collective-permute-start.17 = (bf16[256,768]{1,0:T(8,128)(2,1)S(1)}, bf16[256,768]{1,0:T(8,128)(2,1)S(1)}, u32[]{:S(2)}, u32[]{:S(2)}) collective-permute-start(bf16[256,768]{1,0:T(8,128)(2,1)S(1)} %add_convert_fusion), channel_id=1, source_target_pairs={{0,1},{1,0},{2,3},{3,2},{4,5},{5,4},{6,7},{7,6},{8,9},{9,8},{10,11... | collective-permute-start | bytes 1179656 | tf_op jit(solution)/shard_map/ppermute | solution.py:277
  51.4 5.0 %collective-permute-start.16 = (bf16[16,1536]{1,0:T(8,128)(2,1)S(1)}, bf16[16,1536]{1,0:T(8,128)(2,1)S(1)}, u32[]{:S(2)}, u32[]{:S(2)}) collective-permute-start(bf16[16,1536]{1,0:T(8,128)(2,1)S(1)} %add_convert_fusion.2.refs_2_), channel_id=1, source_target_pairs={{0,16},{4,20},{8,24},{12,28},{16,0},{20,4},{24,8},{28,12},{1,17},{... | collective-permute-start | bytes 147464 | tf_op jit(solution)/shard_map/ppermute | solution.py:277

commit v5 on v4

--- a/solution.py
+++ b/solution.py
@@ -64,11 +64,14 @@
     return total[0:1, :]
 
 
-def mask_kernel(row_ref, mask_ref):
+def token_kernel(ids_ref):
+    ids_ref[...] = lax.broadcasted_iota(jnp.int32, ids_ref.shape, 1)
+
+
+def mask_kernel(ids_ref, row_ref, mask_ref):
     rows = row_ref[...]
     column = jnp.broadcast_to(rows, (8, rows.shape[1])).T[:, 0:1]
-    tokens = lax.broadcasted_iota(jnp.int32, mask_ref.shape, 1)
-    mask_ref[...] = (tokens == column).astype(F32).astype(BF16)
+    mask_ref[...] = (ids_ref[0:1, :] == column).astype(F32).astype(BF16)
 
 
 def gather_kernel(mask_ref, grad_ref, *outs):
@@ -279,15 +282,23 @@
     rows = row_token.reshape(1, slots)
     gate_t, up_t, logits_t = pre_gate.T, pre_up.T, router_logits.T
 
+    ids = pl.pallas_call(
+        token_kernel,
+        out_shape=jax.ShapeDtypeStruct((8, tok_count), jnp.int32),
+        out_specs=vmem(),
+        compiler_params=params(),
+        cost_estimate=cost(10**10, 1),
+        name="token_ids",
+    )()
     places = pl.pallas_call(
         mask_kernel,
         out_shape=jax.ShapeDtypeStruct((slots, tok_count), BF16),
-        in_specs=[vmem()],
+        in_specs=[vmem()] * 2,
         out_specs=vmem(),
         compiler_params=params(),
-        cost_estimate=cost(10**10, 1),
+        cost_estimate=cost(1, 1),
         name="token_mask",
-    )(rows)
+    )(ids, rows)
     own = pl.pallas_call(
         gather_kernel,
         out_shape=[jax.ShapeDtypeStruct((slots, width), BF16)] * cuts,
@@ -406,6 +417,7 @@
     if square:
         via_x, via_y = swap(part[3, 0], 1), swap(part[3, 1], 2)
         out_x, out_y, dgate = lax.optimization_barrier((part[1, 0], part[2, 1], dgate))
+        out_x, via_y = lax.optimization_barrier((out_x, via_y))
         *dots, via_x, via_y, dgate = lax.optimization_barrier((*dots, via_x, via_y, dgate))
         direct_x, direct_y = swap(out_x, 1), swap(out_y, 2)
         sum_y = (part[2, 0] + via_x.astype(F32)).astype(BF16)

time: 61.9 us -> 62.6 us (1.011)
  local copies, waits for them, and re-layouts: 1.71 us -> 3.21 us
  waiting for transfers between devices: 13.7 us -> 12.6 us
    unnamed x14 -> x16, local copies, waits for them, and re-layouts: 1.71 us -> 3.21 us
    ppermute x18, waiting for transfers between devices: 13.7 us -> 12.6 us  [swap(): return lax.ppermute(value, axis, [(i, i ^ flip) for i in range(size)])]
  transfers between devices with their start and end apart: 18 -> 18, of which waited for: 8 -> 6; matrix products, arithmetic and copies ran while one was open for 0% -> 0% of each run, Pallas kernels for 35% -> 35%
where the time goes in v5:
time: 62.6 us; the launch traced here: 62.3 us
  Pallas kernels  23.4 us (37%)
  starting transfers between devices  21.2 us (34%)
  waiting for transfers between devices  12.6 us (20%)
  local copies, waits for them, and re-layouts  3.21 us (5%)
  between operations  1.64 us (3%)
    ppermute x18, starting transfers between devices, swap(): return lax.ppermute(value, axis, [(i, i ^ flip) for i in range(size)])  21.2 us
    ppermute x18, waiting for transfers between devices, swap(): return lax.ppermute(value, axis, [(i, i ^ flip) for i in range(size)])  12.6 us
    pallas_call x1, Pallas kernels, body(): pl.pallas_call(functools.partial(first_forward_kernel, plans[0], cuts), o...  8.75 us
    pallas_call x2, Pallas kernels, body(): pl.pallas_call(functools.partial(back_kernel, [*pieces], cuts, bool(befor...  3.63 us
    unnamed x16, local copies, waits for them, and re-layouts  3.21 us
    pallas_call x1, Pallas kernels, body(): pl.pallas_call(functools.partial(next_forward_kernel, plans[1], cuts), ou...  2.8 us
    pallas_call x1, Pallas kernels, body(): pl.pallas_call(functools.partial(final_back_kernel, [*far], cuts), out_sh...  2.67 us
    pallas_call x2, Pallas kernels, body(): pl.pallas_call(functools.partial(place_kernel, bool(sums)), out_shape=[ja...  1.66 us
  transfers between devices with their start and end apart: 18, of which 6 were waited for; matrix products, arithmetic and copies ran while one was open for 0% of the time, Pallas kernels for 35%

profile of v5, /device:TPU:0, one launch (start us, length us, event | category | flops | bytes accessed | tf_op | source)
XLA Modules:
  0.0 62.3 jit_solution(728839661885771942)
XLA Ops:
  0.7 0.6 %copy-done.7 = s32[256]{0:T(256)S(1)} copy-done((s32[256]{0:T(256)S(1)}, s32[256]{0:T(256)}, u32[]{:S(2)}) %copy-start.7) | copy-done | bytes 1048
  1.9 0.6 gather_rows.1
  2.5 3.0 %collective-permute-start = (bf16[256,768]{1,0:T(8,128)(2,1)S(1)}, bf16[256,768]{1,0:T(8,128)(2,1)S(1)}, u32[]{:S(2)}, u32[]{:S(2)}) collective-permute-start(bf16[256,768]{1,0:T(8,128)(2,1)S(1)} %get-tuple-element.59.refs_0_), channel_id=1, source_target_pairs={{0,1},{1,0},{2,3},{3,2},{4,5},{5,4},{6,7},{7,6},{8,9},{9,8},{10,11... | collective-permute-start | bytes 1179656 | tf_op jit(solution)/shard_map/ppermute | solution.py:280
  5.5 1.5 %collective-permute-start.1 = (bf16[256,768]{1,0:T(8,128)(2,1)S(1)}, bf16[256,768]{1,0:T(8,128)(2,1)S(1)}, u32[]{:S(2)}, u32[]{:S(2)}) collective-permute-start(bf16[256,768]{1,0:T(8,128)(2,1)S(1)} %get-tuple-element.60.refs_1_), channel_id=1, source_target_pairs={{0,2},{1,3},{2,0},{3,1},{4,6},{5,7},{6,4},{7,5},{8,10},{9,11},{10,... | collective-permute-start | bytes 1179656 | tf_op jit(solution)/shard_map/ppermute | solution.py:280
  7.0 0.5 collective-permute-start.5
  7.6 1.1 %copy-done = bf16[256,1344]{0,1:T(8,128)(2,1)S(1)} copy-done((bf16[256,1344]{0,1:T(8,128)(2,1)S(1)}, bf16[256,1344]{0,1:T(8,128)(2,1)}, u32[]{:S(2)}) %copy-start) | copy-done | bytes 688152
  8.7 1.1 %copy-done.2 = bf16[256,1344]{0,1:T(8,128)(2,1)S(1)} copy-done((bf16[256,1344]{0,1:T(8,128)(2,1)S(1)}, bf16[256,1344]{0,1:T(8,128)(2,1)}, u32[]{:S(2)}) %copy-start.2) | copy-done | bytes 688152
  9.8 8.8 %forward_0.1 = (f32[256,768]{1,0:T(8,128)S(1)}, f32[256,768]{1,0:T(8,128)S(1)}, bf16[256,768]{1,0:T(8,128)(2,1)S(1)}, bf16[256,768]{1,0:T(8,128)(2,1)S(1)}, bf16...) custom-call(s32[1]{0:T(128)} %bitcast.me_ref, bf16[1344,256]{1,0:T(8,128)(2,1)S(1)} %bitcast.7, ...), custom_call_target="tpu_custom_call" | custom-call | flops 1 | bytes 1 | tf_op jit(solution)/shard_map/forward_0/pallas_call | solution.py:326
  18.6 2.0 %collective-permute-start.2 = (bf16[256,768]{1,0:T(8,128)(2,1)S(1)}, bf16[256,768]{1,0:T(8,128)(2,1)S(1)}, u32[]{:S(2)}, u32[]{:S(2)}) collective-permute-start(bf16[256,768]{1,0:T(8,128)(2,1)S(1)} %collective-permute-done.refs_2_), channel_id=1, source_target_pairs={{0,2},{1,3},{2,0},{3,1},{4,6},{5,7},{6,4},{7,5},{8,10},{9,11},{10,... | collective-permute-start | bytes 1179656 | tf_op jit(solution)/shard_map/ppermute | solution.py:280
  20.6 1.5 %collective-permute-start.3 = (bf16[256,768]{1,0:T(8,128)(2,1)S(1)}, bf16[256,768]{1,0:T(8,128)(2,1)S(1)}, u32[]{:S(2)}, u32[]{:S(2)}) collective-permute-start(bf16[256,768]{1,0:T(8,128)(2,1)S(1)} %collective-permute-done.1.refs_3_), channel_id=1, source_target_pairs={{0,1},{1,0},{2,3},{3,2},{4,5},{5,4},{6,7},{7,6},{8,9},{9,8},{10,11... | collective-permute-start | bytes 1179656 | tf_op jit(solution)/shard_map/ppermute | solution.py:280
  22.8 2.3 %back_near_0.1.refs_3_ = f32[1344,256]{1,0:T(8,128)S(1)} custom-call(s32[1]{0:T(128)} %bitcast.me_ref, bf16[256,768]{1,0:T(8,128)(2,1)S(1)} %get-tuple-element.59.refs_0_, bf16[256,768]{1,0:T(8,128)(2,1)S(1)} %get-tuple-element.60.refs_1_, bf16[256,768]{1,0:T(8,128)(2,1)S(1)} %collective-permute-done.refs_2_, ...), custom_call_target="tpu_custom_call" | custom-call | flops 1 | bytes 1 | tf_op jit(solution)/shard_map/back_near_0/pallas_call | solution.py:369
  25.1 2.8 %forward_1.1 = (bf16[256,768]{1,0:T(8,128)(2,1)S(1)}, bf16[256,768]{1,0:T(8,128)(2,1)S(1)}, f32[256,768]{1,0:T(8,128)S(1)}, f32[256,768]{1,0:T(8,128)S(1)}, f32[...) custom-call(s32[1]{0:T(128)} %bitcast.me_ref, s32[1,256]{1,0:T(1,128)S(1)} %bitcast.14, ...), custom_call_target="tpu_custom_call" | custom-call | flops 1 | bytes 1 | tf_op jit(solution)/shard_map/forward_1/pallas_call | solution.py:350
  27.9 0.6 collective-permute-start.10
  29.1 1.3 %back_near_1.1.refs_3_ = f32[1344,256]{1,0:T(8,128)S(1)} custom-call(s32[1]{0:T(128)} %bitcast.me_ref, bf16[256,768]{1,0:T(8,128)(2,1)S(1)} %collective-permute-done.4.refs_0_, bf16[256,768]{1,0:T(8,128)(2,1)S(1)} %collective-permute-done.5.refs_1_, bf16[1344,6144]{1,0:T(8,128)(2,1)S(1)} %get-tuple-element.63.kept_ref.refs_4_.refs_2_, ...), custom_call_target="tpu_custom_call" | custom-call | flops 1 | bytes 1 | tf_op jit(solution)/shard_map/back_near_1/pallas_call | solution.py:369
  30.7 3.7 %collective-permute-done.2.refs_0_ = bf16[256,768]{1,0:T(8,128)(2,1)S(1)} collective-permute-done((bf16[256,768]{1,0:T(8,128)(2,1)S(1)}, bf16[256,768]{1,0:T(8,128)(2,1)S(1)}, u32[]{:S(2)}, u32[]{:S(2)}) %collective-permute-start.2) | collective-permute-done | bytes 393248 | tf_op jit(solution)/shard_map/ppermute | solution.py:280
  34.7 1.5 %collective-permute-start.8 = (f32[1,256]{1,0:T(1,128)S(1)}, f32[1,256]{1,0:T(1,128)S(1)}, u32[]{:S(2)}, u32[]{:S(2)}) collective-permute-start(f32[1,256]{1,0:T(1,128)S(1)} %dot_part.5.refs_0_), channel_id=1, source_target_pairs={{0,3},{1,2},{2,1},{3,0},{4,7},{5,6},{6,5},{7,4},{8,11},{9,10},{10,... | collective-permute-start | bytes 3080 | tf_op jit(solution)/shard_map/ppermute | solution.py:280
  36.3 1.9 %collective-permute-start.6 = (f32[1,256]{1,0:T(1,128)S(1)}, f32[1,256]{1,0:T(1,128)S(1)}, u32[]{:S(2)}, u32[]{:S(2)}) collective-permute-start(f32[1,256]{1,0:T(1,128)S(1)} %dot_part.5.refs_0_), channel_id=1, source_target_pairs={{0,1},{1,0},{2,3},{3,2},{4,5},{5,4},{6,7},{7,6},{8,9},{9,8},{10,11... | collective-permute-start | bytes 3080 | tf_op jit(solution)/shard_map/ppermute | solution.py:280
  38.2 2.7 %back_far.1 = (bf16[1344,256]{1,0:T(8,128)(2,1)}, bf16[1344,256]{1,0:T(8,128)(2,1)}) custom-call(s32[1]{0:T(128)} %bitcast.me_ref, f32[1,256]{1,0:T(1,128)S(1)} %get-tuple-element.83.prob_ref, bf16[1344,256]{1,0:T(8,128)(2,1)S(1)} %bitcast.8, bf16[1344,256]{1,0:T(8,128)(2,1)S(1)} %bitcast.10, bf16[256,768]{1,0:T(8,128)(2,1)S(1)} %collective-permute-done.2.refs_0_, ...), custom_call_target="tpu_custom_call" | custom-call | flops 1 | bytes 1 | tf_op jit(solution)/shard_map/back_far/pallas_call | solution.py:399
  40.9 0.5 collective-permute-done.10
  41.4 1.5 %collective-permute-start.15 = (bf16[256,768]{1,0:T(8,128)(2,1)S(1)}, bf16[256,768]{1,0:T(8,128)(2,1)S(1)}, u32[]{:S(2)}, u32[]{:S(2)}) collective-permute-start(bf16[256,768]{1,0:T(8,128)(2,1)S(1)} %get-tuple-element.97.refs_7_), channel_id=1, source_target_pairs={{0,2},{1,3},{2,0},{3,1},{4,6},{5,7},{6,4},{7,5},{8,10},{9,11},{10,... | collective-permute-start | bytes 1179656 | tf_op jit(solution)/shard_map/ppermute | solution.py:280
  42.9 0.5 collective-permute-start.13
  43.5 0.6 router_part.1
  44.2 1.2 %collective-permute-done.11 = f32[16,1536]{1,0:T(8,128)S(1)} collective-permute-done((f32[16,1536]{1,0:T(8,128)S(1)}, f32[16,1536]{1,0:T(8,128)S(1)}, u32[]{:S(2)}, u32[]{:S(2)}) %collective-permute-start.11) | collective-permute-done | bytes 98336 | tf_op jit(solution)/shard_map/ppermute | solution.py:280
  45.4 1.6 %collective-permute-start.12 = (bf16[16,1536]{1,0:T(8,128)(2,1)S(1)}, bf16[16,1536]{1,0:T(8,128)(2,1)S(1)}, u32[]{:S(2)}, u32[]{:S(2)}) collective-permute-start(bf16[16,1536]{1,0:T(8,128)(2,1)S(1)} %add_convert_fusion.3), channel_id=1, source_target_pairs={{0,8},{4,12},{8,0},{12,4},{16,24},{20,28},{24,16},{28,20},{1,9},{5... | collective-permute-start | bytes 147464 | tf_op jit(solution)/shard_map/ppermute | solution.py:280
  47.1 0.6 collective-permute-start.14
  47.7 1.5 %collective-permute-start.17 = (bf16[256,768]{1,0:T(8,128)(2,1)S(1)}, bf16[256,768]{1,0:T(8,128)(2,1)S(1)}, u32[]{:S(2)}, u32[]{:S(2)}) collective-permute-start(bf16[256,768]{1,0:T(8,128)(2,1)S(1)} %add_convert_fusion), channel_id=1, source_target_pairs={{0,1},{1,0},{2,3},{3,2},{4,5},{5,4},{6,7},{7,6},{8,9},{9,8},{10,11... | collective-permute-start | bytes 1179656 | tf_op jit(solution)/shard_map/ppermute | solution.py:280
  49.6 5.0 %collective-permute-done.13.refs_1_ = bf16[256,768]{1,0:T(8,128)(2,1)S(1)} collective-permute-done((bf16[256,768]{1,0:T(8,128)(2,1)S(1)}, bf16[256,768]{1,0:T(8,128)(2,1)S(1)}, u32[]{:S(2)}, u32[]{:S(2)}) %collective-permute-start.13) | collective-permute-done | bytes 393248 | tf_op jit(solution)/shard_map/ppermute | solution.py:280
  54.6 2.6 %collective-permute-start.16 = (bf16[16,1536]{1,0:T(8,128)(2,1)S(1)}, bf16[16,1536]{1,0:T(8,128)(2,1)S(1)}, u32[]{:S(2)}, u32[]{:S(2)}) collective-permute-start(bf16[16,1536]{1,0:T(8,128)(2,1)S(1)} %add_convert_fusion.2.refs_2_), channel_id=1, source_target_pairs={{0,16},{4,20},{8,24},{12,28},{16,0},{20,4},{24,8},{28,12},{1,17},{... | collective-permute-start | bytes 147464 | tf_op jit(solution)/shard_map/ppermute | solution.py:280
  57.2 0.5 place_0.1.placed_ref
  57.7 1.9 %collective-permute-done.16.refs_3_ = bf16[16,1536]{1,0:T(8,128)(2,1)S(1)} collective-permute-done((bf16[16,1536]{1,0:T(8,128)(2,1)S(1)}, bf16[16,1536]{1,0:T(8,128)(2,1)S(1)}, u32[]{:S(2)}, u32[]{:S(2)}) %collective-permute-start.16) | collective-permute-done | bytes 49184 | tf_op jit(solution)/shard_map/ppermute | solution.py:280
  59.6 1.1 %place_1.1 = (f32[384,768]{1,0:T(8,128)S(1)}, f32[16,1536]{1,0:T(8,128)}) custom-call(bf16[384,256]{1,0:T(8,128)(2,1)S(1)} %get-tuple-element.64.pick_ref, f32[256,768]{1,0:T(8,128)S(1)} %get-tuple-element.80.refs_5_.refs_0_, bf16[256,768]{1,0:T(8,128)(2,1)S(1)} %collective-permute-done.15.refs_1_, bf16[16,1536]{1,0:T(8,128)(2,1)S(1)} %add_convert_fusion.2.refs_2_, ...), custom_call_target="tpu_custom_call" | custom-call | flops 1 | bytes 1 | tf_op jit(solution)/shard_map/place_1/pallas_call | solution.py:453
  61.1 1.1 %combine_0.1 = bf16[384,1536]{1,0:T(8,128)(2,1)} custom-call(f32[384,768]{1,0:T(8,128)S(1)} %place_0.1.placed_ref, bf16[384,256]{1,0:T(8,128)(2,1)S(1)} %get-tuple-element.64.pick_ref, f32[384,1]{1,0:T(8,128)S(1)} %get-tuple-element.95.weight_ref, bf16[256,768]{1,0:T(8,128)(2,1)S(1)} %collective-permute-done.14.last_ref, bf16[384,768]{1,0:T(8,128)(2,1)S(1)} %combine_1.1.refs_0_), custom_call_target="tpu_custom_call" | custom-call | flops 1 | bytes 1 | tf_op jit(solution)/shard_map/combine_0/pallas_call | solution.py:476
  (40 shorter events, 3.0 us)
Async XLA Ops:
  0.6 0.7 %copy-start.7 = (s32[256]{0:T(256)S(1)}, s32[256]{0:T(256)}, u32[]{:S(2)}) copy-start(s32[256]{0:T(256)} %param.11) | copy-start | bytes 3076
  0.6 1.3 %copy-start.5 = (bf16[384,1536]{1,0:T(8,128)(2,1)S(1)}, bf16[384,1536]{1,0:T(8,128)(2,1)}, u32[]{:S(2)}) copy-start(bf16[384,1536]{1,0:T(8,128)(2,1)} %grad_ref.1) | copy-start | bytes 3538948
  2.5 16.1 %collective-permute-start = (bf16[256,768]{1,0:T(8,128)(2,1)S(1)}, bf16[256,768]{1,0:T(8,128)(2,1)S(1)}, u32[]{:S(2)}, u32[]{:S(2)}) collective-permute-start(bf16[256,768]{1,0:T(8,128)(2,1)S(1)} %get-tuple-element.59.refs_0_), channel_id=1, source_target_pairs={{0,1},{1,0},{2,3},{3,2},{4,5},{5,4},{6,7},{7,6},{8,9},{9,8},{10,11... | collective-permute-start | bytes 1179656 | tf_op jit(solution)/shard_map/ppermute | solution.py:280
  5.5 13.1 %collective-permute-start.1 = (bf16[256,768]{1,0:T(8,128)(2,1)S(1)}, bf16[256,768]{1,0:T(8,128)(2,1)S(1)}, u32[]{:S(2)}, u32[]{:S(2)}) collective-permute-start(bf16[256,768]{1,0:T(8,128)(2,1)S(1)} %get-tuple-element.60.refs_1_), channel_id=1, source_target_pairs={{0,2},{1,3},{2,0},{3,1},{4,6},{5,7},{6,4},{7,5},{8,10},{9,11},{10,... | collective-permute-start | bytes 1179656 | tf_op jit(solution)/shard_map/ppermute | solution.py:280
  7.0 21.5 %collective-permute-start.5 = (bf16[256,768]{1,0:T(8,128)(2,1)S(1)}, bf16[256,768]{1,0:T(8,128)(2,1)S(1)}, u32[]{:S(2)}, u32[]{:S(2)}) collective-permute-start(bf16[256,768]{1,0:T(8,128)(2,1)S(1)} %get-tuple-element.59.refs_0_), channel_id=1, source_target_pairs={{0,2},{1,3},{2,0},{3,1},{4,6},{5,7},{6,4},{7,5},{8,10},{9,11},{10,... | collective-permute-start | bytes 1179656 | tf_op jit(solution)/shard_map/ppermute | solution.py:280
  7.5 21.6 %collective-permute-start.4 = (bf16[256,768]{1,0:T(8,128)(2,1)S(1)}, bf16[256,768]{1,0:T(8,128)(2,1)S(1)}, u32[]{:S(2)}, u32[]{:S(2)}) collective-permute-start(bf16[256,768]{1,0:T(8,128)(2,1)S(1)} %get-tuple-element.60.refs_1_), channel_id=1, source_target_pairs={{0,1},{1,0},{2,3},{3,2},{4,5},{5,4},{6,7},{7,6},{8,9},{9,8},{10,11... | collective-permute-start | bytes 1179656 | tf_op jit(solution)/shard_map/ppermute | solution.py:280
  7.6 1.1 %copy-start = (bf16[256,1344]{0,1:T(8,128)(2,1)S(1)}, bf16[256,1344]{0,1:T(8,128)(2,1)}, u32[]{:S(2)}) copy-start(bf16[256,1344]{0,1:T(8,128)(2,1)} %param.8) | copy-start | bytes 2064388
  8.7 1.1 %copy-start.2 = (bf16[256,1344]{0,1:T(8,128)(2,1)S(1)}, bf16[256,1344]{0,1:T(8,128)(2,1)}, u32[]{:S(2)}) copy-start(bf16[256,1344]{0,1:T(8,128)(2,1)} %param.9) | copy-start | bytes 2064388
  18.6 15.8 %collective-permute-start.2 = (bf16[256,768]{1,0:T(8,128)(2,1)S(1)}, bf16[256,768]{1,0:T(8,128)(2,1)S(1)}, u32[]{:S(2)}, u32[]{:S(2)}) collective-permute-start(bf16[256,768]{1,0:T(8,128)(2,1)S(1)} %collective-permute-done.refs_2_), channel_id=1, source_target_pairs={{0,2},{1,3},{2,0},{3,1},{4,6},{5,7},{6,4},{7,5},{8,10},{9,11},{10,... | collective-permute-start | bytes 1179656 | tf_op jit(solution)/shard_map/ppermute | solution.py:280
  20.6 13.8 %collective-permute-start.3 = (bf16[256,768]{1,0:T(8,128)(2,1)S(1)}, bf16[256,768]{1,0:T(8,128)(2,1)S(1)}, u32[]{:S(2)}, u32[]{:S(2)}) collective-permute-start(bf16[256,768]{1,0:T(8,128)(2,1)S(1)} %collective-permute-done.1.refs_3_), channel_id=1, source_target_pairs={{0,1},{1,0},{2,3},{3,2},{4,5},{5,4},{6,7},{7,6},{8,9},{9,8},{10,11... | collective-permute-start | bytes 1179656 | tf_op jit(solution)/shard_map/ppermute | solution.py:280
  22.8 2.4 %copy-start.6 = (f32[384,16]{0,1:T(8,128)S(1)}, f32[384,16]{0,1:T(8,128)}, u32[]{:S(2)}) copy-start(f32[384,16]{0,1:T(8,128)} %param.13) | copy-start | bytes 73732
  27.9 13.5 %collective-permute-start.10 = (bf16[256,768]{1,0:T(8,128)(2,1)S(1)}, bf16[256,768]{1,0:T(8,128)(2,1)S(1)}, u32[]{:S(2)}, u32[]{:S(2)}) collective-permute-start(bf16[256,768]{1,0:T(8,128)(2,1)S(1)} %get-tuple-element.75.refs_3_), channel_id=1, source_target_pairs={{0,2},{1,3},{2,0},{3,1},{4,6},{5,7},{6,4},{7,5},{8,10},{9,11},{10,... | collective-permute-start | bytes 1179656 | tf_op jit(solution)/shard_map/ppermute | solution.py:280
  28.5 14.4 %collective-permute-start.9 = (bf16[256,768]{1,0:T(8,128)(2,1)S(1)}, bf16[256,768]{1,0:T(8,128)(2,1)S(1)}, u32[]{:S(2)}, u32[]{:S(2)}) collective-permute-start(bf16[256,768]{1,0:T(8,128)(2,1)S(1)} %get-tuple-element.74.refs_2_), channel_id=1, source_target_pairs={{0,1},{1,0},{2,3},{3,2},{4,5},{5,4},{6,7},{7,6},{8,9},{9,8},{10,11... | collective-permute-start | bytes 1179656 | tf_op jit(solution)/shard_map/ppermute | solution.py:280
  30.7 7.5 %copy-start.1 = (bf16[256,1344]{0,1:T(8,128)(2,1)S(1)}, bf16[256,1344]{0,1:T(8,128)(2,1)}, u32[]{:S(2)}) copy-start(bf16[256,1344]{0,1:T(8,128)(2,1)} %param.8) | copy-start | bytes 2064388
  30.7 7.5 %copy-start.3 = (bf16[256,1344]{0,1:T(8,128)(2,1)S(1)}, bf16[256,1344]{0,1:T(8,128)(2,1)}, u32[]{:S(2)}) copy-start(bf16[256,1344]{0,1:T(8,128)(2,1)} %param.9) | copy-start | bytes 2064388
  34.7 8.7 %collective-permute-start.8 = (f32[1,256]{1,0:T(1,128)S(1)}, f32[1,256]{1,0:T(1,128)S(1)}, u32[]{:S(2)}, u32[]{:S(2)}) collective-permute-start(f32[1,256]{1,0:T(1,128)S(1)} %dot_part.5.refs_0_), channel_id=1, source_target_pairs={{0,3},{1,2},{2,1},{3,0},{4,7},{5,6},{6,5},{7,4},{8,11},{9,10},{10,... | collective-permute-start | bytes 3080 | tf_op jit(solution)/shard_map/ppermute | solution.py:280
  36.2 7.2 %collective-permute-start.7 = (f32[1,256]{1,0:T(1,128)S(1)}, f32[1,256]{1,0:T(1,128)S(1)}, u32[]{:S(2)}, u32[]{:S(2)}) collective-permute-start(f32[1,256]{1,0:T(1,128)S(1)} %dot_part.5.refs_0_), channel_id=1, source_target_pairs={{0,2},{1,3},{2,0},{3,1},{4,6},{5,7},{6,4},{7,5},{8,10},{9,11},{10,... | collective-permute-start | bytes 3080 | tf_op jit(solution)/shard_map/ppermute | solution.py:280
  36.3 7.1 %collective-permute-start.6 = (f32[1,256]{1,0:T(1,128)S(1)}, f32[1,256]{1,0:T(1,128)S(1)}, u32[]{:S(2)}, u32[]{:S(2)}) collective-permute-start(f32[1,256]{1,0:T(1,128)S(1)} %dot_part.5.refs_0_), channel_id=1, source_target_pairs={{0,1},{1,0},{2,3},{3,2},{4,5},{5,4},{6,7},{7,6},{8,9},{9,8},{10,11... | collective-permute-start | bytes 3080 | tf_op jit(solution)/shard_map/ppermute | solution.py:280
  38.2 5.2 %copy-start.4 = (bf16[384,1536]{1,0:T(8,128)(2,1)S(1)}, bf16[384,1536]{1,0:T(8,128)(2,1)}, u32[]{:S(2)}) copy-start(bf16[384,1536]{1,0:T(8,128)(2,1)} %tokens_ref.1) | copy-start | bytes 3538948
  41.4 16.3 %collective-permute-start.15 = (bf16[256,768]{1,0:T(8,128)(2,1)S(1)}, bf16[256,768]{1,0:T(8,128)(2,1)S(1)}, u32[]{:S(2)}, u32[]{:S(2)}) collective-permute-start(bf16[256,768]{1,0:T(8,128)(2,1)S(1)} %get-tuple-element.97.refs_7_), channel_id=1, source_target_pairs={{0,2},{1,3},{2,0},{3,1},{4,6},{5,7},{6,4},{7,5},{8,10},{9,11},{10,... | collective-permute-start | bytes 1179656 | tf_op jit(solution)/shard_map/ppermute | solution.py:280
  42.9 11.7 %collective-permute-start.13 = (bf16[256,768]{1,0:T(8,128)(2,1)S(1)}, bf16[256,768]{1,0:T(8,128)(2,1)S(1)}, u32[]{:S(2)}, u32[]{:S(2)}) collective-permute-start(bf16[256,768]{1,0:T(8,128)(2,1)S(1)} %get-tuple-element.93.refs_6_), channel_id=1, source_target_pairs={{0,1},{1,0},{2,3},{3,2},{4,5},{5,4},{6,7},{7,6},{8,9},{9,8},{10,11... | collective-permute-start | bytes 1179656 | tf_op jit(solution)/shard_map/ppermute | solution.py:280
  44.1 1.3 %collective-permute-start.11 = (f32[16,1536]{1,0:T(8,128)S(1)}, f32[16,1536]{1,0:T(8,128)S(1)}, u32[]{:S(2)}, u32[]{:S(2)}) collective-permute-start(f32[16,1536]{1,0:T(8,128)S(1)} %router_part.1), channel_id=1, source_target_pairs={{0,4},{4,0},{8,12},{12,8},{16,20},{20,16},{24,28},{28,24},{1,5},{5... | collective-permute-start | bytes 294920 | tf_op jit(solution)/shard_map/ppermute | solution.py:280
  45.4 4.2 %collective-permute-start.12 = (bf16[16,1536]{1,0:T(8,128)(2,1)S(1)}, bf16[16,1536]{1,0:T(8,128)(2,1)S(1)}, u32[]{:S(2)}, u32[]{:S(2)}) collective-permute-start(bf16[16,1536]{1,0:T(8,128)(2,1)S(1)} %add_convert_fusion.3), channel_id=1, source_target_pairs={{0,8},{4,12},{8,0},{12,4},{16,24},{20,28},{24,16},{28,20},{1,9},{5... | collective-permute-start | bytes 147464 | tf_op jit(solution)/shard_map/ppermute | solution.py:280
  47.1 13.9 %collective-permute-start.14 = (bf16[256,768]{1,0:T(8,128)(2,1)S(1)}, bf16[256,768]{1,0:T(8,128)(2,1)S(1)}, u32[]{:S(2)}, u32[]{:S(2)}) collective-permute-start(bf16[256,768]{1,0:T(8,128)(2,1)S(1)} %add_convert_fusion.1), channel_id=1, source_target_pairs={{0,2},{1,3},{2,0},{3,1},{4,6},{5,7},{6,4},{7,5},{8,10},{9,11},{10,... | collective-permute-start | bytes 1179656 | tf_op jit(solution)/shard_map/ppermute | solution.py:280
  47.7 13.0 %collective-permute-start.17 = (bf16[256,768]{1,0:T(8,128)(2,1)S(1)}, bf16[256,768]{1,0:T(8,128)(2,1)S(1)}, u32[]{:S(2)}, u32[]{:S(2)}) collective-permute-start(bf16[256,768]{1,0:T(8,128)(2,1)S(1)} %add_convert_fusion), channel_id=1, source_target_pairs={{0,1},{1,0},{2,3},{3,2},{4,5},{5,4},{6,7},{7,6},{8,9},{9,8},{10,11... | collective-permute-start | bytes 1179656 | tf_op jit(solution)/shard_map/ppermute | solution.py:280
  54.6 5.0 %collective-permute-start.16 = (bf16[16,1536]{1,0:T(8,128)(2,1)S(1)}, bf16[16,1536]{1,0:T(8,128)(2,1)S(1)}, u32[]{:S(2)}, u32[]{:S(2)}) collective-permute-start(bf16[16,1536]{1,0:T(8,128)(2,1)S(1)} %add_convert_fusion.2.refs_2_), channel_id=1, source_target_pairs={{0,16},{4,20},{8,24},{12,28},{16,0},{20,4},{24,8},{28,12},{1,17},{... | collective-permute-start | bytes 147464 | tf_op jit(solution)/shard_map/ppermute | solution.py:280
